TPU v7x, 32 devices: a whole 2x2x4 slice. The times are simulated.
32 devices in a mesh: track: 8 (over z, y), det: 4 (over x, core).
Axes of the slice: x: 2, y: 2, z: 4, core: 2. Of those that a mesh axis runs over, the one named last changes fastest.
Arguments:
- jac: float32 [4096, 12, 512], P('track', None, 'det'), may hold values from -1.75 to 1.75
- obs: float32 [4096, 512], P('track', 'det'), may hold values from -6 to 6
- match: int32 [4096], P('track'), may hold values from 0 to 4095, as said below
- tile_knot: int32 [4096], P('track'), may hold values from 0 to 127
- tile_frac: float32 [4096], P('track'), may hold values from 0 to 1
Outputs:
- knot_field: float32 [12, 1024], P(None, 'track')
- tie_residual: float32 [4096, 512], P('track', 'det')
Inputs may be any that keep to these rules, and one draw needn't show every extreme that they name: match[match[i]] = i and match[i] != i; the tiles of each index of track cross exactly 64 tiles of every index of track, itself included.
All inputs are finite; a program needn't handle non-finite values.
Results may differ from a plain program's by a relative error of at most 0.0001.
Values sent between devices are 32-bit elements; how exact they have to be, the bound alone decides.
No kernel may reach another device: no remote copies, remote signals or barrier semaphores. Data moves between devices by JAX's collectives and lax.ppermute only.
A program may use at most 64 MiB of HBM per device.

v0:
```python
import jax
import jax.numpy as jnp
from jax import lax
from jax.sharding import PartitionSpec as P

KNOT_DEV = 128
ITERS = 4


damping = 1.0


def passed_along(value, axis, steps):
    count = lax.axis_size(axis)
    leading, last = (max(0, -steps), min(count, count - steps))
    return lax.ppermute(value, axis, [(source, source + steps) for source in range(leading, last)])


def local(jac, obs, match, tile_knot, tile_frac):
    highest = lax.Precision.HIGHEST
    tiles_dev = jac.shape[0]
    params = jac.shape[1]
    n_track = lax.axis_size("track")
    n_det = lax.axis_size("det")
    per_peer = tiles_dev // n_track
    send_order = jnp.argsort(match // tiles_dev, stable=True)

    def arrange(values):
        return values[send_order].reshape((n_track, per_peer) + values.shape[1:])

    slots_in = lax.all_to_all(
        arrange(match % tiles_dev), "track", split_axis=0, concat_axis=0, tiled=True
    )
    receive_order = jnp.argsort(slots_in.reshape(-1))

    def settle(arrived):
        joined = arrived.reshape((tiles_dev,) + arrived.shape[2:])
        return joined[receive_order]

    def partner_values(values):
        return settle(
            lax.all_to_all(arrange(values), "track", split_axis=0, concat_axis=0, tiled=True)
        )

    knot_rows = lax.broadcasted_iota(jnp.int32, (KNOT_DEV, tiles_dev), 0)
    weights = jnp.where(knot_rows == tile_knot[None, :], 1.0 - tile_frac[None, :], 0.0)
    weights = weights + jnp.where(knot_rows == tile_knot[None, :] + 1, tile_frac[None, :], 0.0)
    weights_back = weights.T
    edge_weight = jnp.where(tile_knot == KNOT_DEV - 1, tile_frac, 0.0)
    misfit = obs - partner_values(obs)

    def adjoint(residual_rows):
        partial_value = jnp.einsum("ipw,iw->pi", jac, residual_rows, precision=highest)
        spread = jnp.dot(partial_value, weights_back, precision=highest)
        spill_over = jnp.dot(partial_value, edge_weight, precision=highest)
        spread, spill_over = lax.psum((spread, spill_over), "det")
        carried = passed_along(spill_over, "track", 1)
        return spread.at[:, 0].add(carried)

    def slope_total(gradient):
        return lax.psum(jnp.sum(gradient * gradient), "track")

    knot_field = jnp.zeros((params, KNOT_DEV), jnp.float32)
    tie_residual = misfit
    gradient = adjoint(tie_residual)
    direction = gradient
    slope_norm = slope_total(gradient)
    for iteration in range(ITERS):
        following = passed_along(direction[:, 0], "track", -1)
        interp = (
            jnp.dot(direction, weights, precision=highest)
            + following[:, None] * edge_weight[None, :]
        )
        own_pred = jnp.einsum("ipw,pi->iw", jac, interp, precision=highest)
        other_pred = partner_values(own_pred)
        change = own_pred - other_pred
        change_sq, direction_sq = lax.psum(
            (jnp.sum(change * change), jnp.sum(direction * direction)), ("track", "det")
        )
        curvature = 0.5 * change_sq + damping * direction_sq / n_det
        step_length = slope_norm / curvature
        knot_field = knot_field + step_length * direction
        tie_residual = tie_residual - step_length * change
        gradient = adjoint(tie_residual) - damping * knot_field
        new_norm = slope_total(gradient)
        direction = gradient + new_norm / slope_norm * direction
        slope_norm = new_norm
    return (knot_field, tie_residual)


def solution(mesh):
    in_specs = (P("track", None, "det"), P("track", "det"), P("track"), P("track"), P("track"))
    out_specs = (P(None, "track"), P("track", "det"))
    return jax.shard_map(local, mesh=mesh, in_specs=in_specs, out_specs=out_specs, check_vma=False)
```

profile of v0, /device:TPU:0, one launch (start us, length us, event | category | flops | bytes accessed | tf_op | source)
XLA Modules:
  0.0 507.5 jit_solution(16333897414643985727)
XLA Ops:
  9.5 7.3 %all-to-all-start.1 = ((s32[8,1,64]{2,1,0:T(1,128)}), s32[8,1,64]{2,1,0:T(1,128)S(1)}, u32[]{:S(2)}, u32[]{:S(2)}) async-start(s32[8,1,64]{2,1,0:T(1,128)} %all_to_all.22), calls=%async_computation.1 | async-start | bytes 8192 | tf_op jit(solution)/shard_map/all_to_all | solution.py:31
  19.1 4.0 all-to-all-done.1
  23.2 4.0 all-to-all-start
  39.7 7.9 %fusion.14 = f32[512,1,12]{2,1,0:T(1,128)S(1)} fusion(f32[512,128,1]{1,2,0:T(1,128)S(1)} %bitcast.105, f32[512,12,128]{2,0,1:T(8,128)S(1)} %copy-done), kind=kOutput, calls=%fused_computation.25 | convolution fusion | flops 9437184 | bytes 3432448 | tf_op jit(solution)/shard_map/ipw,iw->pi/dot_general | solution.py:53
  49.1 5.9 %all-reduce.7 = (f32[12]{0:T(128)S(1)}, f32[12,128]{1,0:T(8,128)S(1)}) all-reduce(f32[12]{0:T(128)S(1)} %convolution_bitcast_fusion.3, f32[12,128]{1,0:T(8,128)S(1)} %fusion.23), channel_id=1, replica_groups=mesh['track'=8,'det'=4] {'det'}, use_global_device_ids=true, to_apply=%region_4.5 | all-reduce | flops 1548 | bytes 12384 | tf_op jit(solution)/shard_map/psum | solution.py:56
  61.8 4.2 collective-permute-done.1
  67.1 6.3 %fusion.12 = f32[512,1,128]{2,1,0:T(1,128)S(1)} fusion(f32[12,512,1]{0,2,1:T(1,128)} %copy.18, f32[512,12,128]{2,0,1:T(8,128)S(1)} %copy-done), kind=kOutput, calls=%fused_computation.23 | convolution fusion | flops 9437184 | bytes 3432448 | tf_op jit(solution)/shard_map/ipw,pi->iw/dot_general | solution.py:74
  75.0 4.2 all-to-all-start.2
  79.8 22.5 %psum.142 = f32[]{:T(128)} all-reduce(f32[]{:T(128)} %multiply_reduce_fusion.10), channel_id=1, replica_groups=mesh['track'=8,'det'=4] {'track'}, use_global_device_ids=true, to_apply=%region_6.7 | all-reduce | flops 1 | bytes 8 | tf_op jit(solution)/shard_map/psum | solution.py:61
  107.3 37.4 %all-reduce.3 = (f32[]{:T(128)}, f32[]{:T(128)}) all-reduce(f32[]{:T(128)} %get-tuple-element.85, f32[]{:T(128)} %multiply_reduce_fusion.10), channel_id=1, replica_groups=mesh['track'=8,'det'=4] {'track','det'}, use_global_device_ids=true, to_apply=%region_8.9 | all-reduce | flops 2 | bytes 16 | tf_op jit(solution)/shard_map/psum | solution.py:77
  148.3 7.9 %fusion.10 = f32[512,1,12]{2,1,0:T(1,128)S(1)} fusion(f32[512,128,1]{1,2,0:T(1,128)S(1)} %bitcast.108, f32[512,12,128]{2,0,1:T(8,128)S(1)} %copy-done), kind=kOutput, calls=%fused_computation.21 | convolution fusion | flops 9437184 | bytes 3432448 | tf_op jit(solution)/shard_map/ipw,iw->pi/dot_general | solution.py:53
  157.0 7.3 %all-reduce.6 = (f32[12,128]{1,0:T(8,128)S(1)}, f32[12]{0:T(128)S(1)}) all-reduce(f32[12,128]{1,0:T(8,128)S(1)} %fusion.21, f32[12]{0:T(128)S(1)} %convolution_bitcast_fusion.2), channel_id=1, replica_groups=mesh['track'=8,'det'=4] {'det'}, use_global_device_ids=true, to_apply=%region_10.11 | all-reduce | flops 1548 | bytes 12384 | tf_op jit(solution)/shard_map/psum | solution.py:56
  170.0 21.7 %psum.147 = f32[]{:T(128)} all-reduce(f32[]{:T(128)} %multiply_reduce_fusion.9), channel_id=1, replica_groups=mesh['track'=8,'det'=4] {'track'}, use_global_device_ids=true, to_apply=%region_13.14 | all-reduce | flops 1 | bytes 8 | tf_op jit(solution)/shard_map/psum | solution.py:61
  200.3 6.3 %fusion.8 = f32[512,1,128]{2,1,0:T(1,128)S(1)} fusion(f32[12,512,1]{0,2,1:T(1,128)} %copy.22, f32[512,12,128]{2,0,1:T(8,128)S(1)} %copy-done), kind=kOutput, calls=%fused_computation.19 | convolution fusion | flops 9437184 | bytes 3432448 | tf_op jit(solution)/shard_map/ipw,pi->iw/dot_general | solution.py:74
  208.3 12.2 %all_to_all.34 = f32[8,64,128]{2,1,0:T(8,128)} all-to-all(f32[8,64,128]{2,1,0:T(8,128)} %bitcast.120), channel_id=1, replica_groups=mesh['track'=8,'det'=4] {'track'}, dimensions={0} | all-to-all | bytes 524288 | tf_op jit(solution)/shard_map/all_to_all | solution.py:42
  225.5 39.5 %all-reduce.2 = (f32[]{:T(128)}, f32[]{:T(128)}) all-reduce(f32[]{:T(128)} %get-tuple-element.83, f32[]{:T(128)} %get-tuple-element.81), channel_id=1, replica_groups=mesh['track'=8,'det'=4] {'track','det'}, use_global_device_ids=true, to_apply=%region_15.16 | all-reduce | flops 2 | bytes 16 | tf_op jit(solution)/shard_map/psum | solution.py:77
  268.5 7.9 %fusion.6 = f32[512,1,12]{2,1,0:T(1,128)S(1)} fusion(f32[512,128,1]{1,2,0:T(1,128)S(1)} %bitcast.107, f32[512,12,128]{2,0,1:T(8,128)S(1)} %copy-done), kind=kOutput, calls=%fused_computation.17 | convolution fusion | flops 9437184 | bytes 3432448 | tf_op jit(solution)/shard_map/ipw,iw->pi/dot_general | solution.py:53
  277.2 6.1 %all-reduce.5 = (f32[12,128]{1,0:T(8,128)S(1)}, f32[12]{0:T(128)S(1)}) all-reduce(f32[12,128]{1,0:T(8,128)S(1)} %fusion.19, f32[12]{0:T(128)S(1)} %convolution_bitcast_fusion.1), channel_id=1, replica_groups=mesh['track'=8,'det'=4] {'det'}, use_global_device_ids=true, to_apply=%region_18.19 | all-reduce | flops 1548 | bytes 12384 | tf_op jit(solution)/shard_map/psum | solution.py:56
  283.4 4.6 collective-permute-start.4
  290.8 20.6 %psum.152 = f32[]{:T(128)} all-reduce(f32[]{:T(128)} %get-tuple-element.78), channel_id=1, replica_groups=mesh['track'=8,'det'=4] {'track'}, use_global_device_ids=true, to_apply=%region_21.22 | all-reduce | flops 1 | bytes 8 | tf_op jit(solution)/shard_map/psum | solution.py:61
  314.9 3.9 collective-permute-done.5
  320.0 6.3 %fusion.4 = f32[512,1,128]{2,1,0:T(1,128)S(1)} fusion(f32[12,512,1]{0,2,1:T(1,128)} %copy.26, f32[512,12,128]{2,0,1:T(8,128)S(1)} %copy-done), kind=kOutput, calls=%fused_computation.15 | convolution fusion | flops 9437184 | bytes 3432448 | tf_op jit(solution)/shard_map/ipw,pi->iw/dot_general | solution.py:74
  327.9 12.2 %all_to_all.35 = f32[8,64,128]{2,1,0:T(8,128)} all-to-all(f32[8,64,128]{2,1,0:T(8,128)} %bitcast.121), channel_id=1, replica_groups=mesh['track'=8,'det'=4] {'track'}, dimensions={0} | all-to-all | bytes 524288 | tf_op jit(solution)/shard_map/all_to_all | solution.py:42
  345.1 38.8 %all-reduce.1 = (f32[]{:T(128)}, f32[]{:T(128)}) all-reduce(f32[]{:T(128)} %get-tuple-element.76, f32[]{:T(128)} %get-tuple-element.74), channel_id=1, replica_groups=mesh['track'=8,'det'=4] {'track','det'}, use_global_device_ids=true, to_apply=%region_23.24 | all-reduce | flops 2 | bytes 16 | tf_op jit(solution)/shard_map/psum | solution.py:77
  387.6 7.9 %fusion.2 = f32[512,1,12]{2,1,0:T(1,128)S(1)} fusion(f32[512,128,1]{1,2,0:T(1,128)S(1)} %bitcast.106, f32[512,12,128]{2,0,1:T(8,128)S(1)} %copy-done), kind=kOutput, calls=%fused_computation.13 | convolution fusion | flops 9437184 | bytes 3432448 | tf_op jit(solution)/shard_map/ipw,iw->pi/dot_general | solution.py:53
  396.3 6.4 %all-reduce.4 = (f32[12,128]{1,0:T(8,128)S(1)}, f32[12]{0:T(128)S(1)}) all-reduce(f32[12,128]{1,0:T(8,128)S(1)} %fusion.17, f32[12]{0:T(128)S(1)} %convolution_bitcast_fusion), channel_id=1, replica_groups=mesh['track'=8,'det'=4] {'det'}, use_global_device_ids=true, to_apply=%region_26.27 | all-reduce | flops 1548 | bytes 12384 | tf_op jit(solution)/shard_map/psum | solution.py:56
  402.7 3.8 collective-permute-start.6
  409.3 21.0 %psum.157 = f32[]{:T(128)} all-reduce(f32[]{:T(128)} %multiply_reduce_fusion.5), channel_id=1, replica_groups=mesh['track'=8,'det'=4] {'track'}, use_global_device_ids=true, to_apply=%region_29.30 | all-reduce | flops 1 | bytes 8 | tf_op jit(solution)/shard_map/psum | solution.py:61
  434.1 3.8 collective-permute-done.7
  439.1 6.3 %fusion = f32[512,1,128]{2,1,0:T(1,128)S(1)} fusion(f32[12,512,1]{0,2,1:T(1,128)} %copy.30, f32[512,12,128]{2,0,1:T(8,128)S(1)} %copy-done), kind=kOutput, calls=%fused_computation.11 | convolution fusion | flops 9437184 | bytes 3432448 | tf_op jit(solution)/shard_map/ipw,pi->iw/dot_general | solution.py:74
  447.0 12.2 %all_to_all.36 = f32[8,64,128]{2,1,0:T(8,128)} all-to-all(f32[8,64,128]{2,1,0:T(8,128)} %bitcast.119), channel_id=1, replica_groups=mesh['track'=8,'det'=4] {'track'}, dimensions={0} | all-to-all | bytes 524288 | tf_op jit(solution)/shard_map/all_to_all | solution.py:42
  464.2 38.6 %all-reduce = (f32[]{:T(128)}, f32[]{:T(128)}) all-reduce(f32[]{:T(128)} %get-tuple-element.72, f32[]{:T(128)} %get-tuple-element.70), channel_id=1, replica_groups=mesh['track'=8,'det'=4] {'track','det'}, use_global_device_ids=true, to_apply=%region_31.32 | all-reduce | flops 2 | bytes 16 | tf_op jit(solution)/shard_map/psum | solution.py:77
  (104 shorter events, 95.4 us)
Async XLA Ops:
  0.6 39.1 %copy-start = (f32[512,12,128]{2,0,1:T(8,128)S(1)}, f32[512,12,128]{2,0,1:T(8,128)}, u32[]{:S(2)}) copy-start(f32[512,12,128]{2,0,1:T(8,128)} %param.13) | copy-start | bytes 9437188
  0.6 26.6 %copy-start.6 = (s32[512]{0:T(512)S(1)}, s32[512]{0:T(512)}, u32[]{:S(2)}) copy-start(s32[512]{0:T(512)} %param.16) | copy-start | bytes 6148
  0.7 16.8 %copy-start.1 = (f32[512,128]{1,0:T(8,128)S(1)}, f32[512,128]{1,0:T(8,128)}, u32[]{:S(2)}) copy-start(f32[512,128]{1,0:T(8,128)} %param.14) | copy-start | bytes 786436
  9.5 13.7 %all-to-all-start.1 = ((s32[8,1,64]{2,1,0:T(1,128)}), s32[8,1,64]{2,1,0:T(1,128)S(1)}, u32[]{:S(2)}, u32[]{:S(2)}) async-start(s32[8,1,64]{2,1,0:T(1,128)} %all_to_all.22), calls=%async_computation.1 | async-start | bytes 8192 | tf_op jit(solution)/shard_map/all_to_all | solution.py:31
  23.2 12.3 %all-to-all-start = ((f32[8,64,128]{2,1,0:T(8,128)}), f32[8,64,128]{2,1,0:T(8,128)}, u32[]{:S(2)}, u32[]{:S(2)}) async-start(f32[8,64,128]{2,1,0:T(8,128)} %bitcast.117), calls=%async_computation | async-start | bytes 524288 | tf_op jit(solution)/shard_map/all_to_all | solution.py:42
  38.0 9.8 %copy-start.7 = (f32[512]{0:T(512)S(1)}, f32[512]{0:T(512)}, u32[]{:S(2)}) copy-start(f32[512]{0:T(512)} %param.17) | copy-start | bytes 6148
  39.0 0.7 copy-start.2
  55.0 4.3 collective-permute-start
  60.3 5.7 %collective-permute-start.1 = (f32[12]{0:T(128)S(1)}, f32[12]{0:T(128)S(1)}, u32[]{:S(2)}, u32[]{:S(2)}) collective-permute-start(f32[12]{0:T(128)S(1)} %get-tuple-element.87), channel_id=1, source_target_pairs={{4,0},{8,4},{12,8},{16,12},{20,16},{24,20},{28,24},{5,1},{9,5},{13... | collective-permute-start | bytes 152 | tf_op jit(solution)/shard_map/ppermute | solution.py:16
  75.0 27.3 %all-to-all-start.2 = ((f32[8,64,128]{2,1,0:T(8,128)}), f32[8,64,128]{2,1,0:T(8,128)}, u32[]{:S(2)}, u32[]{:S(2)}) async-start(f32[8,64,128]{2,1,0:T(8,128)} %bitcast.118), calls=%async_computation.2 | async-start | bytes 524288 | tf_op jit(solution)/shard_map/all_to_all | solution.py:42
  147.6 0.7 copy-start.5
  164.3 4.2 collective-permute-start.2
  193.8 5.4 %collective-permute-start.3 = (f32[12]{0:T(128)S(1)}, f32[12]{0:T(128)S(1)}, u32[]{:S(2)}, u32[]{:S(2)}) collective-permute-start(f32[12]{0:T(128)S(1)} %slice_reduce_fusion.2), channel_id=1, source_target_pairs={{4,0},{8,4},{12,8},{16,12},{20,16},{24,20},{28,24},{5,1},{9,5},{13... | collective-permute-start | bytes 152 | tf_op jit(solution)/shard_map/ppermute | solution.py:16
  267.8 0.7 copy-start.4
  283.4 5.9 %collective-permute-start.4 = (f32[12]{0:T(128)S(1)}, f32[12]{0:T(128)S(1)}, u32[]{:S(2)}, u32[]{:S(2)}) collective-permute-start(f32[12]{0:T(128)S(1)} %get-tuple-element.65), channel_id=1, source_target_pairs={{0,4},{4,8},{8,12},{12,16},{16,20},{20,24},{24,28},{1,5},{5,9},{9,... | collective-permute-start | bytes 152 | tf_op jit(solution)/shard_map/ppermute | solution.py:16
  313.4 5.4 %collective-permute-start.5 = (f32[12]{0:T(128)S(1)}, f32[12]{0:T(128)S(1)}, u32[]{:S(2)}, u32[]{:S(2)}) collective-permute-start(f32[12]{0:T(128)S(1)} %slice_reduce_fusion.1), channel_id=1, source_target_pairs={{4,0},{8,4},{12,8},{16,12},{20,16},{24,20},{28,24},{5,1},{9,5},{13... | collective-permute-start | bytes 152 | tf_op jit(solution)/shard_map/ppermute | solution.py:16
  386.9 0.7 copy-start.3
  402.7 5.1 %collective-permute-start.6 = (f32[12]{0:T(128)S(1)}, f32[12]{0:T(128)S(1)}, u32[]{:S(2)}, u32[]{:S(2)}) collective-permute-start(f32[12]{0:T(128)S(1)} %get-tuple-element.63), channel_id=1, source_target_pairs={{0,4},{4,8},{8,12},{12,16},{16,20},{20,24},{24,28},{1,5},{5,9},{9,... | collective-permute-start | bytes 152 | tf_op jit(solution)/shard_map/ppermute | solution.py:16
  432.5 5.4 %collective-permute-start.7 = (f32[12]{0:T(128)S(1)}, f32[12]{0:T(128)S(1)}, u32[]{:S(2)}, u32[]{:S(2)}) collective-permute-start(f32[12]{0:T(128)S(1)} %slice_reduce_fusion), channel_id=1, source_target_pairs={{4,0},{8,4},{12,8},{16,12},{20,16},{24,20},{28,24},{5,1},{9,5},{13... | collective-permute-start | bytes 152 | tf_op jit(solution)/shard_map/ppermute | solution.py:16
where the time goes:
time: 517 us; the launch traced here: 507 us
  blocking collectives  303 us (59%)
  matrix products  61.2 us (12%)
  starting transfers between devices  36.3 us (7%)
  other arithmetic  33.5 us (6%)
  local copies, waits for them, and re-layouts  33.2 us (6%)
  waiting for transfers between devices  27.9 us (5%)
  between operations  12.8 us (2%)
    psum x4, blocking collectives, local(): lax.psum((jnp.sum(change * change), jnp.sum(direction * direction)), ('tr...  154 us
    psum x4, blocking collectives, slope_total(): return lax.psum(jnp.sum(gradient * gradient), 'track')  85.8 us
    all_to_all x3, blocking collectives, partner_values(): lax.all_to_all(arrange(values), 'track', split_axis=0, concat_axis=0, til...  36.7 us
    dot_general x4, matrix products, adjoint(): jnp.einsum('ipw,iw->pi', jac, residual_rows, precision=highest)  31.6 us
    psum x4, blocking collectives, adjoint(): spread, spill_over = lax.psum((spread, spill_over), 'det')  25.7 us
    dot_general x4, matrix products, local(): own_pred = jnp.einsum('ipw,pi->iw', jac, interp, precision=highest)  25.3 us
    ppermute x8, starting transfers between devices, passed_along(): lax.ppermute(value, axis, [(source, source + steps) for source in range(l...  20.8 us
    ppermute x8, waiting for transfers between devices, passed_along(): lax.ppermute(value, axis, [(source, source + steps) for source in range(l...  20.7 us
  transfers between devices with their start and end apart: 11, of which 10 were waited for; matrix products, arithmetic and copies ran while one was open for 2% of the time, Pallas kernels for 0%

commit v1 on v0

v1 whole, which is shorter than its diff:
```python
import functools

import jax
import jax.numpy as jnp
from jax import lax
from jax.experimental import pallas as pl
from jax.experimental.pallas import tpu as pltpu
from jax.sharding import PartitionSpec as P

KNOT_DEV = 128
ITERS = 4
LANES = 128
SUB = 8
PAD = 16
VMEM_BYTES = 50 * 2**20


damping = 1.0

SMEM = pl.BlockSpec(memory_space=pltpu.SMEM)
VMEM = pl.BlockSpec(memory_space=pltpu.VMEM)
PARAMS = pltpu.CompilerParams(vmem_limit_bytes=VMEM_BYTES)
HIGHEST = lax.Precision.HIGHEST


def f32(*shape):
    return jax.ShapeDtypeStruct(shape, jnp.float32)


def dot(a, b, dims):
    return lax.dot_general(
        a, b, (dims, ((), ())), precision=HIGHEST, preferred_element_type=jnp.float32
    )


def split3(x):
    first = x.astype(jnp.bfloat16)
    rest = x - first.astype(jnp.float32)
    second = rest.astype(jnp.bfloat16)
    third = (rest - second.astype(jnp.float32)).astype(jnp.bfloat16)
    return first, second, third


def bf16_dot(a, b):
    return jnp.dot(a, b, preferred_element_type=jnp.float32)


def turn(x, shift):
    shift = shift % LANES
    return x if shift == 0 else pltpu.roll(x, shift, 1)


def lane_group(shape, q):
    return lax.broadcasted_iota(jnp.int32, shape, 1) // q


def to_crossing(x, perm, q, store):
    tiles = x.shape[0]
    groups = LANES // q
    across = jnp.concatenate(
        [x[c * LANES : (c + 1) * LANES].T for c in range(tiles // LANES)], axis=1
    )
    moved = sum(bf16_dot(part, perm) for part in reversed(split3(across)))
    group = lane_group((q, LANES), q)
    for c in range(tiles // LANES):
        for b in range(groups):
            block = None
            for h in range(groups):
                piece = turn(moved[h * q : (h + 1) * q, c * LANES : (c + 1) * LANES], (h - b) * q)
                block = piece if block is None else jnp.where(group == h, piece, block)
            store(c * groups + b, block)


def from_crossing(load, perm, q, tiles):
    groups = LANES // q
    group = lane_group((q, LANES), q)
    parts = []
    for c in range(tiles // LANES):
        rows = []
        for h in range(groups):
            block = None
            for b in range(groups):
                piece = turn(load(c * groups + b), (b - h) * q)
                block = piece if block is None else jnp.where(group == b, piece, block)
            rows.append(block)
        parts.append(jnp.concatenate(rows, axis=0).T)
    stacked = jnp.concatenate(parts, axis=0)
    return sum(bf16_dot(perm, part) for part in reversed(split3(stacked)))


def order_kernel(q, me_ref, match_ref, knot_ref, frac_ref, obs_ref, perm_ref, weight_ref, obs_out):
    tiles = obs_ref.shape[0]
    groups = LANES // q
    me = me_ref[0]
    match = match_ref[...]
    slot = lax.broadcasted_iota(jnp.int32, (1, tiles), 1)
    peer = match // tiles
    other = match - peer * tiles
    inner = jnp.where(
        peer == me,
        jnp.minimum(slot, other) + jnp.where(slot > other, tiles, 0),
        jnp.where(peer > me, slot, other),
    )
    key = (peer * (2 * tiles) + inner).astype(jnp.float32)
    key_cols = jnp.broadcast_to(key, (LANES, tiles)).T[:, :1]
    place = jnp.sum(jnp.where(key < key_cols, 1.0, 0.0), axis=1, keepdims=True)
    cols = lax.broadcasted_iota(jnp.int32, (tiles, tiles), 1).astype(jnp.float32)
    perm = jnp.where(place == cols, 1.0, 0.0).astype(jnp.bfloat16)
    perm_ref[...] = perm

    def put(index, block):
        obs_out[index * q : (index + 1) * q, :] = block

    to_crossing(obs_ref[...], perm, q, put)

    row = lax.broadcasted_iota(jnp.int32, (SUB, tiles), 0)
    facts = jnp.where(row == 0, knot_ref[...].astype(jnp.float32), frac_ref[...])
    moved = sum(bf16_dot(part, perm) for part in reversed(split3(facts)))
    group = lane_group((SUB, LANES), q)
    knots = lax.broadcasted_iota(jnp.int32, (KNOT_DEV, LANES), 0).astype(jnp.float32)
    first_row = lax.broadcasted_iota(jnp.int32, (SUB, LANES), 0) == 0
    for c in range(tiles // LANES):
        chunk = moved[:, c * LANES : (c + 1) * LANES]
        for b in range(groups):
            block = None
            for h in range(groups):
                piece = turn(chunk, (h - b) * q)
                block = piece if block is None else jnp.where(group == h, piece, block)
            knot = block[0:1]
            frac = block[1:2]
            lanes = slice((c * groups + b) * LANES, (c * groups + b + 1) * LANES)
            weight_ref[0:KNOT_DEV, lanes] = jnp.where(knots == knot, 1.0 - frac, 0.0) + jnp.where(
                knots == knot + 1.0, frac, 0.0
            )
            edge = jnp.where(knot == KNOT_DEV - 1.0, frac, 0.0)
            weight_ref[KNOT_DEV : KNOT_DEV + SUB, lanes] = jnp.where(first_row, edge, 0.0)


def jac_kernel(q, perm_ref, jac_ref, out_ref):
    def put(index, block):
        out_ref[0, index * q : (index + 1) * q, :] = block

    to_crossing(jac_ref[0], perm_ref[...], q, put)


def crossing_values(me, arrived_ref, out_ref, q):
    out_ref[...] = arrived_ref[...]
    own = arrived_ref[pl.ds(pl.multiple_of(me * q, SUB), q), :]
    lane = lax.broadcasted_iota(jnp.int32, (q, LANES), 1)
    swapped = jnp.where(lane % q < q // 2, turn(own, -(q // 2)), turn(own, q // 2))
    out_ref[pl.ds(pl.multiple_of(me * q, SUB), q), :] = swapped


def difference(me, sent_ref, arrived_ref, out_ref, q):
    crossing_values(me, arrived_ref, out_ref, q)
    out_ref[...] = sent_ref[...] - out_ref[...]


def adjoint_kernel(q, me_ref, sent_ref, arrived_ref, jac_ref, weight_ref, diff_ref, send_ref, parts_ref):
    params, tiles, _ = jac_ref.shape
    difference(me_ref[0], sent_ref, arrived_ref, diff_ref, q)

    def block_sums(b, carry):
        rows = pl.ds(pl.multiple_of(b * q, SUB), q)
        diff = diff_ref[rows, :]
        for p in range(params):
            product = jac_ref[p, rows, :] * diff
            folded = product[0:SUB]
            for step in range(1, q // SUB):
                folded = folded + product[step * SUB : (step + 1) * SUB]
            parts_ref[b, p * SUB : (p + 1) * SUB, :] = folded
        return carry

    blocks = tiles // q
    lax.fori_loop(0, blocks, block_sums, 0)
    spread = None
    for b in range(blocks):
        term = dot(parts_ref[b], weight_ref[:, b * LANES : (b + 1) * LANES], ((1,), (1,)))
        spread = term if spread is None else spread + term
    lane = lax.broadcasted_iota(jnp.int32, (1, LANES), 1)
    send_ref[...] = jnp.zeros(send_ref.shape, jnp.float32)
    spill_row = jnp.zeros((1, LANES), jnp.float32)
    rows = []
    for p in range(params):
        total = jnp.sum(spread[p * SUB : (p + 1) * SUB], axis=0, keepdims=True)
        rows.append(total[:, :KNOT_DEV])
        spill_row = jnp.where(lane == p, total[:, KNOT_DEV : KNOT_DEV + 1], spill_row)
    rows.append(spill_row)
    block = jnp.concatenate(rows, axis=0)
    for d in range(send_ref.shape[0]):
        send_ref[d, 0 : params + 1, :] = block


def field_sums(gathered_ref, n_track, n_det, params, store):
    lane = lax.broadcasted_iota(jnp.int32, (PAD, LANES), 1)
    row = lax.broadcasted_iota(jnp.int32, (PAD, LANES), 0)
    spill = jnp.zeros((PAD, 1), jnp.float32)
    for b in range(n_track):
        total = gathered_ref[b * n_det]
        for d in range(1, n_det):
            total = total + gathered_ref[b * n_det + d]
        field = jnp.where(row < params, total, 0.0)
        field = field + jnp.where(lane == 0, spill, 0.0)
        store(b, field)
        spill = jnp.sum(
            jnp.where((lane == row) & (row < params), total[params : params + 1], 0.0),
            axis=1,
            keepdims=True,
        )


def total_of(x):
    return jnp.sum(jnp.sum(x, axis=0), keepdims=True).reshape(1, 1)


def full_dot(a_ref, b_ref):
    total = a_ref[0] * b_ref[0]
    for b in range(1, a_ref.shape[0]):
        total = total + a_ref[b] * b_ref[b]
    return jnp.sum(total, keepdims=True)


def predict(me, q, direction_ref, jac_ref, weight_ref, interp_ref, sent_ref):
    params, tiles, _ = jac_ref.shape
    n_track = direction_ref.shape[0]
    following = direction_ref[jnp.minimum(me + 1, n_track - 1)][:, 0:1]
    following = jnp.where(me + 1 < n_track, following, 0.0)
    own = direction_ref[me]
    blocks = tiles // q
    for b in range(blocks):
        lanes = slice(b * LANES, (b + 1) * LANES)
        interp_ref[b] = (
            dot(own, weight_ref[0:KNOT_DEV, lanes], ((1,), (0,)))
            + following * weight_ref[KNOT_DEV : KNOT_DEV + 1, lanes]
        )

    def block_values(b, carry):
        rows = pl.ds(pl.multiple_of(b * q, SUB), q)
        interp = interp_ref[b]
        total = jac_ref[0, rows, :] * interp[0:1]
        for p in range(1, params):
            total = total + jac_ref[p, rows, :] * interp[p : p + 1]
        sent_ref[rows, :] = total
        return carry

    lax.fori_loop(0, blocks, block_values, 0)


def first_kernel(
    q, n_det, me_ref, gathered_ref, jac_ref, weight_ref, grad_ref, norm_ref, sent_ref, interp_ref
):
    n_track = grad_ref.shape[0]

    def put(b, field):
        grad_ref[b] = field

    field_sums(gathered_ref, n_track, n_det, jac_ref.shape[0], put)
    norm_ref[...] = jnp.broadcast_to(full_dot(grad_ref, grad_ref), norm_ref.shape)
    predict(me_ref[0], q, grad_ref, jac_ref, weight_ref, interp_ref, sent_ref)


def step_kernel(
    q,
    n_det,
    me_ref,
    gathered_ref,
    jac_ref,
    weight_ref,
    grad_ref,
    direction_ref,
    norm_ref,
    knot_ref,
    residual_ref,
    diff_ref,
    grad_out,
    direction_out,
    norm_out,
    knot_out,
    residual_out,
    sent_ref,
    image_ref,
    interp_ref,
):
    n_track = grad_ref.shape[0]
    me = me_ref[0]

    def put(b, field):
        image_ref[b] = field + damping * direction_ref[b]

    field_sums(gathered_ref, n_track, n_det, jac_ref.shape[0], put)
    norm = norm_ref[0:1, 0:1]
    length = norm / full_dot(direction_ref, image_ref)
    knot_out[...] = knot_ref[...] + length * direction_ref[me]
    residual_out[...] = residual_ref[...] - length * diff_ref[...]
    for b in range(n_track):
        grad_out[b] = grad_ref[b] - length * image_ref[b]
    new_norm = full_dot(grad_out, grad_out)
    norm_out[...] = jnp.broadcast_to(new_norm, norm_out.shape)
    ratio = new_norm / norm
    for b in range(n_track):
        direction_out[b] = grad_out[b] + ratio * direction_ref[b]
    predict(me, q, direction_out, jac_ref, weight_ref, interp_ref, sent_ref)


def last_kernel(q, me_ref, sent_ref, arrived_ref, diff_ref, send_ref):
    difference(me_ref[0], sent_ref, arrived_ref, diff_ref, q)
    diff = diff_ref[...]
    squares = jnp.sum(diff * diff, axis=0, keepdims=True)
    send_ref[...] = jnp.broadcast_to(squares[None], send_ref.shape)


def restore_kernel(q, perm_ref, residual_ref, diff_ref, residual_out, diff_out):
    tiles = residual_ref.shape[0]
    for source, target in ((residual_ref, residual_out), (diff_ref, diff_out)):
        target[...] = from_crossing(
            lambda index: source[index * q : (index + 1) * q, :], perm_ref[...], q, tiles
        )


def finish_kernel(
    me_ref, squares_ref, direction_ref, norm_ref, knot_ref, residual_ref, diff_ref, knot_out, residual_out
):
    params = knot_out.shape[0]
    squares = squares_ref[0, 0:1, :]
    for d in range(1, squares_ref.shape[0]):
        squares = squares + squares_ref[d, 0:1, :]
    curvature = 0.5 * jnp.sum(squares, keepdims=True) + damping * full_dot(
        direction_ref, direction_ref
    )
    length = norm_ref[0:1, 0:1] / curvature
    knot = knot_ref[...] + length * direction_ref[me_ref[0]]
    knot_out[...] = knot[0:params]
    residual_out[...] = residual_ref[...] - length * diff_ref[...]


def call(kernel, outs, ins, scratch=()):
    return pl.pallas_call(
        kernel,
        out_shape=outs,
        in_specs=ins,
        out_specs=jax.tree.map(lambda _: VMEM, outs),
        scratch_shapes=list(scratch),
        compiler_params=PARAMS,
    )


def local(jac, obs, match, tile_knot, tile_frac):
    tiles, params, columns = jac.shape
    n_track = lax.axis_size("track")
    n_det = lax.axis_size("det")
    n_all = n_track * n_det
    q = tiles // n_track
    me = lax.axis_index("track").astype(jnp.int32).reshape(1)

    perm, weights, sent = call(
        functools.partial(order_kernel, q),
        (
            jax.ShapeDtypeStruct((tiles, tiles), jnp.bfloat16),
            f32(KNOT_DEV + SUB, n_track * LANES),
            f32(tiles, columns),
        ),
        [SMEM, VMEM, VMEM, VMEM, VMEM],
    )(me, match[None], tile_knot[None], tile_frac[None], obs)

    def crossing(values):
        return lax.all_to_all(values, "track", split_axis=0, concat_axis=0, tiled=True)

    def everywhere(values):
        return lax.all_to_all(values, ("track", "det"), split_axis=0, concat_axis=0, tiled=True)

    arrived = crossing(sent)
    jac_rows = pl.pallas_call(
        functools.partial(jac_kernel, q),
        grid=(params,),
        out_shape=f32(params, tiles, columns),
        in_specs=[
            pl.BlockSpec((tiles, tiles), lambda p: (0, 0)),
            pl.BlockSpec((1, tiles, columns), lambda p: (p, 0, 0)),
        ],
        out_specs=pl.BlockSpec((1, tiles, columns), lambda p: (p, 0, 0)),
        compiler_params=PARAMS,
    )(perm, jnp.transpose(jac, (1, 0, 2)))

    def adjoint(sent, arrived):
        diff, payload = call(
            functools.partial(adjoint_kernel, q),
            (f32(tiles, columns), f32(n_all, PAD, LANES)),
            [SMEM] + [VMEM] * 4,
            [pltpu.VMEM((n_track, params * SUB, LANES), jnp.float32)],
        )(me, sent, arrived, jac_rows, weights)
        return diff, everywhere(payload)

    field = f32(n_track, PAD, LANES)
    interp = pltpu.VMEM((n_track, PAD, LANES), jnp.float32)
    residual, gathered = adjoint(sent, arrived)
    gradient, slope_norm, sent = call(
        functools.partial(first_kernel, q, n_det),
        (field, f32(SUB, LANES), f32(tiles, columns)),
        [SMEM] + [VMEM] * 3,
        [interp],
    )(me, gathered, jac_rows, weights)
    direction = gradient
    knot_field = jnp.zeros((PAD, KNOT_DEV), jnp.float32)
    for iteration in range(ITERS - 1):
        change, gathered = adjoint(sent, crossing(sent))
        gradient, direction, slope_norm, knot_field, residual, sent = call(
            functools.partial(step_kernel, q, n_det),
            (field, field, f32(SUB, LANES), f32(PAD, KNOT_DEV), f32(tiles, columns), f32(tiles, columns)),
            [SMEM] + [VMEM] * 9,
            [pltpu.VMEM((n_track, PAD, LANES), jnp.float32), interp],
        )(
            me, gathered, jac_rows, weights, gradient, direction, slope_norm, knot_field, residual, change
        )
    change, squares = call(
        functools.partial(last_kernel, q),
        (f32(tiles, columns), f32(n_all, SUB, LANES)),
        [SMEM] + [VMEM] * 2,
    )(me, sent, crossing(sent))
    squares = everywhere(squares)
    residual, change = call(
        functools.partial(restore_kernel, q),
        (f32(tiles, columns), f32(tiles, columns)),
        [VMEM] * 3,
    )(perm, residual, change)
    return call(
        finish_kernel,
        (f32(params, KNOT_DEV), f32(tiles, columns)),
        [SMEM] + [VMEM] * 6,
    )(me, squares, direction, slope_norm, knot_field, residual, change)


def solution(mesh):
    in_specs = (P("track", None, "det"), P("track", "det"), P("track"), P("track"), P("track"))
    out_specs = (P(None, "track"), P("track", "det"))
    return jax.shard_map(local, mesh=mesh, in_specs=in_specs, out_specs=out_specs, check_vma=False)
```

time: 517 us -> 169 us (0.33); the launches traced: 507 us -> 168 us
  blocking collectives: 303 us -> 103 us
  matrix products: 61.2 us -> 0 us
  Pallas kernels: 0 us -> 41.7 us
  other arithmetic: 33.5 us -> 0 us
  local copies, waits for them, and re-layouts: 33.2 us -> 4.62 us
  starting transfers between devices: 36.3 us -> 10.3 us
  waiting for transfers between devices: 27.9 us -> 7 us
  between operations: 12.8 us -> 0.74 us
    psum x12 -> x0, blocking collectives: 266 us -> none  [the longest x4 154 us: local(): lax.psum((jnp.sum(change * change), jnp.sum(direction * direction)), ('tr...]
    all_to_all x3 -> x8, blocking collectives: 36.7 us -> 103 us  [the longest x4 56.6 us: everywhere(): lax.all_to_all(values, ('track', 'det'), split_axis=0, concat_axis=0, til...]
    dot_general x20 -> x0, matrix products: 61.2 us -> none  [the longest x4 31.6 us: adjoint(): jnp.einsum('ipw,iw->pi', jac, residual_rows, precision=highest)]
    pallas_call x0 -> x13, Pallas kernels: none -> 41.7 us  [the longest x4 14.3 us: adjoint(): call(functools.partial(adjoint_kernel, q), (f32(tiles, columns), f32(n_al...]
    gather x11 -> x0, local copies, waits for them, and re-layouts: 24.7 us -> none  [the longest x5 12.9 us: settle(): return joined[receive_order]]
    ppermute x8 -> x0, starting transfers between devices: 20.8 us -> none  [passed_along(): lax.ppermute(value, axis, [(source, source + steps) for source in range(l...]
    ppermute x8 -> x0, waiting for transfers between devices: 20.7 us -> none  [passed_along(): lax.ppermute(value, axis, [(source, source + steps) for source in range(l...]
    reduce_sum x11 -> x0, other arithmetic: 13.8 us -> none  [the longest x4 9.39 us: local(): jnp.sum(change * change)]
  transfers between devices with their start and end apart: 11 -> 2, of which waited for: 10 -> 1; matrix products, arithmetic and copies ran while one was open for 2% -> 0% of each run, Pallas kernels for 0% -> 6%
where the time goes in v1:
time: 169 us; the launch traced here: 168 us
  blocking collectives  103 us (61%)
  Pallas kernels  41.7 us (25%)
  starting transfers between devices  10.3 us (6%)
  waiting for transfers between devices  7 us (4%)
  local copies, waits for them, and re-layouts  4.62 us (3%)
    all_to_all x4, blocking collectives, everywhere(): lax.all_to_all(values, ('track', 'det'), split_axis=0, concat_axis=0, til...  56.6 us
    all_to_all x4, blocking collectives, crossing(): lax.all_to_all(values, 'track', split_axis=0, concat_axis=0, tiled=True)  46.8 us
    pallas_call x4, Pallas kernels, adjoint(): call(functools.partial(adjoint_kernel, q), (f32(tiles, columns), f32(n_al...  14.3 us
    pallas_call x3, Pallas kernels, local(): call(functools.partial(step_kernel, q, n_det), (field, field, f32(SUB, LA...  10.1 us
    pallas_call x1, Pallas kernels, local(): pl.pallas_call(functools.partial(jac_kernel, q), grid=(params,), out_shap...  9.53 us
    all_to_all x1, starting transfers between devices, crossing(): lax.all_to_all(values, 'track', split_axis=0, concat_axis=0, tiled=True)  7.28 us
    all_to_all x1, waiting for transfers between devices, everywhere(): lax.all_to_all(values, ('track', 'det'), split_axis=0, concat_axis=0, til...  7 us
    unnamed x10, local copies, waits for them, and re-layouts  4.62 us
  transfers between devices with their start and end apart: 2, of which 1 were waited for; matrix products, arithmetic and copies ran while one was open for 0% of the time, Pallas kernels for 6%

profile of v1, /device:TPU:0, one launch (start us, length us, event | category | flops | bytes accessed | tf_op | source)
XLA Modules:
  0.0 167.7 jit_solution(455206271423296910)
XLA Ops:
  0.6 0.0 copy-start.1
  0.6 0.9 copy-done.1
  1.6 0.7 copy-done.2
  2.3 0.7 copy-done.3
  3.0 0.7 copy-done.4
  3.6 1.9 %shard_map.68 = (bf16[512,512]{1,0:T(8,128)(2,1)S(1)}, f32[136,1024]{1,0:T(8,128)S(1)}, f32[512,128]{1,0:T(8,128)}) custom-call(s32[1]{0:T(128)} %bitcast.me_ref, s32[1,512]{1,0:T(1,128)S(1)} %bitcast.24, s32[1,512]{1,0:T(1,128)S(1)} %bitcast.25, f32[1,512]{1,0:T(1,128)S(1)} %bitcast.26, f32[512,128]{1,0:T(8,128)S(1)} %copy-done.1), custom_call_target="tpu_custom_call" | custom-call | tf_op jit(solution)/shard_map/pallas_call | solution.py:355
  5.6 7.3 %all-to-all-start = ((f32[8,64,128]{2,1,0:T(8,128)}), f32[8,64,128]{2,1,0:T(8,128)S(1)}, u32[]{:S(2)}, u32[]{:S(2)}) async-start(f32[8,64,128]{2,1,0:T(8,128)} %bitcast.4), calls=%async_computation | async-start | bytes 524288 | tf_op jit(solution)/shard_map/all_to_all | solution.py:366
  12.8 9.5 %shard_map.69.jac_ref = f32[12,512,128]{2,1,0:T(8,128)S(1)} custom-call(bf16[512,512]{1,0:T(8,128)(2,1)S(1)} %get-tuple-element.38.perm_ref, f32[12,512,128]{2,1,0:T(8,128)} %bitcast.27), custom_call_target="tpu_custom_call" | custom-call | tf_op jit(solution)/shard_map/pallas_call | solution.py:372
  22.4 0.0 copy-start
  22.4 1.6 copy-done
  24.0 0.0 all-to-all-done
  24.0 3.6 %shard_map.70 = (f32[512,128]{1,0:T(8,128)S(1)}, f32[32,16,128]{2,1,0:T(8,128)S(1)}) custom-call(s32[1]{0:T(128)} %bitcast.me_ref, f32[512,128]{1,0:T(8,128)} %get-tuple-element.37.sent_ref, f32[512,128]{1,0:T(8,128)S(1)} %bitcast.17, f32[12,512,128]{2,1,0:T(8,128)} %copy-done, f32[136,1024]{1,0:T(8,128)S(1)} %get-tuple-element.39.weight_ref), custom_call_target="tpu_custom_call" | custom-call | tf_op jit(solution)/shard_map/pallas_call | solution.py:385
  27.7 16.4 %all_to_all.80.gathered_ref = f32[32,16,128]{2,1,0:T(8,128)S(1)} all-to-all(f32[32,16,128]{2,1,0:T(8,128)S(1)} %get-tuple-element.40), channel_id=1, replica_groups=mesh['track'=8,'det'=4] {'track','det'}, dimensions={0} | all-to-all | bytes 524288 | tf_op jit(solution)/shard_map/all_to_all | solution.py:369
  44.1 2.8 %shard_map.71 = (f32[8,16,128]{2,1,0:T(8,128)S(1)}, f32[8,128]{1,0:T(8,128)S(1)}, f32[512,128]{1,0:T(8,128)S(1)}) custom-call(s32[1]{0:T(128)} %bitcast.me_ref, f32[32,16,128]{2,1,0:T(8,128)S(1)} %all_to_all.80.gathered_ref, f32[12,512,128]{2,1,0:T(8,128)} %copy-done, f32[136,1024]{1,0:T(8,128)S(1)} %get-tuple-element.39.weight_ref), custom_call_target="tpu_custom_call" | custom-call | tf_op jit(solution)/shard_map/pallas_call | solution.py:396
  46.9 11.7 %all_to_all.81 = f32[8,64,128]{2,1,0:T(8,128)S(1)} all-to-all(f32[8,64,128]{2,1,0:T(8,128)S(1)} %bitcast.18), channel_id=1, replica_groups=mesh['track'=8,'det'=4] {'track'}, dimensions={0} | all-to-all | bytes 524288 | tf_op jit(solution)/shard_map/all_to_all | solution.py:366
  58.6 3.6 %shard_map.72 = (f32[512,128]{1,0:T(8,128)S(1)}, f32[32,16,128]{2,1,0:T(8,128)S(1)}) custom-call(s32[1]{0:T(128)} %bitcast.me_ref, f32[512,128]{1,0:T(8,128)S(1)} %get-tuple-element.41.sent_ref, f32[512,128]{1,0:T(8,128)S(1)} %bitcast.19, f32[12,512,128]{2,1,0:T(8,128)} %copy-done, f32[136,1024]{1,0:T(8,128)S(1)} %get-tuple-element.39.weight_ref), custom_call_target="tpu_custom_call" | custom-call | tf_op jit(solution)/shard_map/pallas_call | solution.py:385
  62.2 13.4 %all_to_all.82.gathered_ref = f32[32,16,128]{2,1,0:T(8,128)S(1)} all-to-all(f32[32,16,128]{2,1,0:T(8,128)S(1)} %get-tuple-element.42), channel_id=1, replica_groups=mesh['track'=8,'det'=4] {'track','det'}, dimensions={0} | all-to-all | bytes 524288 | tf_op jit(solution)/shard_map/all_to_all | solution.py:369
  75.6 3.2 %shard_map.73 = (f32[8,16,128]{2,1,0:T(8,128)S(1)}, f32[8,16,128]{2,1,0:T(8,128)S(1)}, f32[8,128]{1,0:T(8,128)S(1)}, f32[16,128]{1,0:T(8,128)S(1)}, f32[512,128]{1,0:T(8,128)S(1)}, /*index=5*/f32[512,128]{1,0:T(8,128)S(1)}) custom-call(s32[1]{0:T(128)} %bitcast.me_ref, f32[32,16,128]{2,1,0:T(8,128)S(1)} %all_to_all.82.gathered_ref, f32[12,512,128]{2,1,0:T(8,128)} %copy-done, ...), custom_call_target="tpu_custom_call" | custom-call | tf_op jit(solution)/shard_map/pallas_call | solution.py:406
  78.7 11.7 %all_to_all.83 = f32[8,64,128]{2,1,0:T(8,128)S(1)} all-to-all(f32[8,64,128]{2,1,0:T(8,128)S(1)} %bitcast.16), channel_id=1, replica_groups=mesh['track'=8,'det'=4] {'track'}, dimensions={0} | all-to-all | bytes 524288 | tf_op jit(solution)/shard_map/all_to_all | solution.py:366
  90.4 3.6 %shard_map.74 = (f32[512,128]{1,0:T(8,128)S(1)}, f32[32,16,128]{2,1,0:T(8,128)S(1)}) custom-call(s32[1]{0:T(128)} %bitcast.me_ref, f32[512,128]{1,0:T(8,128)S(1)} %get-tuple-element.47.sent_ref, f32[512,128]{1,0:T(8,128)S(1)} %bitcast.20, f32[12,512,128]{2,1,0:T(8,128)} %copy-done, f32[136,1024]{1,0:T(8,128)S(1)} %get-tuple-element.39.weight_ref), custom_call_target="tpu_custom_call" | custom-call | tf_op jit(solution)/shard_map/pallas_call | solution.py:385
  94.0 13.4 %all_to_all.84.gathered_ref = f32[32,16,128]{2,1,0:T(8,128)S(1)} all-to-all(f32[32,16,128]{2,1,0:T(8,128)S(1)} %get-tuple-element.48), channel_id=1, replica_groups=mesh['track'=8,'det'=4] {'track','det'}, dimensions={0} | all-to-all | bytes 524288 | tf_op jit(solution)/shard_map/all_to_all | solution.py:369
  107.4 3.2 %shard_map.75 = (f32[8,16,128]{2,1,0:T(8,128)S(1)}, f32[8,16,128]{2,1,0:T(8,128)S(1)}, f32[8,128]{1,0:T(8,128)S(1)}, f32[16,128]{1,0:T(8,128)S(1)}, f32[512,128]{1,0:T(8,128)S(1)}, /*index=5*/f32[512,128]{1,0:T(8,128)S(1)}) custom-call(s32[1]{0:T(128)} %bitcast.me_ref, f32[32,16,128]{2,1,0:T(8,128)S(1)} %all_to_all.84.gathered_ref, f32[12,512,128]{2,1,0:T(8,128)} %copy-done, ...), custom_call_target="tpu_custom_call" | custom-call | tf_op jit(solution)/shard_map/pallas_call | solution.py:406
  110.6 11.7 %all_to_all.85 = f32[8,64,128]{2,1,0:T(8,128)S(1)} all-to-all(f32[8,64,128]{2,1,0:T(8,128)S(1)} %bitcast.15), channel_id=1, replica_groups=mesh['track'=8,'det'=4] {'track'}, dimensions={0} | all-to-all | bytes 524288 | tf_op jit(solution)/shard_map/all_to_all | solution.py:366
  122.2 3.6 %shard_map.76 = (f32[512,128]{1,0:T(8,128)S(1)}, f32[32,16,128]{2,1,0:T(8,128)S(1)}) custom-call(s32[1]{0:T(128)} %bitcast.me_ref, f32[512,128]{1,0:T(8,128)S(1)} %get-tuple-element.55.sent_ref, f32[512,128]{1,0:T(8,128)S(1)} %bitcast.21, f32[12,512,128]{2,1,0:T(8,128)} %copy-done, f32[136,1024]{1,0:T(8,128)S(1)} %get-tuple-element.39.weight_ref), custom_call_target="tpu_custom_call" | custom-call | tf_op jit(solution)/shard_map/pallas_call | solution.py:385
  125.8 13.4 %all_to_all.86.gathered_ref = f32[32,16,128]{2,1,0:T(8,128)S(1)} all-to-all(f32[32,16,128]{2,1,0:T(8,128)S(1)} %get-tuple-element.56), channel_id=1, replica_groups=mesh['track'=8,'det'=4] {'track','det'}, dimensions={0} | all-to-all | bytes 524288 | tf_op jit(solution)/shard_map/all_to_all | solution.py:369
  139.2 3.8 %shard_map.77 = (f32[8,16,128]{2,1,0:T(8,128)}, f32[8,16,128]{2,1,0:T(8,128)S(1)}, f32[8,128]{1,0:T(8,128)S(1)}, f32[16,128]{1,0:T(8,128)S(1)}, f32[512,128]{1,0:T(8,128)S(1)}, /*index=5*/f32[512,128]{1,0:T(8,128)S(1)}) custom-call(s32[1]{0:T(128)} %bitcast.me_ref, f32[32,16,128]{2,1,0:T(8,128)S(1)} %all_to_all.86.gathered_ref, f32[12,512,128]{2,1,0:T(8,128)} %copy-done, ...), custom_call_target="tpu_custom_call" | custom-call | tf_op jit(solution)/shard_map/pallas_call | solution.py:406
  143.0 11.7 %all_to_all.87 = f32[8,64,128]{2,1,0:T(8,128)S(1)} all-to-all(f32[8,64,128]{2,1,0:T(8,128)S(1)} %bitcast.22), channel_id=1, replica_groups=mesh['track'=8,'det'=4] {'track'}, dimensions={0} | all-to-all | bytes 524288 | tf_op jit(solution)/shard_map/all_to_all | solution.py:366
  154.7 0.9 shard_map.78
  155.5 3.0 %all-to-all-start.9 = ((f32[32,8,128]{2,1,0:T(8,128)}), f32[32,8,128]{2,1,0:T(8,128)S(1)}, u32[]{:S(2)}, u32[]{:S(2)}) async-start(f32[32,8,128]{2,1,0:T(8,128)} %get-tuple-element.64), calls=%async_computation.9 | async-start | bytes 262144 | tf_op jit(solution)/shard_map/all_to_all | solution.py:369
  158.5 1.2 shard_map.79
  159.8 7.0 %all-to-all-done.9.squares_ref = f32[32,8,128]{2,1,0:T(8,128)S(1)} async-done(((f32[32,8,128]{2,1,0:T(8,128)}), f32[32,8,128]{2,1,0:T(8,128)S(1)}, u32[]{:S(2)}, u32[]{:S(2)}) %all-to-all-start.9) | async-done | bytes 131104 | tf_op jit(solution)/shard_map/all_to_all | solution.py:369
  166.8 0.9 shard_map.80
  (4 shorter events, 0.0 us)
Async XLA Ops:
  0.6 1.0 copy-start.1
  1.6 0.7 copy-start.2
  2.3 0.7 copy-start.3
  3.0 0.7 copy-start.4
  5.6 18.5 %all-to-all-start = ((f32[8,64,128]{2,1,0:T(8,128)}), f32[8,64,128]{2,1,0:T(8,128)S(1)}, u32[]{:S(2)}, u32[]{:S(2)}) async-start(f32[8,64,128]{2,1,0:T(8,128)} %bitcast.4), calls=%async_computation | async-start | bytes 524288 | tf_op jit(solution)/shard_map/all_to_all | solution.py:366
  22.4 1.6 copy-start
  155.5 11.2 %all-to-all-start.9 = ((f32[32,8,128]{2,1,0:T(8,128)}), f32[32,8,128]{2,1,0:T(8,128)S(1)}, u32[]{:S(2)}, u32[]{:S(2)}) async-start(f32[32,8,128]{2,1,0:T(8,128)} %get-tuple-element.64), calls=%async_computation.9 | async-start | bytes 262144 | tf_op jit(solution)/shard_map/all_to_all | solution.py:369

commit v2 on v1

--- a/solution.py
+++ b/solution.py
@@ -12,7 +12,7 @@
 LANES = 128
 SUB = 8
 PAD = 16
-VMEM_BYTES = 50 * 2**20
+VMEM_BYTES = 14 * 2**20
 
 
 damping = 1.0
@@ -384,11 +384,11 @@
     def adjoint(sent, arrived):
         diff, payload = call(
             functools.partial(adjoint_kernel, q),
-            (f32(tiles, columns), f32(n_all, PAD, LANES)),
+            (f32(tiles, columns), f32(1, PAD, LANES)),
             [SMEM] + [VMEM] * 4,
             [pltpu.VMEM((n_track, params * SUB, LANES), jnp.float32)],
         )(me, sent, arrived, jac_rows, weights)
-        return diff, everywhere(payload)
+        return diff, lax.all_gather(payload, ("track", "det"), axis=0, tiled=True)
 
     field = f32(n_track, PAD, LANES)
     interp = pltpu.VMEM((n_track, PAD, LANES), jnp.float32)

time: 169 us -> 259 us (1.53)
  blocking collectives: 103 us -> 206 us
  Pallas kernels: 41.7 us -> 24.2 us
  local copies, waits for them, and re-layouts: 4.62 us -> 9.61 us
    all_gather x0 -> x4, blocking collectives: none -> 157 us  [adjoint(): return (diff, lax.all_gather(payload, ('track', 'det'), axis=0, tiled=True))]
    all_to_all x4 -> x0, blocking collectives: 56.6 us -> none  [everywhere(): lax.all_to_all(values, ('track', 'det'), split_axis=0, concat_axis=0, til...]
    pallas_call x4, Pallas kernels: 14.3 us -> 7.58 us  [adjoint(): call(functools.partial(adjoint_kernel, q), (f32(tiles, columns), f32(1, P...]
    pallas_call x3, Pallas kernels: 10.1 us -> 4.42 us  [local(): call(functools.partial(step_kernel, q, n_det), (field, field, f32(SUB, LA...]
    unnamed x10 -> x20, local copies, waits for them, and re-layouts: 4.62 us -> 9.61 us
    pallas_call x1, Pallas kernels: 9.53 us -> 6.38 us  [local(): pl.pallas_call(functools.partial(jac_kernel, q), grid=(params,), out_shap...]
  transfers between devices with their start and end apart: 2 -> 2, of which waited for: 1 -> 1; matrix products, arithmetic and copies ran while one was open for 0% -> 0% of each run, Pallas kernels for 6% -> 3%
where the time goes in v2:
time: 259 us; the launch traced here: 258 us
  blocking collectives  206 us (80%)
  Pallas kernels  24.2 us (9%)
  starting transfers between devices  11.4 us (4%)
  local copies, waits for them, and re-layouts  9.61 us (4%)
  waiting for transfers between devices  5.96 us (2%)
    all_gather x4, blocking collectives, adjoint(): return (diff, lax.all_gather(payload, ('track', 'det'), axis=0, tiled=True))  157 us
    all_to_all x4, blocking collectives, crossing(): lax.all_to_all(values, 'track', split_axis=0, concat_axis=0, tiled=True)  48.5 us
    unnamed x20, local copies, waits for them, and re-layouts  9.61 us
    pallas_call x4, Pallas kernels, adjoint(): call(functools.partial(adjoint_kernel, q), (f32(tiles, columns), f32(1, P...  7.58 us
    all_to_all x1, starting transfers between devices, crossing(): lax.all_to_all(values, 'track', split_axis=0, concat_axis=0, tiled=True)  7.28 us
    pallas_call x1, Pallas kernels, local(): pl.pallas_call(functools.partial(jac_kernel, q), grid=(params,), out_shap...  6.38 us
    all_to_all x1, waiting for transfers between devices, everywhere(): lax.all_to_all(values, ('track', 'det'), split_axis=0, concat_axis=0, til...  5.96 us
  transfers between devices with their start and end apart: 2, of which 1 were waited for; matrix products, arithmetic and copies ran while one was open for 0% of the time, Pallas kernels for 3%

profile of v2, /device:TPU:0, one launch (start us, length us, event | category | flops | bytes accessed | tf_op | source)
XLA Modules:
  0.0 257.8 jit_solution(12253090322758053648)
XLA Ops:
  0.6 0.9 copy-done.6
  2.3 0.7 copy-done.8
  3.6 1.9 shard_map.68
  5.6 0.8 copy-done
  6.4 0.8 copy-done.3
  7.2 7.3 %all-to-all-start = ((f32[8,64,128]{2,1,0:T(8,128)}), f32[8,64,128]{2,1,0:T(8,128)S(1)}, u32[]{:S(2)}, u32[]{:S(2)}) async-start(f32[8,64,128]{2,1,0:T(8,128)} %bitcast.4), calls=%async_computation | async-start | bytes 524288 | tf_op jit(solution)/shard_map/all_to_all | solution.py:366
  14.5 1.9 copy-done.2
  16.3 1.0 copy-done.4
  17.4 6.4 %shard_map.69.jac_ref = f32[12,512,128]{2,1,0:T(8,128)S(1)} custom-call(bf16[512,512]{1,0:T(8,128)(2,1)S(1)} %copy-done.4, f32[12,512,128]{2,1,0:T(8,128)S(1)} %bitcast.15), custom_call_target="tpu_custom_call" | custom-call | tf_op jit(solution)/shard_map/pallas_call | solution.py:372
  23.8 1.0 copy-done.1
  24.8 2.6 %shard_map.70 = (f32[512,128]{1,0:T(8,128)S(1)}, f32[1,16,128]{2,1,0:T(8,128)S(1)}) custom-call(s32[1]{0:T(128)} %bitcast.me_ref, f32[512,128]{1,0:T(8,128)} %get-tuple-element.37.sent_ref, f32[512,128]{1,0:T(8,128)S(1)} %bitcast.18, f32[12,512,128]{2,1,0:T(8,128)S(1)} %shard_map.69.jac_ref, f32[136,1024]{1,0:T(8,128)S(1)} %copy-done.1), custom_call_target="tpu_custom_call" | custom-call | tf_op jit(solution)/shard_map/pallas_call | solution.py:385
  27.4 42.6 %all_gather.12.gathered_ref = f32[32,16,128]{2,1,0:T(8,128)S(1)} all-gather(f32[1,16,128]{2,1,0:T(8,128)S(1)} %get-tuple-element.40), channel_id=1, replica_groups=mesh['track'=8,'det'=4] {'track','det'}, dimensions={0}, use_global_device_ids=true | all-gather | bytes 270336 | tf_op jit(solution)/shard_map/all_gather | solution.py:391
  70.1 0.9 shard_map.71
  71.0 12.1 %all_to_all.60 = f32[8,64,128]{2,1,0:T(8,128)S(1)} all-to-all(f32[8,64,128]{2,1,0:T(8,128)S(1)} %bitcast.19), channel_id=1, replica_groups=mesh['track'=8,'det'=4] {'track'}, dimensions={0} | all-to-all | bytes 524288 | tf_op jit(solution)/shard_map/all_to_all | solution.py:366
  83.1 1.7 shard_map.72
  84.8 37.0 %all_gather.13.gathered_ref = f32[32,16,128]{2,1,0:T(8,128)S(1)} all-gather(f32[1,16,128]{2,1,0:T(8,128)S(1)} %get-tuple-element.42), channel_id=1, replica_groups=mesh['track'=8,'det'=4] {'track','det'}, dimensions={0}, use_global_device_ids=true | all-gather | bytes 270336 | tf_op jit(solution)/shard_map/all_gather | solution.py:391
  121.8 1.3 shard_map.73
  123.1 12.1 %all_to_all.61 = f32[8,64,128]{2,1,0:T(8,128)S(1)} all-to-all(f32[8,64,128]{2,1,0:T(8,128)S(1)} %bitcast.17), channel_id=1, replica_groups=mesh['track'=8,'det'=4] {'track'}, dimensions={0} | all-to-all | bytes 524288 | tf_op jit(solution)/shard_map/all_to_all | solution.py:366
  135.2 1.7 shard_map.74
  136.9 40.7 %all_gather.14.gathered_ref = f32[32,16,128]{2,1,0:T(8,128)S(1)} all-gather(f32[1,16,128]{2,1,0:T(8,128)S(1)} %get-tuple-element.48), channel_id=1, replica_groups=mesh['track'=8,'det'=4] {'track','det'}, dimensions={0}, use_global_device_ids=true | all-gather | bytes 270336 | tf_op jit(solution)/shard_map/all_gather | solution.py:391
  177.6 1.3 shard_map.75
  178.9 12.1 %all_to_all.62 = f32[8,64,128]{2,1,0:T(8,128)S(1)} all-to-all(f32[8,64,128]{2,1,0:T(8,128)S(1)} %bitcast.16), channel_id=1, replica_groups=mesh['track'=8,'det'=4] {'track'}, dimensions={0} | all-to-all | bytes 524288 | tf_op jit(solution)/shard_map/all_to_all | solution.py:366
  191.0 1.7 shard_map.76
  192.6 37.0 %all_gather.15.gathered_ref = f32[32,16,128]{2,1,0:T(8,128)S(1)} all-gather(f32[1,16,128]{2,1,0:T(8,128)S(1)} %get-tuple-element.56), channel_id=1, replica_groups=mesh['track'=8,'det'=4] {'track','det'}, dimensions={0}, use_global_device_ids=true | all-gather | bytes 270336 | tf_op jit(solution)/shard_map/all_gather | solution.py:391
  229.7 1.9 shard_map.77
  231.6 12.1 %all_to_all.63 = f32[8,64,128]{2,1,0:T(8,128)S(1)} all-to-all(f32[8,64,128]{2,1,0:T(8,128)S(1)} %bitcast.23), channel_id=1, replica_groups=mesh['track'=8,'det'=4] {'track'}, dimensions={0} | all-to-all | bytes 524288 | tf_op jit(solution)/shard_map/all_to_all | solution.py:366
  243.7 0.8 shard_map.78
  244.5 4.1 %all-to-all-start.5 = ((f32[32,8,128]{2,1,0:T(8,128)}), f32[32,8,128]{2,1,0:T(8,128)S(1)}, u32[]{:S(2)}, u32[]{:S(2)}) async-start(f32[32,8,128]{2,1,0:T(8,128)} %get-tuple-element.64), calls=%async_computation.5 | async-start | bytes 262144 | tf_op jit(solution)/shard_map/all_to_all | solution.py:369
  248.6 1.0 copy-done.5
  249.7 1.2 shard_map.79
  250.9 6.0 %all-to-all-done.5.squares_ref = f32[32,8,128]{2,1,0:T(8,128)S(1)} async-done(((f32[32,8,128]{2,1,0:T(8,128)}), f32[32,8,128]{2,1,0:T(8,128)S(1)}, u32[]{:S(2)}, u32[]{:S(2)}) %all-to-all-start.5) | async-done | bytes 131104 | tf_op jit(solution)/shard_map/all_to_all | solution.py:369
  256.8 0.9 shard_map.80
  (14 shorter events, 1.4 us)
Async XLA Ops:
  0.6 1.0 copy-start.6
  1.6 0.7 copy-start.7
  2.3 0.7 copy-start.8
  3.0 0.7 copy-start.9
  5.6 0.8 copy-start
  6.4 0.8 copy-start.3
  7.2 16.6 %all-to-all-start = ((f32[8,64,128]{2,1,0:T(8,128)}), f32[8,64,128]{2,1,0:T(8,128)S(1)}, u32[]{:S(2)}, u32[]{:S(2)}) async-start(f32[8,64,128]{2,1,0:T(8,128)} %bitcast.4), calls=%async_computation | async-start | bytes 524288 | tf_op jit(solution)/shard_map/all_to_all | solution.py:366
  14.4 1.9 copy-start.2
  16.3 1.0 copy-start.4
  23.8 1.1 copy-start.1
  244.5 12.3 %all-to-all-start.5 = ((f32[32,8,128]{2,1,0:T(8,128)}), f32[32,8,128]{2,1,0:T(8,128)S(1)}, u32[]{:S(2)}, u32[]{:S(2)}) async-start(f32[32,8,128]{2,1,0:T(8,128)} %get-tuple-element.64), calls=%async_computation.5 | async-start | bytes 262144 | tf_op jit(solution)/shard_map/all_to_all | solution.py:369
  248.6 1.0 copy-start.5

commit v3 on v1

--- a/solution.py
+++ b/solution.py
@@ -1,4 +1,5 @@
 import functools
+import math
 
 import jax
 import jax.numpy as jnp
@@ -12,13 +13,14 @@
 LANES = 128
 SUB = 8
 PAD = 16
-VMEM_BYTES = 50 * 2**20
+VMEM_BYTES = 14 * 2**20
 
 
 damping = 1.0
 
 SMEM = pl.BlockSpec(memory_space=pltpu.SMEM)
 VMEM = pl.BlockSpec(memory_space=pltpu.VMEM)
+ANY = pl.BlockSpec(memory_space=pl.ANY)
 PARAMS = pltpu.CompilerParams(vmem_limit_bytes=VMEM_BYTES)
 HIGHEST = lax.Precision.HIGHEST
 
@@ -54,21 +56,31 @@
     return lax.broadcasted_iota(jnp.int32, shape, 1) // q
 
 
-def to_crossing(x, perm, q, store):
-    tiles = x.shape[0]
+def to_crossing(arrays, perm, q, store):
+    tiles = arrays[0].shape[0]
     groups = LANES // q
-    across = jnp.concatenate(
-        [x[c * LANES : (c + 1) * LANES].T for c in range(tiles // LANES)], axis=1
-    )
-    moved = sum(bf16_dot(part, perm) for part in reversed(split3(across)))
+    stacked = []
+    for x in arrays:
+        across = jnp.concatenate(
+            [x[c * LANES : (c + 1) * LANES].T for c in range(tiles // LANES)], axis=1
+        )
+        stacked.extend(split3(across))
+    moved = bf16_dot(jnp.concatenate(stacked, axis=0), perm)
     group = lane_group((q, LANES), q)
-    for c in range(tiles // LANES):
-        for b in range(groups):
-            block = None
-            for h in range(groups):
-                piece = turn(moved[h * q : (h + 1) * q, c * LANES : (c + 1) * LANES], (h - b) * q)
-                block = piece if block is None else jnp.where(group == h, piece, block)
-            store(c * groups + b, block)
+    for index in range(len(arrays)):
+        third, second, first = (
+            moved[(3 * index + part) * LANES : (3 * index + part + 1) * LANES] for part in (2, 1, 0)
+        )
+        whole = third + second + first
+        for c in range(tiles // LANES):
+            for b in range(groups):
+                block = None
+                for h in range(groups):
+                    piece = turn(
+                        whole[h * q : (h + 1) * q, c * LANES : (c + 1) * LANES], (h - b) * q
+                    )
+                    block = piece if block is None else jnp.where(group == h, piece, block)
+                store(index, c * groups + b, block)
 
 
 def from_crossing(load, perm, q, tiles):
@@ -88,8 +100,31 @@
     return sum(bf16_dot(perm, part) for part in reversed(split3(stacked)))
 
 
-def order_kernel(q, me_ref, match_ref, knot_ref, frac_ref, obs_ref, perm_ref, weight_ref, obs_out):
+def order_kernel(
+    q,
+    me_ref,
+    match_hbm,
+    knot_hbm,
+    frac_hbm,
+    obs_hbm,
+    perm_ref,
+    weight_ref,
+    obs_out,
+    match_ref,
+    knot_ref,
+    frac_ref,
+    obs_ref,
+    sems,
+):
     tiles = obs_ref.shape[0]
+    pairs = ((match_hbm, match_ref), (knot_hbm, knot_ref), (frac_hbm, frac_ref), (obs_hbm, obs_ref))
+    copies = [
+        pltpu.make_async_copy(source, target, sems.at[index])
+        for index, (source, target) in enumerate(pairs)
+    ]
+    for copy in copies:
+        copy.start()
+    copies[0].wait()
     groups = LANES // q
     me = me_ref[0]
     match = match_ref[...]
@@ -108,11 +143,14 @@
     perm = jnp.where(place == cols, 1.0, 0.0).astype(jnp.bfloat16)
     perm_ref[...] = perm
 
-    def put(index, block):
+    def put(_, index, block):
         obs_out[index * q : (index + 1) * q, :] = block
 
-    to_crossing(obs_ref[...], perm, q, put)
-
+    copies[3].wait()
+    to_crossing([obs_ref[...]], perm, q, put)
+
+    copies[1].wait()
+    copies[2].wait()
     row = lax.broadcasted_iota(jnp.int32, (SUB, tiles), 0)
     facts = jnp.where(row == 0, knot_ref[...].astype(jnp.float32), frac_ref[...])
     moved = sum(bf16_dot(part, perm) for part in reversed(split3(facts)))
@@ -136,11 +174,21 @@
             weight_ref[KNOT_DEV : KNOT_DEV + SUB, lanes] = jnp.where(first_row, edge, 0.0)
 
 
-def jac_kernel(q, perm_ref, jac_ref, out_ref):
-    def put(index, block):
-        out_ref[0, index * q : (index + 1) * q, :] = block
-
-    to_crossing(jac_ref[0], perm_ref[...], q, put)
+def jac_kernel(q, together, perm_ref, jac_hbm, out_ref, jac_ref, sems):
+    params = jac_ref.shape[0]
+    copies = [
+        pltpu.make_async_copy(jac_hbm.at[p], jac_ref.at[p], sems.at[p]) for p in range(params)
+    ]
+    for copy in copies:
+        copy.start()
+    for first in range(0, params, together):
+        for p in range(first, first + together):
+            copies[p].wait()
+
+        def put(index, block_index, block):
+            out_ref[first + index, block_index * q : (block_index + 1) * q, :] = block
+
+        to_crossing([jac_ref[p] for p in range(first, first + together)], perm_ref[...], q, put)
 
 
 def crossing_values(me, arrived_ref, out_ref, q):
@@ -321,9 +369,9 @@
     me_ref, squares_ref, direction_ref, norm_ref, knot_ref, residual_ref, diff_ref, knot_out, residual_out
 ):
     params = knot_out.shape[0]
-    squares = squares_ref[0, 0:1, :]
+    squares = squares_ref[0]
     for d in range(1, squares_ref.shape[0]):
-        squares = squares + squares_ref[d, 0:1, :]
+        squares = squares + squares_ref[d]
     curvature = 0.5 * jnp.sum(squares, keepdims=True) + damping * full_dot(
         direction_ref, direction_ref
     )
@@ -359,7 +407,14 @@
             f32(KNOT_DEV + SUB, n_track * LANES),
             f32(tiles, columns),
         ),
-        [SMEM, VMEM, VMEM, VMEM, VMEM],
+        [SMEM, ANY, ANY, ANY, ANY],
+        [
+            pltpu.VMEM((1, tiles), jnp.int32),
+            pltpu.VMEM((1, tiles), jnp.int32),
+            pltpu.VMEM((1, tiles), jnp.float32),
+            pltpu.VMEM((tiles, columns), jnp.float32),
+            pltpu.SemaphoreType.DMA((4,)),
+        ],
     )(me, match[None], tile_knot[None], tile_frac[None], obs)
 
     def crossing(values):
@@ -369,16 +424,14 @@
         return lax.all_to_all(values, ("track", "det"), split_axis=0, concat_axis=0, tiled=True)
 
     arrived = crossing(sent)
-    jac_rows = pl.pallas_call(
-        functools.partial(jac_kernel, q),
-        grid=(params,),
-        out_shape=f32(params, tiles, columns),
-        in_specs=[
-            pl.BlockSpec((tiles, tiles), lambda p: (0, 0)),
-            pl.BlockSpec((1, tiles, columns), lambda p: (p, 0, 0)),
+    jac_rows = call(
+        functools.partial(jac_kernel, q, math.gcd(params, 3)),
+        f32(params, tiles, columns),
+        [VMEM, ANY],
+        [
+            pltpu.VMEM((params, tiles, columns), jnp.float32),
+            pltpu.SemaphoreType.DMA((params,)),
         ],
-        out_specs=pl.BlockSpec((1, tiles, columns), lambda p: (p, 0, 0)),
-        compiler_params=PARAMS,
     )(perm, jnp.transpose(jac, (1, 0, 2)))
 
     def adjoint(sent, arrived):
@@ -413,7 +466,7 @@
         )
     change, squares = call(
         functools.partial(last_kernel, q),
-        (f32(tiles, columns), f32(n_all, SUB, LANES)),
+        (f32(tiles, columns), f32(n_all, 1, LANES)),
         [SMEM] + [VMEM] * 2,
     )(me, sent, crossing(sent))
     squares = everywhere(squares)

time: 169 us -> 151 us (0.89)
  Pallas kernels: 41.7 us -> 21.6 us
  local copies, waits for them, and re-layouts: 4.62 us -> 9.61 us
  blocking collectives: 103 us -> 101 us
    pallas_call x4, Pallas kernels: 14.3 us -> 7.61 us  [adjoint(): call(functools.partial(adjoint_kernel, q), (f32(tiles, columns), f32(n_al...]
    pallas_call x3, Pallas kernels: 10.1 us -> 4.42 us  [local(): call(functools.partial(step_kernel, q, n_det), (field, field, f32(SUB, LA...]
    pallas_call x1, Pallas kernels: 9.53 us -> 4.01 us  [local(): call(functools.partial(jac_kernel, q, math.gcd(params, 3)), f32(params, t...]
    unnamed x10 -> x20, local copies, waits for them, and re-layouts: 4.62 us -> 9.61 us
    all_to_all x1, waiting for transfers between devices: 7 us -> 4.81 us  [everywhere(): lax.all_to_all(values, ('track', 'det'), split_axis=0, concat_axis=0, til...]
    all_to_all x1, waiting for transfers between devices: 0.01 us -> 1.97 us  [crossing(): lax.all_to_all(values, 'track', split_axis=0, concat_axis=0, tiled=True)]
    all_to_all x4, blocking collectives: 56.6 us -> 54.7 us  [everywhere(): lax.all_to_all(values, ('track', 'det'), split_axis=0, concat_axis=0, til...]
    pallas_call x1, Pallas kernels: 2.81 us -> 0.92 us  [local(): call(functools.partial(first_kernel, q, n_det), (field, f32(SUB, LANES),...]
  transfers between devices with their start and end apart: 2 -> 2, of which waited for: 1 -> 2; matrix products, arithmetic and copies ran while one was open for 0% -> 0% of each run, Pallas kernels for 6% -> 3%
where the time goes in v3:
time: 151 us; the launch traced here: 150 us
  blocking collectives  101 us (67%)
  Pallas kernels  21.6 us (14%)
  starting transfers between devices  10.3 us (7%)
  local copies, waits for them, and re-layouts  9.61 us (6%)
  waiting for transfers between devices  6.78 us (4%)
    all_to_all x4, blocking collectives, everywhere(): lax.all_to_all(values, ('track', 'det'), split_axis=0, concat_axis=0, til...  54.7 us
    all_to_all x4, blocking collectives, crossing(): lax.all_to_all(values, 'track', split_axis=0, concat_axis=0, tiled=True)  46.8 us
    unnamed x20, local copies, waits for them, and re-layouts  9.61 us
    pallas_call x4, Pallas kernels, adjoint(): call(functools.partial(adjoint_kernel, q), (f32(tiles, columns), f32(n_al...  7.61 us
    all_to_all x1, starting transfers between devices, crossing(): lax.all_to_all(values, 'track', split_axis=0, concat_axis=0, tiled=True)  7.28 us
    all_to_all x1, waiting for transfers between devices, everywhere(): lax.all_to_all(values, ('track', 'det'), split_axis=0, concat_axis=0, til...  4.81 us
    pallas_call x3, Pallas kernels, local(): call(functools.partial(step_kernel, q, n_det), (field, field, f32(SUB, LA...  4.42 us
    pallas_call x1, Pallas kernels, local(): call(functools.partial(jac_kernel, q, math.gcd(params, 3)), f32(params, t...  4.01 us
  transfers between devices with their start and end apart: 2, of which 2 were waited for; matrix products, arithmetic and copies ran while one was open for 0% of the time, Pallas kernels for 3%

profile of v3, /device:TPU:0, one launch (start us, length us, event | category | flops | bytes accessed | tf_op | source)
XLA Modules:
  0.0 150.4 jit_solution(7155468941991386278)
XLA Ops:
  0.6 0.9 copy-done.6
  3.6 1.7 %shard_map.68 = (bf16[512,512]{1,0:T(8,128)(2,1)S(1)}, f32[136,1024]{1,0:T(8,128)S(1)}, f32[512,128]{1,0:T(8,128)}) custom-call(s32[1]{0:T(128)} %bitcast.me_ref, s32[1,512]{1,0:T(1,128)S(1)} %bitcast.25, s32[1,512]{1,0:T(1,128)S(1)} %bitcast.26, f32[1,512]{1,0:T(1,128)S(1)} %bitcast.27, f32[512,128]{1,0:T(8,128)S(1)} %copy-done.6), custom_call_target="tpu_custom_call" | custom-call | tf_op jit(solution)/shard_map/pallas_call | solution.py:403
  5.3 0.8 copy-done
  6.1 0.8 copy-done.3
  6.9 7.3 %all-to-all-start = ((f32[8,64,128]{2,1,0:T(8,128)}), f32[8,64,128]{2,1,0:T(8,128)S(1)}, u32[]{:S(2)}, u32[]{:S(2)}) async-start(f32[8,64,128]{2,1,0:T(8,128)} %bitcast.4), calls=%async_computation | async-start | bytes 524288 | tf_op jit(solution)/shard_map/all_to_all | solution.py:421
  14.2 1.9 %copy-done.2 = f32[512,12,128]{2,0,1:T(8,128)S(1)} copy-done((f32[512,12,128]{2,0,1:T(8,128)S(1)}, f32[512,12,128]{2,0,1:T(8,128)}, u32[]{:S(2)}) %copy-start.2) | copy-done | bytes 3145752
  16.1 1.0 copy-done.4
  17.1 4.0 %shard_map.69.jac_ref = f32[12,512,128]{2,1,0:T(8,128)S(1)} custom-call(bf16[512,512]{1,0:T(8,128)(2,1)S(1)} %copy-done.4, f32[12,512,128]{2,1,0:T(8,128)S(1)} %bitcast.15), custom_call_target="tpu_custom_call" | custom-call | tf_op jit(solution)/shard_map/pallas_call | solution.py:427
  21.1 2.0 %all-to-all-done = f32[8,64,128]{2,1,0:T(8,128)S(1)} async-done(((f32[8,64,128]{2,1,0:T(8,128)}), f32[8,64,128]{2,1,0:T(8,128)S(1)}, u32[]{:S(2)}, u32[]{:S(2)}) %all-to-all-start) | async-done | bytes 262176 | tf_op jit(solution)/shard_map/all_to_all | solution.py:421
  23.1 1.1 copy-done.1
  24.2 2.6 %shard_map.70 = (f32[512,128]{1,0:T(8,128)S(1)}, f32[32,16,128]{2,1,0:T(8,128)S(1)}) custom-call(s32[1]{0:T(128)} %bitcast.me_ref, f32[512,128]{1,0:T(8,128)} %get-tuple-element.37.sent_ref, f32[512,128]{1,0:T(8,128)S(1)} %bitcast.18, f32[12,512,128]{2,1,0:T(8,128)S(1)} %shard_map.69.jac_ref, f32[136,1024]{1,0:T(8,128)S(1)} %copy-done.1), custom_call_target="tpu_custom_call" | custom-call | tf_op jit(solution)/shard_map/pallas_call | solution.py:438
  26.8 14.5 %all_to_all.80.gathered_ref = f32[32,16,128]{2,1,0:T(8,128)S(1)} all-to-all(f32[32,16,128]{2,1,0:T(8,128)S(1)} %get-tuple-element.40), channel_id=1, replica_groups=mesh['track'=8,'det'=4] {'track','det'}, dimensions={0} | all-to-all | bytes 524288 | tf_op jit(solution)/shard_map/all_to_all | solution.py:424
  41.2 0.9 shard_map.71
  42.2 11.7 %all_to_all.81 = f32[8,64,128]{2,1,0:T(8,128)S(1)} all-to-all(f32[8,64,128]{2,1,0:T(8,128)S(1)} %bitcast.19), channel_id=1, replica_groups=mesh['track'=8,'det'=4] {'track'}, dimensions={0} | all-to-all | bytes 524288 | tf_op jit(solution)/shard_map/all_to_all | solution.py:421
  53.9 1.7 %shard_map.72 = (f32[512,128]{1,0:T(8,128)S(1)}, f32[32,16,128]{2,1,0:T(8,128)S(1)}) custom-call(s32[1]{0:T(128)} %bitcast.me_ref, f32[512,128]{1,0:T(8,128)S(1)} %get-tuple-element.41.sent_ref, f32[512,128]{1,0:T(8,128)S(1)} %bitcast.20, f32[12,512,128]{2,1,0:T(8,128)S(1)} %shard_map.69.jac_ref, f32[136,1024]{1,0:T(8,128)S(1)} %copy-done.1), custom_call_target="tpu_custom_call" | custom-call | tf_op jit(solution)/shard_map/pallas_call | solution.py:438
  55.5 13.4 %all_to_all.82.gathered_ref = f32[32,16,128]{2,1,0:T(8,128)S(1)} all-to-all(f32[32,16,128]{2,1,0:T(8,128)S(1)} %get-tuple-element.42), channel_id=1, replica_groups=mesh['track'=8,'det'=4] {'track','det'}, dimensions={0} | all-to-all | bytes 524288 | tf_op jit(solution)/shard_map/all_to_all | solution.py:424
  68.9 1.3 shard_map.73
  70.2 11.7 %all_to_all.83 = f32[8,64,128]{2,1,0:T(8,128)S(1)} all-to-all(f32[8,64,128]{2,1,0:T(8,128)S(1)} %bitcast.17), channel_id=1, replica_groups=mesh['track'=8,'det'=4] {'track'}, dimensions={0} | all-to-all | bytes 524288 | tf_op jit(solution)/shard_map/all_to_all | solution.py:421
  81.9 1.7 %shard_map.74 = (f32[512,128]{1,0:T(8,128)S(1)}, f32[32,16,128]{2,1,0:T(8,128)S(1)}) custom-call(s32[1]{0:T(128)} %bitcast.me_ref, f32[512,128]{1,0:T(8,128)S(1)} %get-tuple-element.47.sent_ref, f32[512,128]{1,0:T(8,128)S(1)} %bitcast.21, f32[12,512,128]{2,1,0:T(8,128)S(1)} %shard_map.69.jac_ref, f32[136,1024]{1,0:T(8,128)S(1)} %copy-done.1), custom_call_target="tpu_custom_call" | custom-call | tf_op jit(solution)/shard_map/pallas_call | solution.py:438
  83.6 13.4 %all_to_all.84.gathered_ref = f32[32,16,128]{2,1,0:T(8,128)S(1)} all-to-all(f32[32,16,128]{2,1,0:T(8,128)S(1)} %get-tuple-element.48), channel_id=1, replica_groups=mesh['track'=8,'det'=4] {'track','det'}, dimensions={0} | all-to-all | bytes 524288 | tf_op jit(solution)/shard_map/all_to_all | solution.py:424
  97.0 1.3 shard_map.75
  98.3 11.7 %all_to_all.85 = f32[8,64,128]{2,1,0:T(8,128)S(1)} all-to-all(f32[8,64,128]{2,1,0:T(8,128)S(1)} %bitcast.16), channel_id=1, replica_groups=mesh['track'=8,'det'=4] {'track'}, dimensions={0} | all-to-all | bytes 524288 | tf_op jit(solution)/shard_map/all_to_all | solution.py:421
  110.0 1.7 %shard_map.76 = (f32[512,128]{1,0:T(8,128)S(1)}, f32[32,16,128]{2,1,0:T(8,128)S(1)}) custom-call(s32[1]{0:T(128)} %bitcast.me_ref, f32[512,128]{1,0:T(8,128)S(1)} %get-tuple-element.55.sent_ref, f32[512,128]{1,0:T(8,128)S(1)} %bitcast.22, f32[12,512,128]{2,1,0:T(8,128)S(1)} %shard_map.69.jac_ref, f32[136,1024]{1,0:T(8,128)S(1)} %copy-done.1), custom_call_target="tpu_custom_call" | custom-call | tf_op jit(solution)/shard_map/pallas_call | solution.py:438
  111.6 13.4 %all_to_all.86.gathered_ref = f32[32,16,128]{2,1,0:T(8,128)S(1)} all-to-all(f32[32,16,128]{2,1,0:T(8,128)S(1)} %get-tuple-element.56), channel_id=1, replica_groups=mesh['track'=8,'det'=4] {'track','det'}, dimensions={0} | all-to-all | bytes 524288 | tf_op jit(solution)/shard_map/all_to_all | solution.py:424
  125.0 1.9 %shard_map.77 = (f32[8,16,128]{2,1,0:T(8,128)}, f32[8,16,128]{2,1,0:T(8,128)S(1)}, f32[8,128]{1,0:T(8,128)S(1)}, f32[16,128]{1,0:T(8,128)S(1)}, f32[512,128]{1,0:T(8,128)S(1)}, /*index=5*/f32[512,128]{1,0:T(8,128)S(1)}) custom-call(s32[1]{0:T(128)} %bitcast.me_ref, f32[32,16,128]{2,1,0:T(8,128)S(1)} %all_to_all.86.gathered_ref, ...), custom_call_target="tpu_custom_call" | custom-call | tf_op jit(solution)/shard_map/pallas_call | solution.py:459
  126.9 11.7 %all_to_all.87 = f32[8,64,128]{2,1,0:T(8,128)S(1)} all-to-all(f32[8,64,128]{2,1,0:T(8,128)S(1)} %bitcast.23), channel_id=1, replica_groups=mesh['track'=8,'det'=4] {'track'}, dimensions={0} | all-to-all | bytes 524288 | tf_op jit(solution)/shard_map/all_to_all | solution.py:421
  138.6 0.8 shard_map.78
  139.4 3.0 %all-to-all-start.9 = ((f32[32,1,128]{2,1,0:T(1,128)}), f32[32,1,128]{2,1,0:T(1,128)S(1)}, u32[]{:S(2)}, u32[]{:S(2)}) async-start(f32[32,1,128]{2,1,0:T(1,128)} %get-tuple-element.64), calls=%async_computation.9 | async-start | bytes 32768 | tf_op jit(solution)/shard_map/all_to_all | solution.py:424
  142.4 1.0 copy-done.5
  143.5 1.2 shard_map.79
  144.7 4.8 %all-to-all-done.9.squares_ref = f32[32,1,128]{2,1,0:T(1,128)S(1)} async-done(((f32[32,1,128]{2,1,0:T(1,128)}), f32[32,1,128]{2,1,0:T(1,128)S(1)}, u32[]{:S(2)}, u32[]{:S(2)}) %all-to-all-start.9) | async-done | bytes 16416 | tf_op jit(solution)/shard_map/all_to_all | solution.py:424
  149.5 0.9 shard_map.80
  (14 shorter events, 2.1 us)
Async XLA Ops:
  0.6 1.0 copy-start.6
  1.6 0.7 copy-start.7
  2.3 0.7 copy-start.8
  3.0 0.7 copy-start.9
  5.3 0.8 copy-start
  6.1 0.8 copy-start.3
  6.9 16.2 %all-to-all-start = ((f32[8,64,128]{2,1,0:T(8,128)}), f32[8,64,128]{2,1,0:T(8,128)S(1)}, u32[]{:S(2)}, u32[]{:S(2)}) async-start(f32[8,64,128]{2,1,0:T(8,128)} %bitcast.4), calls=%async_computation | async-start | bytes 524288 | tf_op jit(solution)/shard_map/all_to_all | solution.py:421
  14.2 1.9 %copy-start.2 = (f32[512,12,128]{2,0,1:T(8,128)S(1)}, f32[512,12,128]{2,0,1:T(8,128)}, u32[]{:S(2)}) copy-start(f32[512,12,128]{2,0,1:T(8,128)} %param.5) | copy-start | bytes 9437188
  16.1 1.0 copy-start.4
  23.1 1.1 copy-start.1
  139.4 10.1 %all-to-all-start.9 = ((f32[32,1,128]{2,1,0:T(1,128)}), f32[32,1,128]{2,1,0:T(1,128)S(1)}, u32[]{:S(2)}, u32[]{:S(2)}) async-start(f32[32,1,128]{2,1,0:T(1,128)} %get-tuple-element.64), calls=%async_computation.9 | async-start | bytes 32768 | tf_op jit(solution)/shard_map/all_to_all | solution.py:424
  142.4 1.0 copy-start.5

commit v4 on v3

--- a/solution.py
+++ b/solution.py
@@ -23,6 +23,14 @@
 ANY = pl.BlockSpec(memory_space=pl.ANY)
 PARAMS = pltpu.CompilerParams(vmem_limit_bytes=VMEM_BYTES)
 HIGHEST = lax.Precision.HIGHEST
+
+
+def kept(shape, dtype=jnp.float32):
+    return pltpu.VMEM(shape, dtype)
+
+
+def from_hbm(x):
+    return pltpu.with_memory_space_constraint(x, pltpu.HBM)
 
 
 def f32(*shape):
@@ -403,8 +411,8 @@
     perm, weights, sent = call(
         functools.partial(order_kernel, q),
         (
-            jax.ShapeDtypeStruct((tiles, tiles), jnp.bfloat16),
-            f32(KNOT_DEV + SUB, n_track * LANES),
+            kept((tiles, tiles), jnp.bfloat16),
+            kept((KNOT_DEV + SUB, n_track * LANES)),
             f32(tiles, columns),
         ),
         [SMEM, ANY, ANY, ANY, ANY],
@@ -415,7 +423,7 @@
             pltpu.VMEM((tiles, columns), jnp.float32),
             pltpu.SemaphoreType.DMA((4,)),
         ],
-    )(me, match[None], tile_knot[None], tile_frac[None], obs)
+    )(me, *map(from_hbm, (match[None], tile_knot[None], tile_frac[None], obs)))
 
     def crossing(values):
         return lax.all_to_all(values, "track", split_axis=0, concat_axis=0, tiled=True)
@@ -426,13 +434,13 @@
     arrived = crossing(sent)
     jac_rows = call(
         functools.partial(jac_kernel, q, math.gcd(params, 3)),
-        f32(params, tiles, columns),
+        kept((params, tiles, columns)),
         [VMEM, ANY],
         [
             pltpu.VMEM((params, tiles, columns), jnp.float32),
             pltpu.SemaphoreType.DMA((params,)),
         ],
-    )(perm, jnp.transpose(jac, (1, 0, 2)))
+    )(perm, from_hbm(jnp.transpose(jac, (1, 0, 2))))
 
     def adjoint(sent, arrived):
         diff, payload = call(

time: 151 us -> 148 us (0.980)
  local copies, waits for them, and re-layouts: 9.61 us -> 4.72 us
    unnamed x20 -> x10, local copies, waits for them, and re-layouts: 9.61 us -> 4.72 us
    pallas_call x2, Pallas kernels: 5.66 us -> 7.2 us  [the longest x1 4.89 us: local(): call(functools.partial(jac_kernel, q, math.gcd(params, 3)), kept((params,...]
  transfers between devices with their start and end apart: 2 -> 2, of which waited for: 2 -> 2; matrix products, arithmetic and copies ran while one was open for 0% -> 0% of each run, Pallas kernels for 3% -> 4%
where the time goes in v4:
time: 148 us
  blocking collectives  101 us (68%)
  Pallas kernels  23.1 us (16%)
  starting transfers between devices  10.3 us (7%)
  waiting for transfers between devices  7.78 us (5%)
  local copies, waits for them, and re-layouts  4.72 us (3%)
    all_to_all x4, blocking collectives, everywhere(): lax.all_to_all(values, ('track', 'det'), split_axis=0, concat_axis=0, til...  54.2 us
    all_to_all x4, blocking collectives, crossing(): lax.all_to_all(values, 'track', split_axis=0, concat_axis=0, tiled=True)  46.8 us
    pallas_call x4, Pallas kernels, adjoint(): call(functools.partial(adjoint_kernel, q), (f32(tiles, columns), f32(n_al...  7.61 us
    all_to_all x1, starting transfers between devices, crossing(): lax.all_to_all(values, 'track', split_axis=0, concat_axis=0, tiled=True)  7.28 us
    pallas_call x1, Pallas kernels, local(): call(functools.partial(jac_kernel, q, math.gcd(params, 3)), kept((params,...  4.89 us
    all_to_all x1, waiting for transfers between devices, everywhere(): lax.all_to_all(values, ('track', 'det'), split_axis=0, concat_axis=0, til...  4.81 us
    unnamed x10, local copies, waits for them, and re-layouts  4.72 us
    pallas_call x3, Pallas kernels, local(): call(functools.partial(step_kernel, q, n_det), (field, field, f32(SUB, LA...  4.42 us
  transfers between devices with their start and end apart: 2, of which 2 were waited for; matrix products, arithmetic and copies ran while one was open for 0% of the time, Pallas kernels for 4%

profile of v4, /device:TPU:0, one launch (start us, length us, event | category | flops | bytes accessed | tf_op | source)
XLA Modules:
  0.0 147.6 jit_solution(8886865910509843930)
XLA Ops:
  0.6 2.3 %shard_map.68 = (bf16[512,512]{1,0:T(8,128)(2,1)S(1)}, f32[136,1024]{1,0:T(8,128)S(1)}, f32[512,128]{1,0:T(8,128)}) custom-call(s32[1]{0:T(128)} %bitcast.me_ref, s32[1,512]{1,0:T(1,128)} %bitcast.25, s32[1,512]{1,0:T(1,128)} %bitcast.26, f32[1,512]{1,0:T(1,128)} %bitcast.27, f32[512,128]{1,0:T(8,128)} %obs_hbm.1), custom_call_target="tpu_custom_call" | custom-call | tf_op jit(solution)/shard_map/pallas_call | solution.py:411
  3.0 0.0 copy-start
  3.0 0.8 copy-done
  3.8 0.8 copy-done.2
  4.6 7.3 %all-to-all-start = ((f32[8,64,128]{2,1,0:T(8,128)}), f32[8,64,128]{2,1,0:T(8,128)S(1)}, u32[]{:S(2)}, u32[]{:S(2)}) async-start(f32[8,64,128]{2,1,0:T(8,128)} %bitcast.4), calls=%async_computation | async-start | bytes 524288 | tf_op jit(solution)/shard_map/all_to_all | solution.py:429
  11.8 1.0 copy-done.3
  12.9 4.9 %shard_map.69.jac_ref = f32[12,512,128]{2,1,0:T(8,128)S(1)} custom-call(bf16[512,512]{1,0:T(8,128)(2,1)S(1)} %copy-done.3, f32[12,512,128]{2,1,0:T(8,128)} %bitcast.24), custom_call_target="tpu_custom_call" | custom-call | tf_op jit(solution)/shard_map/pallas_call | solution.py:435
  17.8 3.0 %all-to-all-done = f32[8,64,128]{2,1,0:T(8,128)S(1)} async-done(((f32[8,64,128]{2,1,0:T(8,128)}), f32[8,64,128]{2,1,0:T(8,128)S(1)}, u32[]{:S(2)}, u32[]{:S(2)}) %all-to-all-start) | async-done | bytes 262176 | tf_op jit(solution)/shard_map/all_to_all | solution.py:429
  20.8 1.1 copy-done.1
  21.8 2.6 %shard_map.70 = (f32[512,128]{1,0:T(8,128)S(1)}, f32[32,16,128]{2,1,0:T(8,128)S(1)}) custom-call(s32[1]{0:T(128)} %bitcast.me_ref, f32[512,128]{1,0:T(8,128)} %get-tuple-element.37.sent_ref, f32[512,128]{1,0:T(8,128)S(1)} %bitcast.17, f32[12,512,128]{2,1,0:T(8,128)S(1)} %shard_map.69.jac_ref, f32[136,1024]{1,0:T(8,128)S(1)} %copy-done.1), custom_call_target="tpu_custom_call" | custom-call | tf_op jit(solution)/shard_map/pallas_call | solution.py:446
  24.4 14.0 %all_to_all.80.gathered_ref = f32[32,16,128]{2,1,0:T(8,128)S(1)} all-to-all(f32[32,16,128]{2,1,0:T(8,128)S(1)} %get-tuple-element.40), channel_id=1, replica_groups=mesh['track'=8,'det'=4] {'track','det'}, dimensions={0} | all-to-all | bytes 524288 | tf_op jit(solution)/shard_map/all_to_all | solution.py:432
  38.4 0.9 shard_map.71
  39.4 11.7 %all_to_all.81 = f32[8,64,128]{2,1,0:T(8,128)S(1)} all-to-all(f32[8,64,128]{2,1,0:T(8,128)S(1)} %bitcast.18), channel_id=1, replica_groups=mesh['track'=8,'det'=4] {'track'}, dimensions={0} | all-to-all | bytes 524288 | tf_op jit(solution)/shard_map/all_to_all | solution.py:429
  51.1 1.7 %shard_map.72 = (f32[512,128]{1,0:T(8,128)S(1)}, f32[32,16,128]{2,1,0:T(8,128)S(1)}) custom-call(s32[1]{0:T(128)} %bitcast.me_ref, f32[512,128]{1,0:T(8,128)S(1)} %get-tuple-element.41.sent_ref, f32[512,128]{1,0:T(8,128)S(1)} %bitcast.19, f32[12,512,128]{2,1,0:T(8,128)S(1)} %shard_map.69.jac_ref, f32[136,1024]{1,0:T(8,128)S(1)} %copy-done.1), custom_call_target="tpu_custom_call" | custom-call | tf_op jit(solution)/shard_map/pallas_call | solution.py:446
  52.7 13.4 %all_to_all.82.gathered_ref = f32[32,16,128]{2,1,0:T(8,128)S(1)} all-to-all(f32[32,16,128]{2,1,0:T(8,128)S(1)} %get-tuple-element.42), channel_id=1, replica_groups=mesh['track'=8,'det'=4] {'track','det'}, dimensions={0} | all-to-all | bytes 524288 | tf_op jit(solution)/shard_map/all_to_all | solution.py:432
  66.2 1.3 shard_map.73
  67.4 11.7 %all_to_all.83 = f32[8,64,128]{2,1,0:T(8,128)S(1)} all-to-all(f32[8,64,128]{2,1,0:T(8,128)S(1)} %bitcast.16), channel_id=1, replica_groups=mesh['track'=8,'det'=4] {'track'}, dimensions={0} | all-to-all | bytes 524288 | tf_op jit(solution)/shard_map/all_to_all | solution.py:429
  79.1 1.7 %shard_map.74 = (f32[512,128]{1,0:T(8,128)S(1)}, f32[32,16,128]{2,1,0:T(8,128)S(1)}) custom-call(s32[1]{0:T(128)} %bitcast.me_ref, f32[512,128]{1,0:T(8,128)S(1)} %get-tuple-element.47.sent_ref, f32[512,128]{1,0:T(8,128)S(1)} %bitcast.20, f32[12,512,128]{2,1,0:T(8,128)S(1)} %shard_map.69.jac_ref, f32[136,1024]{1,0:T(8,128)S(1)} %copy-done.1), custom_call_target="tpu_custom_call" | custom-call | tf_op jit(solution)/shard_map/pallas_call | solution.py:446
  80.8 13.4 %all_to_all.84.gathered_ref = f32[32,16,128]{2,1,0:T(8,128)S(1)} all-to-all(f32[32,16,128]{2,1,0:T(8,128)S(1)} %get-tuple-element.48), channel_id=1, replica_groups=mesh['track'=8,'det'=4] {'track','det'}, dimensions={0} | all-to-all | bytes 524288 | tf_op jit(solution)/shard_map/all_to_all | solution.py:432
  94.2 1.3 shard_map.75
  95.5 11.7 %all_to_all.85 = f32[8,64,128]{2,1,0:T(8,128)S(1)} all-to-all(f32[8,64,128]{2,1,0:T(8,128)S(1)} %bitcast.15), channel_id=1, replica_groups=mesh['track'=8,'det'=4] {'track'}, dimensions={0} | all-to-all | bytes 524288 | tf_op jit(solution)/shard_map/all_to_all | solution.py:429
  107.2 1.7 %shard_map.76 = (f32[512,128]{1,0:T(8,128)S(1)}, f32[32,16,128]{2,1,0:T(8,128)S(1)}) custom-call(s32[1]{0:T(128)} %bitcast.me_ref, f32[512,128]{1,0:T(8,128)S(1)} %get-tuple-element.55.sent_ref, f32[512,128]{1,0:T(8,128)S(1)} %bitcast.21, f32[12,512,128]{2,1,0:T(8,128)S(1)} %shard_map.69.jac_ref, f32[136,1024]{1,0:T(8,128)S(1)} %copy-done.1), custom_call_target="tpu_custom_call" | custom-call | tf_op jit(solution)/shard_map/pallas_call | solution.py:446
  108.8 13.4 %all_to_all.86.gathered_ref = f32[32,16,128]{2,1,0:T(8,128)S(1)} all-to-all(f32[32,16,128]{2,1,0:T(8,128)S(1)} %get-tuple-element.56), channel_id=1, replica_groups=mesh['track'=8,'det'=4] {'track','det'}, dimensions={0} | all-to-all | bytes 524288 | tf_op jit(solution)/shard_map/all_to_all | solution.py:432
  122.2 1.9 %shard_map.77 = (f32[8,16,128]{2,1,0:T(8,128)}, f32[8,16,128]{2,1,0:T(8,128)S(1)}, f32[8,128]{1,0:T(8,128)S(1)}, f32[16,128]{1,0:T(8,128)S(1)}, f32[512,128]{1,0:T(8,128)S(1)}, /*index=5*/f32[512,128]{1,0:T(8,128)S(1)}) custom-call(s32[1]{0:T(128)} %bitcast.me_ref, f32[32,16,128]{2,1,0:T(8,128)S(1)} %all_to_all.86.gathered_ref, ...), custom_call_target="tpu_custom_call" | custom-call | tf_op jit(solution)/shard_map/pallas_call | solution.py:467
  124.1 11.7 %all_to_all.87 = f32[8,64,128]{2,1,0:T(8,128)S(1)} all-to-all(f32[8,64,128]{2,1,0:T(8,128)S(1)} %bitcast.22), channel_id=1, replica_groups=mesh['track'=8,'det'=4] {'track'}, dimensions={0} | all-to-all | bytes 524288 | tf_op jit(solution)/shard_map/all_to_all | solution.py:429
  135.8 0.8 shard_map.78
  136.6 3.0 %all-to-all-start.9 = ((f32[32,1,128]{2,1,0:T(1,128)}), f32[32,1,128]{2,1,0:T(1,128)S(1)}, u32[]{:S(2)}, u32[]{:S(2)}) async-start(f32[32,1,128]{2,1,0:T(1,128)} %get-tuple-element.64), calls=%async_computation.9 | async-start | bytes 32768 | tf_op jit(solution)/shard_map/all_to_all | solution.py:432
  139.6 0.0 copy-start.4
  139.6 1.0 copy-done.4
  140.7 1.2 shard_map.79
  141.9 4.8 %all-to-all-done.9.squares_ref = f32[32,1,128]{2,1,0:T(1,128)S(1)} async-done(((f32[32,1,128]{2,1,0:T(1,128)}), f32[32,1,128]{2,1,0:T(1,128)S(1)}, u32[]{:S(2)}, u32[]{:S(2)}) %all-to-all-start.9) | async-done | bytes 16416 | tf_op jit(solution)/shard_map/all_to_all | solution.py:432
  146.7 0.9 shard_map.80
  (4 shorter events, 0.0 us)
Async XLA Ops:
  3.0 0.8 copy-start
  3.8 0.8 copy-start.2
  4.6 16.2 %all-to-all-start = ((f32[8,64,128]{2,1,0:T(8,128)}), f32[8,64,128]{2,1,0:T(8,128)S(1)}, u32[]{:S(2)}, u32[]{:S(2)}) async-start(f32[8,64,128]{2,1,0:T(8,128)} %bitcast.4), calls=%async_computation | async-start | bytes 524288 | tf_op jit(solution)/shard_map/all_to_all | solution.py:429
  11.8 1.0 copy-start.3
  20.8 1.1 copy-start.1
  136.6 10.1 %all-to-all-start.9 = ((f32[32,1,128]{2,1,0:T(1,128)}), f32[32,1,128]{2,1,0:T(1,128)S(1)}, u32[]{:S(2)}, u32[]{:S(2)}) async-start(f32[32,1,128]{2,1,0:T(1,128)} %get-tuple-element.64), calls=%async_computation.9 | async-start | bytes 32768 | tf_op jit(solution)/shard_map/all_to_all | solution.py:432
  139.6 1.0 copy-start.4

commit v5 on v4

--- a/solution.py
+++ b/solution.py
@@ -106,6 +106,23 @@
         parts.append(jnp.concatenate(rows, axis=0).T)
     stacked = jnp.concatenate(parts, axis=0)
     return sum(bf16_dot(perm, part) for part in reversed(split3(stacked)))
+
+
+def crossing_order(me, match):
+    tiles = match.shape[1]
+    slot = lax.broadcasted_iota(jnp.int32, (1, tiles), 1)
+    peer = match // tiles
+    other = match - peer * tiles
+    inner = jnp.where(
+        peer == me,
+        jnp.minimum(slot, other) + jnp.where(slot > other, tiles, 0),
+        jnp.where(peer > me, slot, other),
+    )
+    key = (peer * (2 * tiles) + inner).astype(jnp.float32)
+    key_cols = jnp.broadcast_to(key, (LANES, tiles)).T[:, :1]
+    place = jnp.sum(jnp.where(key < key_cols, 1.0, 0.0), axis=1, keepdims=True)
+    cols = lax.broadcasted_iota(jnp.int32, (tiles, tiles), 1).astype(jnp.float32)
+    return jnp.where(place == cols, 1.0, 0.0).astype(jnp.bfloat16)
 
 
 def order_kernel(
@@ -135,20 +152,7 @@
     copies[0].wait()
     groups = LANES // q
     me = me_ref[0]
-    match = match_ref[...]
-    slot = lax.broadcasted_iota(jnp.int32, (1, tiles), 1)
-    peer = match // tiles
-    other = match - peer * tiles
-    inner = jnp.where(
-        peer == me,
-        jnp.minimum(slot, other) + jnp.where(slot > other, tiles, 0),
-        jnp.where(peer > me, slot, other),
-    )
-    key = (peer * (2 * tiles) + inner).astype(jnp.float32)
-    key_cols = jnp.broadcast_to(key, (LANES, tiles)).T[:, :1]
-    place = jnp.sum(jnp.where(key < key_cols, 1.0, 0.0), axis=1, keepdims=True)
-    cols = lax.broadcasted_iota(jnp.int32, (tiles, tiles), 1).astype(jnp.float32)
-    perm = jnp.where(place == cols, 1.0, 0.0).astype(jnp.bfloat16)
+    perm = crossing_order(me, match_ref[...])
     perm_ref[...] = perm
 
     def put(_, index, block):
@@ -247,14 +251,14 @@
         send_ref[d, 0 : params + 1, :] = block
 
 
-def field_sums(gathered_ref, n_track, n_det, params, store):
+def field_sums(gathered_ref, n_track, n_det, params, store, base=0):
     lane = lax.broadcasted_iota(jnp.int32, (PAD, LANES), 1)
     row = lax.broadcasted_iota(jnp.int32, (PAD, LANES), 0)
     spill = jnp.zeros((PAD, 1), jnp.float32)
     for b in range(n_track):
-        total = gathered_ref[b * n_det]
+        total = gathered_ref[b * n_det, base : base + PAD, :]
         for d in range(1, n_det):
-            total = total + gathered_ref[b * n_det + d]
+            total = total + gathered_ref[b * n_det + d, base : base + PAD, :]
         field = jnp.where(row < params, total, 0.0)
         field = field + jnp.where(lane == 0, spill, 0.0)
         store(b, field)
@@ -400,12 +404,575 @@
     )
 
 
+def row_sums(parts):
+    row = lax.broadcasted_iota(jnp.int32, (SUB, LANES), 0)
+    level = list(parts)
+    zero = jnp.zeros((SUB, LANES), jnp.float32)
+    while len(level) % SUB:
+        level.append(zero)
+    for distance in (1, 2, 4):
+        first = (row // distance) % 2 == 0
+        level = [
+            jnp.where(first, a, b) + pltpu.roll(jnp.where(first, b, a), distance, 0)
+            for a, b in zip(level[::2], level[1::2])
+        ]
+    return level[0] if len(level) == 1 else jnp.concatenate(level, axis=0)
+
+
+def fold_rows(x):
+    total = x[0:SUB]
+    for step in range(1, x.shape[0] // SUB):
+        total = total + x[step * SUB : (step + 1) * SUB]
+    return total
+
+
+def fold_lanes(x, half):
+    shift = half
+    while shift < LANES:
+        x = x + pltpu.roll(x, shift, 1)
+        shift *= 2
+    return x
+
+
+def pair_index(p, other):
+    low, high = min(p, other), max(p, other)
+    return high * (high + 1) // 2 + low
+
+
+def pad_to(x, unit):
+    return -(-x // unit) * unit
+
+
+def weight_rows(knot, frac):
+    knots = lax.broadcasted_iota(jnp.int32, (KNOT_DEV, knot.shape[1]), 0).astype(jnp.float32)
+    main = jnp.where(knots == knot, 1.0 - frac, 0.0) + jnp.where(knots == knot + 1.0, frac, 0.0)
+    first = lax.broadcasted_iota(jnp.int32, (SUB, knot.shape[1]), 0) == 0
+    edge = jnp.where(first, jnp.where(knot == KNOT_DEV - 1.0, frac, 0.0), 0.0)
+    return main, edge
+
+
+def setup_kernel(
+    half,
+    together,
+    me_ref,
+    match_hbm,
+    knot_hbm,
+    frac_hbm,
+    obs_hbm,
+    jac_hbm,
+    perm_ref,
+    weight_ref,
+    rows_ref,
+    message_ref,
+    match_ref,
+    knot_ref,
+    frac_ref,
+    obs_ref,
+    jac_ref,
+    sems,
+):
+    params, tiles, _ = jac_ref.shape
+    n_track = message_ref.shape[0]
+    q = 2 * half
+    pairs = [(match_hbm, match_ref), (knot_hbm, knot_ref), (frac_hbm, frac_ref), (obs_hbm, obs_ref)]
+    pairs += [(jac_hbm.at[p], jac_ref.at[p]) for p in range(params)]
+    copies = [
+        pltpu.make_async_copy(source, target, sems.at[index])
+        for index, (source, target) in enumerate(pairs)
+    ]
+    for copy in copies:
+        copy.start()
+    copies[0].wait()
+    me = me_ref[0]
+    perm_ref[...] = crossing_order(me, match_ref[...])
+    perm = perm_ref[...]
+    for copy in copies[1:4]:
+        copy.wait()
+
+    row = lax.broadcasted_iota(jnp.int32, (SUB, tiles), 0)
+    facts = jnp.where(row == 0, knot_ref[...].astype(jnp.float32), frac_ref[...])
+    moved = sum(bf16_dot(part, perm) for part in reversed(split3(facts)))
+    main, edge = weight_rows(moved[0:1], moved[1:2])
+    weight_ref[0:KNOT_DEV, :] = main
+    weight_ref[KNOT_DEV : KNOT_DEV + SUB, :] = edge
+
+    obs_row = params * half
+    per_chunk = LANES // q
+    for b in range(n_track):
+        chunk = moved[:, b // per_chunk * LANES : (b // per_chunk + 1) * LANES]
+        message_ref[b, obs_row + q : obs_row + q + SUB, :] = turn(chunk, -(b % per_chunk) * q)
+
+    def put_obs(_, s, block):
+        first = obs_row + (s % 2) * half
+        message_ref[s // 2, first : first + half, :] = block
+
+    to_crossing([obs_ref[...]], perm, half, put_obs)
+
+    for first in range(0, params, together):
+        for p in range(first, first + together):
+            copies[4 + p].wait()
+
+        def put(index, s, block):
+            rows_ref[first + index, s * half : (s + 1) * half, :] = block
+
+        to_crossing([jac_ref[p] for p in range(first, first + together)], perm, half, put)
+    for b in range(n_track):
+        offset = pl.multiple_of(jnp.where(me <= b, 2 * b + 1, 2 * b) * half, SUB)
+        for p in range(params):
+            message_ref[b, p * half : (p + 1) * half, :] = rows_ref[p, pl.ds(offset, half), :]
+
+
+def payload_rows(spread, params):
+    lane = lax.broadcasted_iota(jnp.int32, (PAD, LANES), 1)
+    row = lax.broadcasted_iota(jnp.int32, (PAD, LANES), 0)
+    spill = jnp.sum(
+        jnp.where(lane == row, spread[:, KNOT_DEV : KNOT_DEV + 1], 0.0), axis=0, keepdims=True
+    )
+    return jnp.where(row < params, spread[:, :KNOT_DEV], jnp.where(row == params, spill, 0.0))
+
+
+def gram_kernel(half, me_ref, sent_ref, arrived_ref, rows_ref, weight_ref, misfit_ref, partner_ref, back_ref, diag_ref):
+    params, tiles, _ = rows_ref.shape
+    n_track = arrived_ref.shape[0]
+    q = 2 * half
+    me = me_ref[0]
+    obs_row = params * half
+    group = lax.broadcasted_iota(jnp.int32, (PAD, LANES), 1) // half
+    lane8 = lax.broadcasted_iota(jnp.int32, (SUB, LANES), 1)
+    subs = LANES // half
+
+    per_chunk = LANES // q
+    for c in range(tiles // LANES):
+        facts = None
+        for b in range(per_chunk):
+            block = c * per_chunk + b
+            piece = arrived_ref[block, obs_row + q : obs_row + q + SUB, :]
+            swapped = jnp.where(lane8 < half, turn(piece, -half), turn(piece, half))
+            piece = turn(jnp.where(me == block, swapped, piece), b * q)
+            facts = piece if facts is None else jnp.where(lane8 // q == b, piece, facts)
+        main, edge = weight_rows(facts[0:1], facts[1:2])
+        lanes = slice(c * LANES, (c + 1) * LANES)
+        partner_ref[0:KNOT_DEV, lanes] = main
+        partner_ref[KNOT_DEV : KNOT_DEV + SUB, lanes] = edge
+
+    for s in range(2 * n_track):
+        b = s // 2
+        own = sent_ref[b, obs_row + (s % 2) * half : obs_row + (s % 2 + 1) * half, :]
+        first = pl.multiple_of(obs_row + jnp.where(me == b, 1 - s % 2, s % 2) * half, SUB)
+        misfit_ref[s * half : (s + 1) * half, :] = own - arrived_ref[b, pl.ds(first, half), :]
+
+    held = -(-params // subs)
+
+    def cross(b, carry):
+        offset = pl.multiple_of(jnp.where(me <= b, 2 * b, 2 * b + 1) * half, SUB)
+        for slot in range(held):
+            total = jnp.zeros((PAD, LANES), jnp.float32)
+            for j in range(subs):
+                p = j * held + slot
+                if p >= params:
+                    continue
+                own = rows_ref[p, pl.ds(offset, half), :]
+                parts = [
+                    fold_rows(own * arrived_ref[b, other * half : (other + 1) * half, :])
+                    for other in range(params)
+                ]
+                total = jnp.where(group == j, fold_lanes(row_sums(parts), half), total)
+            back_ref[b, slot * PAD : (slot + 1) * PAD, :] = total
+        return carry
+
+    lax.fori_loop(0, n_track, cross, 0)
+
+    n_pairs = params * (params + 1) // 2
+    spread = None
+    for c in range(tiles // LANES):
+        lanes = slice(c * LANES, (c + 1) * LANES)
+
+        def own_block(b, carry):
+            totals, values = carry
+            rows = pl.ds(pl.multiple_of((c * subs + b) * half, SUB), half)
+            miss = misfit_ref[rows, :]
+            parts = []
+            for high in range(params):
+                right = rows_ref[high, rows, :]
+                for low in range(high + 1):
+                    parts.append(fold_rows(rows_ref[low, rows, :] * right))
+            sums = fold_lanes(row_sums(parts), half)
+            wide = lax.broadcasted_iota(jnp.int32, sums.shape, 1) // half
+            totals = jnp.where(wide == b, sums, totals)
+            sums = fold_lanes(
+                row_sums([fold_rows(rows_ref[p, rows, :] * miss) for p in range(params)]), half
+            )
+            return totals, jnp.where(group == b, sums, values)
+
+        totals, values = lax.fori_loop(
+            0,
+            subs,
+            own_block,
+            (
+                jnp.zeros((pad_to(n_pairs, SUB), LANES), jnp.float32),
+                jnp.zeros((PAD, LANES), jnp.float32),
+            ),
+        )
+        diag_ref[:, lanes] = totals
+        term = dot(values, weight_ref[:, lanes], ((1,), (1,)))
+        spread = term if spread is None else spread + term
+    block = payload_rows(spread, params)
+    for b in range(n_track):
+        back_ref[b, held * PAD : (held + 1) * PAD, :] = block
+
+
+def following_of(field_ref, index):
+    n_track = field_ref.shape[0]
+    if isinstance(index, int):
+        if index + 1 == n_track:
+            return jnp.zeros((PAD, 1), jnp.float32)
+        return field_ref[index + 1][:, 0:1]
+    values = field_ref[jnp.minimum(index + 1, n_track - 1)][:, 0:1]
+    return jnp.where(index + 1 < n_track, values, 0.0)
+
+
+def interp_own(me, field_ref, weight_ref):
+    return (
+        dot(field_ref[me], weight_ref[0:KNOT_DEV, :], ((1,), (0,)))
+        + following_of(field_ref, me) * weight_ref[KNOT_DEV : KNOT_DEV + 1, :]
+    )
+
+
+def normal_rows(half, params, me, field_ref, cross_ref, diag_ref, weight_ref, partner_ref):
+    tiles = weight_ref.shape[1]
+    q = 2 * half
+    own = interp_own(me, field_ref, weight_ref)
+    lane = lax.broadcasted_iota(jnp.int32, (PAD, LANES), 1)
+    per_chunk = LANES // q
+    spread = None
+    for c in range(tiles // LANES):
+        lanes = slice(c * LANES, (c + 1) * LANES)
+        other = None
+        for b in range(per_chunk):
+            block = c * per_chunk + b
+            piece = (
+                dot(field_ref[block], partner_ref[0:KNOT_DEV, lanes], ((1,), (0,)))
+                + following_of(field_ref, block) * partner_ref[KNOT_DEV : KNOT_DEV + 1, lanes]
+            )
+            other = piece if other is None else jnp.where(lane // q == b, piece, other)
+        total = None
+        by_slot = None
+        by_row = []
+        for p in range(params):
+            term = diag_ref[p, :, lanes] * own[p : p + 1, lanes]
+            total = term if total is None else total + term
+            matrix = cross_ref[p, :, lanes]
+            term = matrix * other[p : p + 1]
+            by_slot = term if by_slot is None else by_slot + term
+            by_row.append(fold_rows(matrix * other))
+        block = c * per_chunk + lane // q
+        is_first = (lane // half) % 2 == 0
+        is_owner = jnp.where(is_first, me, block) <= jnp.where(is_first, block, me - 1)
+        total = total - jnp.where(is_owner, row_sums(by_row), by_slot)
+        term = dot(total, weight_ref[:, lanes], ((1,), (1,)))
+        spread = term if spread is None else spread + term
+    return spread
+
+
+def send_rows(send_ref, block):
+    for b in range(send_ref.shape[0]):
+        send_ref[b] = block
+
+
+def start_kernel(
+    half,
+    me_ref,
+    kept_ref,
+    arrived_ref,
+    pairs_ref,
+    weight_ref,
+    partner_ref,
+    cross_ref,
+    diag_ref,
+    grad_ref,
+    norm_ref,
+    send_ref,
+):
+    params = cross_ref.shape[0]
+    tiles = cross_ref.shape[2]
+    n_track = grad_ref.shape[0]
+    me = me_ref[0]
+    subs = LANES // half
+    held = -(-params // subs)
+    group = lax.broadcasted_iota(jnp.int32, (PAD, LANES), 1) // half
+    for s in range(tiles // half):
+        b = s // 2
+        is_owner = me <= b if s % 2 == 0 else me > b
+        lanes = slice(s // subs * LANES, (s // subs + 1) * LANES)
+        for p in range(params):
+            rows = slice(p % held * PAD, (p % held + 1) * PAD)
+            piece = jnp.where(is_owner, kept_ref[b, rows, :], arrived_ref[b, rows, :])
+            piece = turn(piece, (s % subs - p // held) * half)
+            if s % subs:
+                piece = jnp.where(group == s % subs, piece, cross_ref[p, :, lanes])
+            cross_ref[p, :, lanes] = piece
+    diag_ref[...] = jnp.zeros(diag_ref.shape, jnp.float32)
+    for p in range(params):
+        for other in range(params):
+            index = pair_index(p, other)
+            diag_ref[p, other : other + 1, :] = pairs_ref[index : index + 1, :]
+
+    def put(b, field):
+        grad_ref[b] = field
+
+    field_sums(arrived_ref, n_track, 1, params, put, held * PAD)
+    norm_ref[...] = jnp.broadcast_to(full_dot(grad_ref, grad_ref), norm_ref.shape)
+    spread = normal_rows(half, params, me, grad_ref, cross_ref, diag_ref, weight_ref, partner_ref)
+    send_rows(send_ref, payload_rows(spread, params))
+
+
+def advance(params, gathered_ref, grad_ref, direction_ref, norm_ref, knot_ref, grad_out, direction_out, norm_out, knot_out, image_ref):
+    n_track = grad_ref.shape[0]
+
+    def put(b, field):
+        image_ref[b] = field + damping * direction_ref[b]
+
+    field_sums(gathered_ref, n_track, 1, params, put)
+    norm = norm_ref[0:1, 0:1]
+    length = norm / full_dot(direction_ref, image_ref)
+    for b in range(n_track):
+        knot_out[b] = knot_ref[b] + length * direction_ref[b]
+        grad_out[b] = grad_ref[b] - length * image_ref[b]
+    new_norm = full_dot(grad_out, grad_out)
+    norm_out[...] = jnp.broadcast_to(new_norm, norm_out.shape)
+    ratio = new_norm / norm
+    for b in range(n_track):
+        direction_out[b] = grad_out[b] + ratio * direction_ref[b]
+
+
+def next_kernel(
+    half,
+    me_ref,
+    gathered_ref,
+    grad_ref,
+    direction_ref,
+    norm_ref,
+    knot_ref,
+    cross_ref,
+    diag_ref,
+    weight_ref,
+    partner_ref,
+    grad_out,
+    direction_out,
+    norm_out,
+    knot_out,
+    send_ref,
+    image_ref,
+):
+    params = cross_ref.shape[0]
+    advance(
+        params, gathered_ref, grad_ref, direction_ref, norm_ref, knot_ref, grad_out, direction_out, norm_out, knot_out, image_ref
+    )
+    spread = normal_rows(
+        half, params, me_ref[0], direction_out, cross_ref, diag_ref, weight_ref, partner_ref
+    )
+    send_rows(send_ref, payload_rows(spread, params))
+
+
+def final_kernel(
+    half,
+    me_ref,
+    gathered_ref,
+    grad_ref,
+    direction_ref,
+    norm_ref,
+    knot_ref,
+    cross_ref,
+    diag_ref,
+    weight_ref,
+    partner_ref,
+    rows_ref,
+    direction_out,
+    norm_out,
+    knot_out,
+    send_ref,
+    image_ref,
+    grad_out,
+    interp_ref,
+):
+    params, tiles, _ = rows_ref.shape
+    n_track = send_ref.shape[0]
+    me = me_ref[0]
+    q = 2 * half
+    subs = LANES // half
+    advance(
+        params, gathered_ref, grad_ref, direction_ref, norm_ref, knot_ref, grad_out, direction_out, norm_out, knot_out, image_ref
+    )
+    spread = normal_rows(
+        half, params, me, direction_out, cross_ref, diag_ref, weight_ref, partner_ref
+    )
+    block = spread[:, :KNOT_DEV] * direction_out[me]
+    edge = spread[:, KNOT_DEV : KNOT_DEV + 1] * following_of(direction_out, me)
+    share = jnp.sum(block, keepdims=True) + jnp.sum(edge, keepdims=True)
+    group = lax.broadcasted_iota(jnp.int32, (PAD, LANES), 1) // half
+    for index, field in enumerate((knot_out, direction_out)):
+        interp = interp_own(me, field, weight_ref)
+        for s in range(tiles // half):
+            chunk = interp[:, s // subs * LANES : (s // subs + 1) * LANES]
+            wide = None
+            for h in range(subs):
+                piece = turn(chunk, (h - s % subs) * half)
+                wide = piece if wide is None else jnp.where(group == h, piece, wide)
+            interp_ref[index, s] = wide
+
+    def values(b, carry):
+        for s in range(2):
+            rows = pl.ds(pl.multiple_of((2 * b + s) * half, SUB), half)
+            sums = [None, None]
+            knot_interp = interp_ref[0, 2 * b + s]
+            direction_interp = interp_ref[1, 2 * b + s]
+            for p in range(params):
+                jac = rows_ref[p, rows, :]
+                for index, interp in enumerate((knot_interp, direction_interp)):
+                    term = jac * interp[p : p + 1]
+                    sums[index] = term if sums[index] is None else sums[index] + term
+            for index in range(2):
+                first = index * q + s * half
+                send_ref[b, first : first + half, :] = sums[index]
+        send_ref[b, 2 * q : 2 * q + SUB, :] = jnp.broadcast_to(share, (SUB, LANES))
+        return carry
+
+    lax.fori_loop(0, n_track, values, 0)
+
+
+def close_kernel(
+    half,
+    me_ref,
+    sent_ref,
+    arrived_ref,
+    direction_ref,
+    norm_ref,
+    knot_ref,
+    misfit_ref,
+    perm_ref,
+    knot_out,
+    residual_out,
+    residual_ref,
+):
+    params = knot_out.shape[0]
+    n_track = sent_ref.shape[0]
+    tiles = misfit_ref.shape[0]
+    me = me_ref[0]
+    q = 2 * half
+    share = arrived_ref[0, 2 * q : 2 * q + 1, :]
+    for b in range(1, n_track):
+        share = share + arrived_ref[b, 2 * q : 2 * q + 1, :]
+    curvature = share[:, 0:1] + damping * full_dot(direction_ref, direction_ref)
+    length = norm_ref[0:1, 0:1] / curvature
+    knot = knot_ref[me] + length * direction_ref[me]
+    knot_out[...] = knot[0:params]
+    for s in range(2 * n_track):
+        b = s // 2
+        here = (s % 2) * half
+        there = jnp.where(me == b, 1 - s % 2, s % 2) * half
+        first = pl.ds(pl.multiple_of(there, SUB), half)
+        second = pl.ds(pl.multiple_of(q + there, SUB), half)
+        own = sent_ref[b, here : here + half, :] - arrived_ref[b, first, :]
+        step = sent_ref[b, q + here : q + here + half, :] - arrived_ref[b, second, :]
+        rows = slice(s * half, (s + 1) * half)
+        residual_ref[rows, :] = misfit_ref[rows, :] - own - length * step
+    residual_out[...] = from_crossing(
+        lambda index: residual_ref[index * half : (index + 1) * half, :], perm_ref[...], half, tiles
+    )
+
+
+def local_blocks(jac, obs, match, tile_knot, tile_frac):
+    tiles, params, columns = jac.shape
+    n_track = lax.axis_size("track")
+    half = tiles // n_track // 2
+    q = 2 * half
+    held = -(-params // (LANES // half))
+    n_pairs = pad_to(params * (params + 1) // 2, SUB)
+    me = lax.axis_index("track").astype(jnp.int32).reshape(1)
+
+    def crossing(values):
+        return lax.all_to_all(values, "track", split_axis=0, concat_axis=0, tiled=True)
+
+    weight_shape = (KNOT_DEV + SUB, tiles)
+    perm, weights, rows, message = call(
+        functools.partial(setup_kernel, half, math.gcd(params, 3)),
+        (
+            kept((tiles, tiles), jnp.bfloat16),
+            kept(weight_shape),
+            kept((params, tiles, columns)),
+            kept((n_track, params * half + q + SUB, LANES)),
+        ),
+        [SMEM] + [ANY] * 5,
+        [
+            pltpu.VMEM((1, tiles), jnp.int32),
+            pltpu.VMEM((1, tiles), jnp.int32),
+            pltpu.VMEM((1, tiles), jnp.float32),
+            pltpu.VMEM((tiles, columns), jnp.float32),
+            pltpu.VMEM((params, tiles, columns), jnp.float32),
+            pltpu.SemaphoreType.DMA((4 + params,)),
+        ],
+    )(
+        me,
+        *map(
+            from_hbm,
+            (match[None], tile_knot[None], tile_frac[None], obs, jnp.transpose(jac, (1, 0, 2))),
+        ),
+    )
+    misfit, partners, back, pairs = call(
+        functools.partial(gram_kernel, half),
+        (
+            kept((tiles, columns)),
+            kept(weight_shape),
+            f32(n_track, (held + 1) * PAD, LANES),
+            f32(n_pairs, tiles),
+        ),
+        [SMEM] + [VMEM] * 4,
+    )(me, message, crossing(message), rows, weights)
+    back, pairs = lax.psum((back, pairs), "det")
+    field = f32(n_track, PAD, LANES)
+    field_ref = pltpu.VMEM((n_track, PAD, LANES), jnp.float32)
+    matrix = kept((params, PAD, tiles))
+    norm_shape = f32(SUB, LANES)
+    cross, diag, gradient, slope_norm, send = call(
+        functools.partial(start_kernel, half),
+        (matrix, matrix, field, norm_shape, field),
+        [SMEM] + [VMEM] * 5,
+    )(me, back, crossing(back), pairs, weights, partners)
+    direction = gradient
+    knot_field = jnp.zeros((n_track, PAD, LANES), jnp.float32)
+    for iteration in range(ITERS - 2):
+        gradient, direction, slope_norm, knot_field, send = call(
+            functools.partial(next_kernel, half),
+            (field, field, norm_shape, field, field),
+            [SMEM] + [VMEM] * 9,
+            [field_ref],
+        )(
+            me, crossing(send), gradient, direction, slope_norm, knot_field, cross, diag, weights, partners
+        )
+    direction, slope_norm, knot_field, send = call(
+        functools.partial(final_kernel, half),
+        (field, norm_shape, field, f32(n_track, 2 * q + SUB, LANES)),
+        [SMEM] + [VMEM] * 10,
+        [field_ref, field_ref, pltpu.VMEM((2, tiles // half, PAD, LANES), jnp.float32)],
+    )(
+        me, crossing(send), gradient, direction, slope_norm, knot_field, cross, diag, weights, partners, rows
+    )
+    return call(
+        functools.partial(close_kernel, half),
+        (f32(params, KNOT_DEV), f32(tiles, columns)),
+        [SMEM] + [VMEM] * 7,
+        [pltpu.VMEM((tiles, columns), jnp.float32)],
+    )(me, send, crossing(send), direction, slope_norm, knot_field, misfit, perm)
+
+
 def local(jac, obs, match, tile_knot, tile_frac):
     tiles, params, columns = jac.shape
     n_track = lax.axis_size("track")
     n_det = lax.axis_size("det")
     n_all = n_track * n_det
     q = tiles // n_track
+    if (q // 2) % SUB == 0:
+        return local_blocks(jac, obs, match, tile_knot, tile_frac)
     me = lax.axis_index("track").astype(jnp.int32).reshape(1)
 
     perm, weights, sent = call(

time: 148 us -> 186 us (1.26)
  waiting for transfers between devices: 7.78 us -> 31.2 us
  between operations: 0.75 us -> 14.1 us
  starting transfers between devices: 10.3 us -> 0.04 us
  blocking collectives: 101 us -> 107 us
  Pallas kernels: 23.1 us -> 25.8 us
    all_to_all x4 -> x6, blocking collectives: 46.8 us -> 107 us  [crossing(): lax.all_to_all(values, 'track', split_axis=0, concat_axis=0, tiled=True)]
    all_to_all x4 -> x0, blocking collectives: 54.2 us -> none  [everywhere(): lax.all_to_all(values, ('track', 'det'), split_axis=0, concat_axis=0, til...]
    psum x0 -> x1, waiting for transfers between devices: none -> 31.2 us  [local_blocks(): back, pairs = lax.psum((back, pairs), 'det')]
    all_to_all x2 -> x0, starting transfers between devices: 10.3 us -> none  [the longest x1 7.28 us: crossing(): lax.all_to_all(values, 'track', split_axis=0, concat_axis=0, tiled=True)]
    all_to_all x2 -> x0, waiting for transfers between devices: 7.78 us -> none  [the longest x1 4.81 us: everywhere(): lax.all_to_all(values, ('track', 'det'), split_axis=0, concat_axis=0, til...]
    pallas_call x13 -> x7, Pallas kernels: 23.1 us -> 25.8 us  [the longest x1 8.58 us: local_blocks(): call(functools.partial(gram_kernel, half), (kept((tiles, columns)), kept(...]
    unnamed x10 -> x20, local copies, waits for them, and re-layouts: 4.72 us -> 6.42 us
  transfers between devices with their start and end apart: 2 -> 1, of which waited for: 2 -> 1; matrix products, arithmetic and copies ran while one was open for 0% -> 0% of each run, Pallas kernels for 4% -> 0%
where the time goes in v5:
time: 186 us; the launch traced here: 185 us
  blocking collectives  107 us (58%)
  waiting for transfers between devices  31.2 us (17%)
  Pallas kernels  25.8 us (14%)
  between operations  14.1 us (8%)
  local copies, waits for them, and re-layouts  6.43 us (3%)
    all_to_all x6, blocking collectives, crossing(): lax.all_to_all(values, 'track', split_axis=0, concat_axis=0, tiled=True)  107 us
    psum x1, waiting for transfers between devices, local_blocks(): back, pairs = lax.psum((back, pairs), 'det')  31.2 us
    pallas_call x1, Pallas kernels, local_blocks(): call(functools.partial(gram_kernel, half), (kept((tiles, columns)), kept(...  8.58 us
    pallas_call x1, Pallas kernels, local_blocks(): call(functools.partial(setup_kernel, half, math.gcd(params, 3)), (kept((t...  7.4 us
    unnamed x20, local copies, waits for them, and re-layouts  6.42 us
    pallas_call x2, Pallas kernels, local_blocks(): call(functools.partial(next_kernel, half), (field, field, norm_shape, fie...  3.92 us
  transfers between devices with their start and end apart: 1, of which 1 were waited for; matrix products, arithmetic and copies ran while one was open for 0% of the time, Pallas kernels for 0%

profile of v5, /device:TPU:0, one launch (start us, length us, event | category | flops | bytes accessed | tf_op | source)
XLA Modules:
  0.0 185.0 jit_solution(5253218655398338320)
XLA Ops:
  7.2 0.0 all-reduce.3.cloned.1.call-start
  7.2 7.4 %shard_map.68 = (bf16[512,512]{1,0:T(8,128)(2,1)S(1)}, f32[136,512]{1,0:T(8,128)S(1)}, f32[12,512,128]{2,1,0:T(8,128)S(1)}, f32[8,456,128]{2,1,0:T(8,128)S(1)}) custom-call(s32[1]{0:T(128)} %bitcast.me_ref, s32[1,512]{1,0:T(1,128)} %bitcast.6, s32[1,512]{1,0:T(1,128)} %bitcast.7, f32[1,512]{1,0:T(1,128)} %bitcast.8, f32[512,128]{1,0:T(8,128)} %obs_hbm.1, ...), custom_call_target="tpu_custom_call" | custom-call | tf_op jit(solution)/shard_map/pallas_call | solution.py:897
  14.6 0.0 copy-start.3
  14.6 0.8 copy-done.3
  15.4 51.2 %all_to_all.30.arrived_ref = f32[8,456,128]{2,1,0:T(8,128)S(1)} all-to-all(f32[8,456,128]{2,1,0:T(8,128)S(1)} %get-tuple-element.29.sent_ref), channel_id=1, replica_groups=mesh['track'=8,'det'=4] {'track'}, dimensions={0} | all-to-all | bytes 3735552 | tf_op jit(solution)/shard_map/all_to_all | solution.py:894
  66.6 8.6 %shard_map.69 = (f32[512,128]{1,0:T(8,128)S(1)}, f32[136,512]{1,0:T(8,128)S(1)}, f32[8,64,128]{2,1,0:T(8,128)S(1)}, f32[80,512]{1,0:T(8,128)S(1)}) custom-call(s32[1]{0:T(128)} %bitcast.me_ref, f32[8,456,128]{2,1,0:T(8,128)S(1)} %get-tuple-element.29.sent_ref, f32[8,456,128]{2,1,0:T(8,128)S(1)} %all_to_all.30.arrived_ref, ...), custom_call_target="tpu_custom_call" | custom-call | tf_op jit(solution)/shard_map/pallas_call | solution.py:921
  75.2 0.0 copy-start
  75.2 0.7 copy-done
  75.9 0.0 copy-start.5
  75.9 0.7 copy-done.5
  76.6 0.0 copy-start.7
  76.6 0.7 copy-done.7
  77.3 0.6 copy-done.9
  78.0 0.0 all-reduce.3.cloned.1.call-update
  78.0 31.2 %all-reduce.3.cloned.1.call-done = (f32[8,64,128]{2,1,0:T(8,128)}, f32[80,512]{1,0:T(8,128)}) async-done(((f32[8,64,128]{2,1,0:T(8,128)}, f32[80,512]{1,0:T(8,128)}), (f32[8,64,128]{2,1,0:T(8,128)}, f32[80,512]{1,0:T(8,128)})) %all-reduce.3.cloned.1.call-update) | async-done | bytes 426000 | tf_op jit(solution)/shard_map/psum | solution.py:931
  109.2 13.7 %all_to_all.31.arrived_ref = f32[8,64,128]{2,1,0:T(8,128)S(1)} all-to-all(f32[8,64,128]{2,1,0:T(8,128)} %get-tuple-element.56.kept_ref), channel_id=1, replica_groups=mesh['track'=8,'det'=4] {'track'}, dimensions={0} | all-to-all | bytes 524288 | tf_op jit(solution)/shard_map/all_to_all | solution.py:894
  122.9 1.0 copy-done.1
  123.9 0.9 copy-done.2
  124.8 0.9 copy-done.8
  125.8 1.7 shard_map.70
  127.5 10.0 %all_to_all.32.gathered_ref = f32[8,16,128]{2,1,0:T(8,128)S(1)} all-to-all(f32[8,16,128]{2,1,0:T(8,128)S(1)} %get-tuple-element.35), channel_id=1, replica_groups=mesh['track'=8,'det'=4] {'track'}, dimensions={0} | all-to-all | bytes 131072 | tf_op jit(solution)/shard_map/all_to_all | solution.py:894
  137.5 2.0 %shard_map.71 = (f32[8,16,128]{2,1,0:T(8,128)S(1)}, f32[8,16,128]{2,1,0:T(8,128)S(1)}, f32[8,128]{1,0:T(8,128)S(1)}, f32[8,16,128]{2,1,0:T(8,128)S(1)}, f32[8,16,128]{2,1,0:T(8,128)S(1)}) custom-call(s32[1]{0:T(128)} %bitcast.me_ref, f32[8,16,128]{2,1,0:T(8,128)S(1)} %all_to_all.32.gathered_ref, f32[8,16,128]{2,1,0:T(8,128)S(1)} %get-tuple-element.36.grad_ref.direction_ref, ...), custom_call_target="tpu_custom_call" | custom-call | tf_op jit(solution)/shard_map/pallas_call | solution.py:944
  139.4 9.3 %all_to_all.33.gathered_ref = f32[8,16,128]{2,1,0:T(8,128)S(1)} all-to-all(f32[8,16,128]{2,1,0:T(8,128)S(1)} %get-tuple-element.40), channel_id=1, replica_groups=mesh['track'=8,'det'=4] {'track'}, dimensions={0} | all-to-all | bytes 131072 | tf_op jit(solution)/shard_map/all_to_all | solution.py:894
  148.8 2.0 %shard_map.72 = (f32[8,16,128]{2,1,0:T(8,128)S(1)}, f32[8,16,128]{2,1,0:T(8,128)S(1)}, f32[8,128]{1,0:T(8,128)S(1)}, f32[8,16,128]{2,1,0:T(8,128)S(1)}, f32[8,16,128]{2,1,0:T(8,128)S(1)}) custom-call(s32[1]{0:T(128)} %bitcast.me_ref, f32[8,16,128]{2,1,0:T(8,128)S(1)} %all_to_all.33.gathered_ref, f32[8,16,128]{2,1,0:T(8,128)S(1)} %get-tuple-element.41.grad_ref, ...), custom_call_target="tpu_custom_call" | custom-call | tf_op jit(solution)/shard_map/pallas_call | solution.py:944
  150.7 0.0 copy-start.4
  150.7 0.0 copy-start.6
  150.8 9.4 %all_to_all.34.gathered_ref = f32[8,16,128]{2,1,0:T(8,128)S(1)} all-to-all(f32[8,16,128]{2,1,0:T(8,128)S(1)} %get-tuple-element.45), channel_id=1, replica_groups=mesh['track'=8,'det'=4] {'track'}, dimensions={0} | all-to-all | bytes 131072 | tf_op jit(solution)/shard_map/all_to_all | solution.py:894
  160.2 2.4 %shard_map.73 = (f32[8,16,128]{2,1,0:T(8,128)S(1)}, f32[8,128]{1,0:T(8,128)S(1)}, f32[8,16,128]{2,1,0:T(8,128)S(1)}, f32[8,136,128]{2,1,0:T(8,128)S(1)}) custom-call(s32[1]{0:T(128)} %bitcast.me_ref, f32[8,16,128]{2,1,0:T(8,128)S(1)} %all_to_all.34.gathered_ref, f32[8,16,128]{2,1,0:T(8,128)S(1)} %get-tuple-element.46.grad_ref, ...), custom_call_target="tpu_custom_call" | custom-call | tf_op jit(solution)/shard_map/pallas_call | solution.py:952
  162.6 13.8 %all_to_all.35.arrived_ref = f32[8,136,128]{2,1,0:T(8,128)S(1)} all-to-all(f32[8,136,128]{2,1,0:T(8,128)S(1)} %get-tuple-element.50.sent_ref), channel_id=1, replica_groups=mesh['track'=8,'det'=4] {'track'}, dimensions={0} | all-to-all | bytes 1114112 | tf_op jit(solution)/shard_map/all_to_all | solution.py:894
  176.4 0.0 copy-done.4
  176.4 0.0 copy-done.6
  176.4 1.8 shard_map.74
  (5 shorter events, 0.0 us)
Async XLA Ops:
  7.2 102.0 %all-reduce.3.cloned.1.call-start = ((), (), s32[]{:S(2)}) async-start(), calls=%async_computation.6 | async-start | bytes 851968 | tf_op jit(solution)/shard_map/psum | solution.py:931
  14.6 0.8 copy-start.3
  75.2 0.7 copy-start
  75.9 0.7 copy-start.5
  76.6 0.7 copy-start.7
  77.3 0.7 copy-start.9
  122.9 1.0 copy-start.1
  123.9 0.9 copy-start.2
  124.8 0.9 copy-start.8
  150.7 25.7 %copy-start.4 = (bf16[512,512]{1,0:T(8,128)(2,1)S(1)}, bf16[512,512]{1,0:T(8,128)(2,1)}, u32[]{:S(2)}) copy-start(bf16[512,512]{1,0:T(8,128)(2,1)} %copy-done.3) | copy-start | bytes 1572868
  150.7 25.7 %copy-start.6 = (f32[512,128]{1,0:T(8,128)S(1)}, f32[512,128]{1,0:T(8,128)}, u32[]{:S(2)}) copy-start(f32[512,128]{1,0:T(8,128)} %copy-done.5) | copy-start | bytes 786436
Sparse Core Ops, SparseCore 0:
  78.1 31.0 all-reduce.2

commit v6 on v4

v6 whole, which is shorter than its diff:
```python
import functools
import math

import jax
import jax.numpy as jnp
from jax import lax
from jax.experimental import pallas as pl
from jax.experimental.pallas import tpu as pltpu
from jax.sharding import PartitionSpec as P

KNOT_DEV = 128
ITERS = 4
LANES = 128
SUB = 8
PAD = 16
VMEM_BYTES = 14 * 2**20


damping = 1.0

SMEM = pl.BlockSpec(memory_space=pltpu.SMEM)
VMEM = pl.BlockSpec(memory_space=pltpu.VMEM)
ANY = pl.BlockSpec(memory_space=pl.ANY)
PARAMS = pltpu.CompilerParams(vmem_limit_bytes=VMEM_BYTES)
HIGHEST = lax.Precision.HIGHEST


def kept(shape, dtype=jnp.float32):
    return pltpu.VMEM(shape, dtype)


def from_hbm(x):
    return pltpu.with_memory_space_constraint(x, pltpu.HBM)


def f32(*shape):
    return jax.ShapeDtypeStruct(shape, jnp.float32)


def dot(a, b, dims):
    return lax.dot_general(
        a, b, (dims, ((), ())), precision=HIGHEST, preferred_element_type=jnp.float32
    )


def split3(x):
    first = x.astype(jnp.bfloat16)
    rest = x - first.astype(jnp.float32)
    second = rest.astype(jnp.bfloat16)
    third = (rest - second.astype(jnp.float32)).astype(jnp.bfloat16)
    return first, second, third


def bf16_dot(a, b):
    return jnp.dot(a, b, preferred_element_type=jnp.float32)


def turn(x, shift):
    shift = shift % LANES
    return x if shift == 0 else pltpu.roll(x, shift, 1)


def lane_group(shape, q):
    return lax.broadcasted_iota(jnp.int32, shape, 1) // q


def to_crossing(arrays, perm, q, store):
    tiles = arrays[0].shape[0]
    groups = LANES // q
    stacked = []
    for x in arrays:
        across = jnp.concatenate(
            [x[c * LANES : (c + 1) * LANES].T for c in range(tiles // LANES)], axis=1
        )
        stacked.extend(split3(across))
    moved = bf16_dot(jnp.concatenate(stacked, axis=0), perm)
    group = lane_group((q, LANES), q)
    for index in range(len(arrays)):
        third, second, first = (
            moved[(3 * index + part) * LANES : (3 * index + part + 1) * LANES] for part in (2, 1, 0)
        )
        whole = third + second + first
        for c in range(tiles // LANES):
            for b in range(groups):
                block = None
                for h in range(groups):
                    piece = turn(
                        whole[h * q : (h + 1) * q, c * LANES : (c + 1) * LANES], (h - b) * q
                    )
                    block = piece if block is None else jnp.where(group == h, piece, block)
                store(index, c * groups + b, block)


def from_crossing(load, perm, q, tiles):
    groups = LANES // q
    group = lane_group((q, LANES), q)
    parts = []
    for c in range(tiles // LANES):
        rows = []
        for h in range(groups):
            block = None
            for b in range(groups):
                piece = turn(load(c * groups + b), (b - h) * q)
                block = piece if block is None else jnp.where(group == b, piece, block)
            rows.append(block)
        parts.append(jnp.concatenate(rows, axis=0).T)
    stacked = jnp.concatenate(parts, axis=0)
    return sum(bf16_dot(perm, part) for part in reversed(split3(stacked)))


def crossing_order(me, match):
    tiles = match.shape[1]
    slot = lax.broadcasted_iota(jnp.int32, (1, tiles), 1)
    peer = match // tiles
    other = match - peer * tiles
    inner = jnp.where(
        peer == me,
        jnp.minimum(slot, other) + jnp.where(slot > other, tiles, 0),
        jnp.where(peer > me, slot, other),
    )
    key = (peer * (2 * tiles) + inner).astype(jnp.float32)
    key_cols = jnp.broadcast_to(key, (LANES, tiles)).T[:, :1]
    place = jnp.sum(jnp.where(key < key_cols, 1.0, 0.0), axis=1, keepdims=True)
    cols = lax.broadcasted_iota(jnp.int32, (tiles, tiles), 1).astype(jnp.float32)
    return jnp.where(place == cols, 1.0, 0.0).astype(jnp.bfloat16)


def order_kernel(q, me_ref, match_hbm, obs_hbm, obs_out, match_ref, obs_ref, sems):
    copies = [
        pltpu.make_async_copy(match_hbm, match_ref, sems.at[0]),
        pltpu.make_async_copy(obs_hbm, obs_ref, sems.at[1]),
    ]
    for copy in copies:
        copy.start()
    copies[0].wait()
    perm = crossing_order(me_ref[0], match_ref[...])
    copies[1].wait()

    def put(_, index, block):
        obs_out[index * q : (index + 1) * q, :] = block

    to_crossing([obs_ref[...]], perm, q, put)


def jac_kernel(
    q,
    together,
    me_ref,
    match_hbm,
    knot_hbm,
    frac_hbm,
    sent_hbm,
    jac_hbm,
    perm_ref,
    weight_ref,
    edge_ref,
    sent_ref,
    out_ref,
    match_ref,
    knot_ref,
    frac_ref,
    jac_ref,
    sems,
):
    params, tiles, _ = jac_ref.shape
    pairs = [(match_hbm, match_ref), (knot_hbm, knot_ref), (frac_hbm, frac_ref)]
    pairs += [(jac_hbm.at[p], jac_ref.at[p]) for p in range(params)]
    pairs += [(sent_hbm, sent_ref)]
    copies = [
        pltpu.make_async_copy(source, target, sems.at[index])
        for index, (source, target) in enumerate(pairs)
    ]
    for copy in copies:
        copy.start()
    for copy in copies[:3]:
        copy.wait()
    perm = crossing_order(me_ref[0], match_ref[...])
    perm_ref[...] = perm

    row = lax.broadcasted_iota(jnp.int32, (SUB, tiles), 0)
    facts = jnp.where(row == 0, knot_ref[...].astype(jnp.float32), frac_ref[...])
    moved = sum(bf16_dot(part, perm) for part in reversed(split3(facts)))
    knot, frac = moved[0:1], moved[1:2]
    knots = lax.broadcasted_iota(jnp.int32, (KNOT_DEV, tiles), 0).astype(jnp.float32)
    main = jnp.where(knots == knot, 1.0 - frac, 0.0) + jnp.where(knots == knot + 1.0, frac, 0.0)
    first_row = lax.broadcasted_iota(jnp.int32, (PAD, tiles), 0) == 0
    edge = jnp.where(first_row, jnp.where(knot == KNOT_DEV - 1.0, frac, 0.0), 0.0)
    edge_ref[...] = edge[0:SUB]
    for index, (upper, lower) in enumerate(zip(split3(main), split3(edge))):
        weight_ref[index, 0:KNOT_DEV, :] = upper
        weight_ref[index, KNOT_DEV : KNOT_DEV + PAD, :] = lower

    for first in range(0, params, together):
        for p in range(first, first + together):
            copies[3 + p].wait()

        def put(index, block_index, block):
            out_ref[first + index, block_index * q : (block_index + 1) * q, :] = block

        to_crossing([jac_ref[p] for p in range(first, first + together)], perm, q, put)
    copies[3 + params].wait()


def weight_dot(x, parts, over_tiles):
    dims = (((1,), (1 if over_tiles else 0,)), ((), ()))
    stacked = jnp.concatenate(split3(x), axis=0)
    first, second, third = (
        lax.dot_general(
            stacked[0 : (3 - index) * PAD], part, dims, preferred_element_type=jnp.float32
        )
        for index, part in enumerate(parts)
    )
    small = third + second[PAD : 2 * PAD] + first[2 * PAD : 3 * PAD]
    return (small + (second[0:PAD] + first[PAD : 2 * PAD])) + first[0:PAD]


def row_sums(parts):
    row = lax.broadcasted_iota(jnp.int32, (SUB, LANES), 0)
    level = list(parts)
    zero = jnp.zeros((SUB, LANES), jnp.float32)
    while len(level) % SUB:
        level.append(zero)
    for distance in (1, 2, 4):
        first = (row // distance) % 2 == 0
        level = [
            jnp.where(first, a, b) + pltpu.roll(jnp.where(first, b, a), distance, 0)
            for a, b in zip(level[::2], level[1::2])
        ]
    return level[0] if len(level) == 1 else jnp.concatenate(level, axis=0)


def fold_rows(x):
    total = x[0:SUB]
    for step in range(1, x.shape[0] // SUB):
        total = total + x[step * SUB : (step + 1) * SUB]
    return total


def fold_lanes(x, q):
    shift = q
    while shift < LANES:
        x = x + pltpu.roll(x, shift, 1)
        shift *= 2
    return x


def crossing_values(me, arrived_ref, out_ref, q):
    out_ref[...] = arrived_ref[...]
    own = arrived_ref[pl.ds(pl.multiple_of(me * q, SUB), q), :]
    lane = lax.broadcasted_iota(jnp.int32, (q, LANES), 1)
    swapped = jnp.where(lane % q < q // 2, turn(own, -(q // 2)), turn(own, q // 2))
    out_ref[pl.ds(pl.multiple_of(me * q, SUB), q), :] = swapped


def difference(me, sent_ref, arrived_ref, out_ref, q):
    crossing_values(me, arrived_ref, out_ref, q)
    out_ref[...] = sent_ref[...] - out_ref[...]


def adjoint_kernel(
    q, me_ref, sent_ref, arrived_ref, jac_ref, weight_ref, diff_ref, send_ref, values_ref
):
    params, tiles, _ = jac_ref.shape
    difference(me_ref[0], sent_ref, arrived_ref, diff_ref, q)
    groups = LANES // q
    group = lane_group((PAD, LANES), q)
    for c in range(tiles // LANES):
        values = None
        for i in range(groups):
            rows = slice((c * groups + i) * q, (c * groups + i + 1) * q)
            diff = diff_ref[rows, :]
            sums = fold_lanes(
                row_sums([fold_rows(jac_ref[p, rows, :] * diff) for p in range(params)]), q
            )
            values = sums if values is None else jnp.where(group == i, sums, values)
        values_ref[:, c * LANES : (c + 1) * LANES] = values
    spread = weight_dot(values_ref[...], [weight_ref[index] for index in range(3)], True)
    lane = lax.broadcasted_iota(jnp.int32, (PAD, LANES), 1)
    row = lax.broadcasted_iota(jnp.int32, (PAD, LANES), 0)
    spill = jnp.sum(
        jnp.where(lane == row, spread[:, KNOT_DEV : KNOT_DEV + 1], 0.0), axis=0, keepdims=True
    )
    block = jnp.where(row < params, spread[:, :KNOT_DEV], jnp.where(row == params, spill, 0.0))
    for d in range(send_ref.shape[0]):
        send_ref[d] = block


def field_sums(gathered_ref, n_track, n_det, params, store, base=0):
    lane = lax.broadcasted_iota(jnp.int32, (PAD, LANES), 1)
    row = lax.broadcasted_iota(jnp.int32, (PAD, LANES), 0)
    spill = jnp.zeros((PAD, 1), jnp.float32)
    for b in range(n_track):
        total = gathered_ref[b * n_det, base : base + PAD, :]
        for d in range(1, n_det):
            total = total + gathered_ref[b * n_det + d, base : base + PAD, :]
        field = jnp.where(row < params, total, 0.0)
        field = field + jnp.where(lane == 0, spill, 0.0)
        store(b, field)
        spill = jnp.sum(
            jnp.where((lane == row) & (row < params), total[params : params + 1], 0.0),
            axis=1,
            keepdims=True,
        )


def total_of(x):
    return jnp.sum(jnp.sum(x, axis=0), keepdims=True).reshape(1, 1)


def full_dot(a_ref, b_ref):
    total = a_ref[0] * b_ref[0]
    for b in range(1, a_ref.shape[0]):
        total = total + a_ref[b] * b_ref[b]
    return jnp.sum(total, keepdims=True)


def predict(me, q, direction_ref, jac_ref, weight_ref, edge_ref, interp_ref, sent_ref):
    params, tiles, _ = jac_ref.shape
    n_track = direction_ref.shape[0]
    following = direction_ref[jnp.minimum(me + 1, n_track - 1)][:, 0:1]
    following = jnp.where(me + 1 < n_track, following, 0.0)
    parts = [weight_ref[index, 0:KNOT_DEV, :] for index in range(3)]
    interp = weight_dot(direction_ref[me], parts, False) + following * edge_ref[0:1, :]
    groups = LANES // q
    group = lane_group((PAD, LANES), q)
    for c in range(tiles // LANES):
        chunk = interp[:, c * LANES : (c + 1) * LANES]
        for i in range(groups):
            wide = None
            for h in range(groups):
                piece = turn(chunk, (h - i) * q)
                wide = piece if wide is None else jnp.where(group == h, piece, wide)
            interp_ref[c * groups + i] = wide

    def block_values(b, carry):
        rows = pl.ds(pl.multiple_of(b * q, SUB), q)
        interp = interp_ref[b]
        total = jac_ref[0, rows, :] * interp[0:1]
        for p in range(1, params):
            total = total + jac_ref[p, rows, :] * interp[p : p + 1]
        sent_ref[rows, :] = total
        return carry

    lax.fori_loop(0, tiles // q, block_values, 0)


def first_kernel(
    q,
    n_det,
    me_ref,
    gathered_ref,
    jac_ref,
    weight_ref,
    edge_ref,
    grad_ref,
    norm_ref,
    sent_ref,
    interp_ref,
):
    n_track = grad_ref.shape[0]

    def put(b, field):
        grad_ref[b] = field

    field_sums(gathered_ref, n_track, n_det, jac_ref.shape[0], put)
    norm_ref[...] = jnp.broadcast_to(full_dot(grad_ref, grad_ref), norm_ref.shape)
    predict(me_ref[0], q, grad_ref, jac_ref, weight_ref, edge_ref, interp_ref, sent_ref)


def step_kernel(
    q,
    n_det,
    me_ref,
    gathered_ref,
    jac_ref,
    weight_ref,
    edge_ref,
    grad_ref,
    direction_ref,
    norm_ref,
    knot_ref,
    grad_out,
    direction_out,
    norm_out,
    knot_out,
    length_out,
    sent_ref,
    image_ref,
    interp_ref,
):
    n_track = grad_ref.shape[0]
    me = me_ref[0]

    def put(b, field):
        image_ref[b] = field + damping * direction_ref[b]

    field_sums(gathered_ref, n_track, n_det, jac_ref.shape[0], put)
    norm = norm_ref[0:1, 0:1]
    length = norm / full_dot(direction_ref, image_ref)
    length_out[...] = jnp.broadcast_to(length, length_out.shape)
    knot_out[...] = knot_ref[...] + length * direction_ref[me]
    for b in range(n_track):
        grad_out[b] = grad_ref[b] - length * image_ref[b]
    new_norm = full_dot(grad_out, grad_out)
    norm_out[...] = jnp.broadcast_to(new_norm, norm_out.shape)
    ratio = new_norm / norm
    for b in range(n_track):
        direction_out[b] = grad_out[b] + ratio * direction_ref[b]
    predict(me, q, direction_out, jac_ref, weight_ref, edge_ref, interp_ref, sent_ref)


def last_kernel(q, me_ref, sent_ref, arrived_ref, diff_ref, send_ref):
    difference(me_ref[0], sent_ref, arrived_ref, diff_ref, q)
    diff = diff_ref[...]
    squares = jnp.sum(diff * diff, axis=0, keepdims=True)
    send_ref[...] = jnp.broadcast_to(squares[None], send_ref.shape)


def restore_kernel(q, perm_ref, misfit_ref, diff_ref, *refs):
    steps = (len(refs) - 3) // 2
    residual_out, diff_out, residual_ref = refs[2 * steps :]
    tiles = misfit_ref.shape[0]
    residual = misfit_ref[...]
    for length_ref, change_ref in zip(refs[:steps], refs[steps : 2 * steps]):
        residual = residual - length_ref[0:1, 0:1] * change_ref[...]
    residual_ref[...] = residual
    for source, target in ((residual_ref, residual_out), (diff_ref, diff_out)):
        target[...] = from_crossing(
            lambda index: source[index * q : (index + 1) * q, :], perm_ref[...], q, tiles
        )


def finish_kernel(
    me_ref, squares_ref, direction_ref, norm_ref, knot_ref, residual_ref, diff_ref, knot_out, residual_out
):
    params = knot_out.shape[0]
    squares = squares_ref[0]
    for d in range(1, squares_ref.shape[0]):
        squares = squares + squares_ref[d]
    curvature = 0.5 * jnp.sum(squares, keepdims=True) + damping * full_dot(
        direction_ref, direction_ref
    )
    length = norm_ref[0:1, 0:1] / curvature
    knot = knot_ref[...] + length * direction_ref[me_ref[0]]
    knot_out[...] = knot[0:params]
    residual_out[...] = residual_ref[...] - length * diff_ref[...]


def call(kernel, outs, ins, scratch=()):
    return pl.pallas_call(
        kernel,
        out_shape=outs,
        in_specs=ins,
        out_specs=jax.tree.map(lambda _: VMEM, outs),
        scratch_shapes=list(scratch),
        compiler_params=PARAMS,
    )


def local(jac, obs, match, tile_knot, tile_frac):
    tiles, params, columns = jac.shape
    n_track = lax.axis_size("track")
    n_det = lax.axis_size("det")
    n_all = n_track * n_det
    q = tiles // n_track
    me = lax.axis_index("track").astype(jnp.int32).reshape(1)

    def crossing(values):
        return lax.all_to_all(values, "track", split_axis=0, concat_axis=0, tiled=True)

    def everywhere(values):
        return lax.all_to_all(values, ("track", "det"), split_axis=0, concat_axis=0, tiled=True)

    match_row = from_hbm(match[None])
    row_scratch = [pltpu.VMEM((1, tiles), jnp.int32)] * 2 + [pltpu.VMEM((1, tiles), jnp.float32)]
    sent = call(
        functools.partial(order_kernel, q),
        f32(tiles, columns),
        [SMEM, ANY, ANY],
        [
            row_scratch[0],
            pltpu.VMEM((tiles, columns), jnp.float32),
            pltpu.SemaphoreType.DMA((2,)),
        ],
    )(me, match_row, from_hbm(obs))
    arrived = crossing(sent)
    perm, weights, edge, sent, jac_rows = call(
        functools.partial(jac_kernel, q, math.gcd(params, 3)),
        (
            kept((tiles, tiles), jnp.bfloat16),
            kept((3, KNOT_DEV + PAD, tiles), jnp.bfloat16),
            kept((SUB, tiles)),
            kept((tiles, columns)),
            kept((params, tiles, columns)),
        ),
        [SMEM] + [ANY] * 5,
        row_scratch
        + [
            pltpu.VMEM((params, tiles, columns), jnp.float32),
            pltpu.SemaphoreType.DMA((4 + params,)),
        ],
    )(
        me,
        match_row,
        from_hbm(tile_knot[None]),
        from_hbm(tile_frac[None]),
        from_hbm(sent),
        from_hbm(jnp.transpose(jac, (1, 0, 2))),
    )

    def adjoint(sent, arrived):
        diff, payload = call(
            functools.partial(adjoint_kernel, q),
            (f32(tiles, columns), f32(n_all, PAD, LANES)),
            [SMEM] + [VMEM] * 4,
            [pltpu.VMEM((PAD, tiles), jnp.float32)],
        )(me, sent, arrived, jac_rows, weights)
        return diff, everywhere(payload)

    field = f32(n_track, PAD, LANES)
    scalar = f32(SUB, LANES)
    interp = pltpu.VMEM((n_track, PAD, LANES), jnp.float32)
    misfit, gathered = adjoint(sent, arrived)
    gradient, slope_norm, sent = call(
        functools.partial(first_kernel, q, n_det),
        (field, scalar, f32(tiles, columns)),
        [SMEM] + [VMEM] * 4,
        [interp],
    )(me, gathered, jac_rows, weights, edge)
    direction = gradient
    knot_field = jnp.zeros((PAD, KNOT_DEV), jnp.float32)
    lengths, changes = [], []
    for iteration in range(ITERS - 1):
        change, gathered = adjoint(sent, crossing(sent))
        gradient, direction, slope_norm, knot_field, length, sent = call(
            functools.partial(step_kernel, q, n_det),
            (field, field, scalar, f32(PAD, KNOT_DEV), scalar, f32(tiles, columns)),
            [SMEM] + [VMEM] * 8,
            [pltpu.VMEM((n_track, PAD, LANES), jnp.float32), interp],
        )(
            me, gathered, jac_rows, weights, edge, gradient, direction, slope_norm, knot_field
        )
        lengths.append(length)
        changes.append(change)
    change, squares = call(
        functools.partial(last_kernel, q),
        (f32(tiles, columns), f32(n_all, 1, LANES)),
        [SMEM] + [VMEM] * 2,
    )(me, sent, crossing(sent))
    squares = everywhere(squares)
    residual, change = call(
        functools.partial(restore_kernel, q),
        (f32(tiles, columns), f32(tiles, columns)),
        [VMEM] * (3 + 2 * len(changes)),
        [pltpu.VMEM((tiles, columns), jnp.float32)],
    )(perm, misfit, change, *lengths, *changes)
    return call(
        finish_kernel,
        (f32(params, KNOT_DEV), f32(tiles, columns)),
        [SMEM] + [VMEM] * 6,
    )(me, squares, direction, slope_norm, knot_field, residual, change)


def solution(mesh):
    in_specs = (P("track", None, "det"), P("track", "det"), P("track"), P("track"), P("track"))
    out_specs = (P(None, "track"), P("track", "det"))
    return jax.shard_map(local, mesh=mesh, in_specs=in_specs, out_specs=out_specs, check_vma=False)
```

time: 148 us -> 144 us (0.973)
  Pallas kernels: 23.1 us -> 17.5 us
  local copies, waits for them, and re-layouts: 4.72 us -> 9.51 us
  waiting for transfers between devices: 7.78 us -> 3.22 us
    pallas_call x4, Pallas kernels: 7.61 us -> 2.69 us  [adjoint(): call(functools.partial(adjoint_kernel, q), (f32(tiles, columns), f32(n_al...]
    unnamed x10 -> x28, local copies, waits for them, and re-layouts: 4.72 us -> 9.51 us
    all_to_all x1, waiting for transfers between devices: 4.81 us -> 2 us  [everywhere(): lax.all_to_all(values, ('track', 'det'), split_axis=0, concat_axis=0, til...]
    all_to_all x1, waiting for transfers between devices: 2.98 us -> 1.23 us  [crossing(): lax.all_to_all(values, 'track', split_axis=0, concat_axis=0, tiled=True)]
  transfers between devices with their start and end apart: 2 -> 2, of which waited for: 2 -> 2; matrix products, arithmetic and copies ran while one was open for 0% -> 0% of each run, Pallas kernels for 4% -> 5%
where the time goes in v6:
time: 144 us
  blocking collectives  102 us (71%)
  Pallas kernels  17.5 us (12%)
  starting transfers between devices  10.3 us (7%)
  local copies, waits for them, and re-layouts  9.51 us (7%)
  waiting for transfers between devices  3.22 us (2%)
    all_to_all x4, blocking collectives, everywhere(): lax.all_to_all(values, ('track', 'det'), split_axis=0, concat_axis=0, til...  55.4 us
    all_to_all x4, blocking collectives, crossing(): lax.all_to_all(values, 'track', split_axis=0, concat_axis=0, tiled=True)  46.8 us
    unnamed x28, local copies, waits for them, and re-layouts  9.51 us
    all_to_all x1, starting transfers between devices, crossing(): lax.all_to_all(values, 'track', split_axis=0, concat_axis=0, tiled=True)  7.29 us
    pallas_call x1, Pallas kernels, local(): call(functools.partial(jac_kernel, q, math.gcd(params, 3)), (kept((tiles,...  5.42 us
    pallas_call x3, Pallas kernels, local(): call(functools.partial(step_kernel, q, n_det), (field, field, scalar, f32...  3.51 us
    all_to_all x1, starting transfers between devices, everywhere(): lax.all_to_all(values, ('track', 'det'), split_axis=0, concat_axis=0, til...  3 us
  transfers between devices with their start and end apart: 2, of which 2 were waited for; matrix products, arithmetic and copies ran while one was open for 0% of the time, Pallas kernels for 5%

profile of v6, /device:TPU:0, one launch (start us, length us, event | category | flops | bytes accessed | tf_op | source)
XLA Modules:
  0.0 143.5 jit_solution(14136263879084372224)
XLA Ops:
  0.6 2.3 %shard_map.68.sent_hbm = f32[512,128]{1,0:T(8,128)} custom-call(s32[1]{0:T(128)} %bitcast.me_ref, s32[1,512]{1,0:T(1,128)} %bitcast.25, f32[512,128]{1,0:T(8,128)} %obs_hbm.1), custom_call_target="tpu_custom_call" | custom-call | tf_op jit(solution)/shard_map/pallas_call | solution.py:476
  2.9 7.3 %all-to-all-start = ((f32[8,64,128]{2,1,0:T(8,128)}), f32[8,64,128]{2,1,0:T(8,128)S(1)}, u32[]{:S(2)}, u32[]{:S(2)}) async-start(f32[8,64,128]{2,1,0:T(8,128)} %bitcast.5), calls=%async_computation | async-start | bytes 524288 | tf_op jit(solution)/shard_map/all_to_all | solution.py:469
  10.2 5.4 %shard_map.69 = (bf16[512,512]{1,0:T(8,128)(2,1)S(1)}, bf16[3,144,512]{2,1,0:T(8,128)(2,1)S(1)}, f32[8,512]{1,0:T(8,128)S(1)}, f32[512,128]{1,0:T(8,128)S(1)}, f32[12,512,128]{2,1,0:T(8,128)S(1)}) custom-call(s32[1]{0:T(128)} %bitcast.me_ref, s32[1,512]{1,0:T(1,128)} %bitcast.26, s32[1,512]{1,0:T(1,128)} %bitcast.27, f32[1,512]{1,0:T(1,128)} %bitcast.28, ...), custom_call_target="tpu_custom_call" | custom-call | tf_op jit(solution)/shard_map/pallas_call | solution.py:487
  15.7 0.8 copy-done
  16.4 0.8 copy-done.2
  17.2 0.7 copy-done.12
  17.9 1.2 all-to-all-done
  19.1 1.0 copy-done.1
  20.2 0.9 copy-done.13
  21.8 0.7 copy-done.4
  22.5 15.2 %all_to_all.80.gathered_ref = f32[32,16,128]{2,1,0:T(8,128)S(1)} all-to-all(f32[32,16,128]{2,1,0:T(8,128)S(1)} %get-tuple-element.42), channel_id=1, replica_groups=mesh['track'=8,'det'=4] {'track','det'}, dimensions={0} | all-to-all | bytes 524288 | tf_op jit(solution)/shard_map/all_to_all | solution.py:472
  38.4 11.7 %all_to_all.81 = f32[8,64,128]{2,1,0:T(8,128)S(1)} all-to-all(f32[8,64,128]{2,1,0:T(8,128)S(1)} %bitcast.18), channel_id=1, replica_groups=mesh['track'=8,'det'=4] {'track'}, dimensions={0} | all-to-all | bytes 524288 | tf_op jit(solution)/shard_map/all_to_all | solution.py:469
  50.0 0.7 shard_map.72
  50.7 13.4 %all_to_all.82.gathered_ref = f32[32,16,128]{2,1,0:T(8,128)S(1)} all-to-all(f32[32,16,128]{2,1,0:T(8,128)S(1)} %get-tuple-element.45), channel_id=1, replica_groups=mesh['track'=8,'det'=4] {'track','det'}, dimensions={0} | all-to-all | bytes 524288 | tf_op jit(solution)/shard_map/all_to_all | solution.py:472
  64.2 1.0 shard_map.73
  65.1 11.7 %all_to_all.83 = f32[8,64,128]{2,1,0:T(8,128)S(1)} all-to-all(f32[8,64,128]{2,1,0:T(8,128)S(1)} %bitcast.17), channel_id=1, replica_groups=mesh['track'=8,'det'=4] {'track'}, dimensions={0} | all-to-all | bytes 524288 | tf_op jit(solution)/shard_map/all_to_all | solution.py:469
  77.5 13.4 %all_to_all.84.gathered_ref = f32[32,16,128]{2,1,0:T(8,128)S(1)} all-to-all(f32[32,16,128]{2,1,0:T(8,128)S(1)} %get-tuple-element.49), channel_id=1, replica_groups=mesh['track'=8,'det'=4] {'track','det'}, dimensions={0} | all-to-all | bytes 524288 | tf_op jit(solution)/shard_map/all_to_all | solution.py:472
  90.9 1.0 shard_map.75
  91.9 11.7 %all_to_all.85 = f32[8,64,128]{2,1,0:T(8,128)S(1)} all-to-all(f32[8,64,128]{2,1,0:T(8,128)S(1)} %bitcast.16), channel_id=1, replica_groups=mesh['track'=8,'det'=4] {'track'}, dimensions={0} | all-to-all | bytes 524288 | tf_op jit(solution)/shard_map/all_to_all | solution.py:469
  104.3 0.7 copy-done.10
  105.0 13.4 %all_to_all.86.gathered_ref = f32[32,16,128]{2,1,0:T(8,128)S(1)} all-to-all(f32[32,16,128]{2,1,0:T(8,128)S(1)} %get-tuple-element.55), channel_id=1, replica_groups=mesh['track'=8,'det'=4] {'track','det'}, dimensions={0} | all-to-all | bytes 524288 | tf_op jit(solution)/shard_map/all_to_all | solution.py:472
  118.4 1.6 %shard_map.77 = (f32[8,16,128]{2,1,0:T(8,128)}, f32[8,16,128]{2,1,0:T(8,128)S(1)}, f32[8,128]{1,0:T(8,128)S(1)}, f32[16,128]{1,0:T(8,128)S(1)}, f32[8,128]{1,0:T(8,128)S(1)}, /*index=5*/f32[512,128]{1,0:T(8,128)S(1)}) custom-call(s32[1]{0:T(128)} %bitcast.me_ref, f32[32,16,128]{2,1,0:T(8,128)S(1)} %all_to_all.86.gathered_ref, ...), custom_call_target="tpu_custom_call" | custom-call | tf_op jit(solution)/shard_map/pallas_call | solution.py:535
  120.0 11.7 %all_to_all.87 = f32[8,64,128]{2,1,0:T(8,128)S(1)} all-to-all(f32[8,64,128]{2,1,0:T(8,128)S(1)} %bitcast.22), channel_id=1, replica_groups=mesh['track'=8,'det'=4] {'track'}, dimensions={0} | all-to-all | bytes 524288 | tf_op jit(solution)/shard_map/all_to_all | solution.py:469
  131.7 0.8 shard_map.78
  132.5 3.0 %all-to-all-start.9 = ((f32[32,1,128]{2,1,0:T(1,128)}), f32[32,1,128]{2,1,0:T(1,128)S(1)}, u32[]{:S(2)}, u32[]{:S(2)}) async-start(f32[32,1,128]{2,1,0:T(1,128)} %get-tuple-element.61), calls=%async_computation.9 | async-start | bytes 32768 | tf_op jit(solution)/shard_map/all_to_all | solution.py:472
  135.5 1.0 copy-done.3
  136.5 0.9 copy-done.7
  137.5 0.9 copy-done.9
  138.4 0.9 copy-done.11
  139.4 1.2 shard_map.79
  140.6 2.0 %all-to-all-done.9.squares_ref = f32[32,1,128]{2,1,0:T(1,128)S(1)} async-done(((f32[32,1,128]{2,1,0:T(1,128)}), f32[32,1,128]{2,1,0:T(1,128)S(1)}, u32[]{:S(2)}, u32[]{:S(2)}) %all-to-all-start.9) | async-done | bytes 16416 | tf_op jit(solution)/shard_map/all_to_all | solution.py:472
  142.6 0.9 shard_map.80
  (22 shorter events, 2.7 us)
Async XLA Ops:
  2.9 16.2 %all-to-all-start = ((f32[8,64,128]{2,1,0:T(8,128)}), f32[8,64,128]{2,1,0:T(8,128)S(1)}, u32[]{:S(2)}, u32[]{:S(2)}) async-start(f32[8,64,128]{2,1,0:T(8,128)} %bitcast.5), calls=%async_computation | async-start | bytes 524288 | tf_op jit(solution)/shard_map/all_to_all | solution.py:469
  15.6 0.8 copy-start
  16.4 0.8 copy-start.2
  17.2 0.7 copy-start.12
  19.1 1.0 copy-start.1
  20.2 0.9 copy-start.13
  21.8 0.7 copy-start.4
  50.7 26.8 %copy-start.6 = (f32[512,128]{1,0:T(8,128)}, f32[512,128]{1,0:T(8,128)S(1)}, u32[]{:S(2)}) copy-start(f32[512,128]{1,0:T(8,128)S(1)} %get-tuple-element.71.refs_3_) | copy-start | bytes 786436
  77.5 26.8 %copy-start.8 = (f32[512,128]{1,0:T(8,128)}, f32[512,128]{1,0:T(8,128)S(1)}, u32[]{:S(2)}) copy-start(f32[512,128]{1,0:T(8,128)S(1)} %get-tuple-element.72.refs_4_) | copy-start | bytes 786436
  104.3 0.7 copy-start.10
  105.0 30.5 %copy-start.5 = (f32[512,128]{1,0:T(8,128)S(1)}, f32[512,128]{1,0:T(8,128)}, u32[]{:S(2)}) copy-start(f32[512,128]{1,0:T(8,128)} %copy-done.4) | copy-start | bytes 786436
  132.5 10.2 %all-to-all-start.9 = ((f32[32,1,128]{2,1,0:T(1,128)}), f32[32,1,128]{2,1,0:T(1,128)S(1)}, u32[]{:S(2)}, u32[]{:S(2)}) async-start(f32[32,1,128]{2,1,0:T(1,128)} %get-tuple-element.61), calls=%async_computation.9 | async-start | bytes 32768 | tf_op jit(solution)/shard_map/all_to_all | solution.py:472
  135.5 1.0 copy-start.3
  136.5 0.9 copy-start.7
  137.5 0.9 copy-start.9
  138.4 0.9 copy-start.11

commit v7 on v6

--- a/solution.py
+++ b/solution.py
@@ -31,6 +31,10 @@
 
 def from_hbm(x):
     return pltpu.with_memory_space_constraint(x, pltpu.HBM)
+
+
+def in_vmem(*arrays):
+    return [pltpu.with_memory_space_constraint(x, pltpu.VMEM) for x in arrays]
 
 
 def f32(*shape):
@@ -511,10 +515,10 @@
     def adjoint(sent, arrived):
         diff, payload = call(
             functools.partial(adjoint_kernel, q),
-            (f32(tiles, columns), f32(n_all, PAD, LANES)),
+            (kept((tiles, columns)), f32(n_all, PAD, LANES)),
             [SMEM] + [VMEM] * 4,
             [pltpu.VMEM((PAD, tiles), jnp.float32)],
-        )(me, sent, arrived, jac_rows, weights)
+        )(me, *in_vmem(sent, arrived, jac_rows, weights))
         return diff, everywhere(payload)
 
     field = f32(n_track, PAD, LANES)
@@ -526,7 +530,7 @@
         (field, scalar, f32(tiles, columns)),
         [SMEM] + [VMEM] * 4,
         [interp],
-    )(me, gathered, jac_rows, weights, edge)
+    )(me, *in_vmem(gathered, jac_rows, weights, edge))
     direction = gradient
     knot_field = jnp.zeros((PAD, KNOT_DEV), jnp.float32)
     lengths, changes = [], []
@@ -538,27 +542,30 @@
             [SMEM] + [VMEM] * 8,
             [pltpu.VMEM((n_track, PAD, LANES), jnp.float32), interp],
         )(
-            me, gathered, jac_rows, weights, edge, gradient, direction, slope_norm, knot_field
+            me,
+            *in_vmem(
+                gathered, jac_rows, weights, edge, gradient, direction, slope_norm, knot_field
+            ),
         )
         lengths.append(length)
         changes.append(change)
     change, squares = call(
         functools.partial(last_kernel, q),
-        (f32(tiles, columns), f32(n_all, 1, LANES)),
+        (kept((tiles, columns)), f32(n_all, 1, LANES)),
         [SMEM] + [VMEM] * 2,
-    )(me, sent, crossing(sent))
+    )(me, *in_vmem(sent, crossing(sent)))
     squares = everywhere(squares)
     residual, change = call(
         functools.partial(restore_kernel, q),
         (f32(tiles, columns), f32(tiles, columns)),
         [VMEM] * (3 + 2 * len(changes)),
         [pltpu.VMEM((tiles, columns), jnp.float32)],
-    )(perm, misfit, change, *lengths, *changes)
+    )(*in_vmem(perm, misfit, change, *lengths, *changes))
     return call(
         finish_kernel,
         (f32(params, KNOT_DEV), f32(tiles, columns)),
         [SMEM] + [VMEM] * 6,
-    )(me, squares, direction, slope_norm, knot_field, residual, change)
+    )(me, *in_vmem(squares, direction, slope_norm, knot_field, residual, change))
 
 
 def solution(mesh):

time: 144 us -> 144 us (level)
  no operation moved by 1% of the time
where the time goes in v7:
time: 144 us
  blocking collectives  102 us (71%)
  Pallas kernels  17.5 us (12%)
  starting transfers between devices  10.3 us (7%)
  local copies, waits for them, and re-layouts  9.51 us (7%)
  waiting for transfers between devices  3.22 us (2%)
    all_to_all x4, blocking collectives, everywhere(): lax.all_to_all(values, ('track', 'det'), split_axis=0, concat_axis=0, til...  55.4 us
    all_to_all x4, blocking collectives, crossing(): lax.all_to_all(values, 'track', split_axis=0, concat_axis=0, tiled=True)  46.8 us
    unnamed x28, local copies, waits for them, and re-layouts  9.51 us
    all_to_all x1, starting transfers between devices, crossing(): lax.all_to_all(values, 'track', split_axis=0, concat_axis=0, tiled=True)  7.29 us
    pallas_call x1, Pallas kernels, local(): call(functools.partial(jac_kernel, q, math.gcd(params, 3)), (kept((tiles,...  5.42 us
    pallas_call x3, Pallas kernels, local(): call(functools.partial(step_kernel, q, n_det), (field, field, scalar, f32...  3.51 us
    all_to_all x1, starting transfers between devices, everywhere(): lax.all_to_all(values, ('track', 'det'), split_axis=0, concat_axis=0, til...  3 us
  transfers between devices with their start and end apart: 2, of which 2 were waited for; matrix products, arithmetic and copies ran while one was open for 0% of the time, Pallas kernels for 5%

profile of v7, /device:TPU:0, one launch (start us, length us, event | category | flops | bytes accessed | tf_op | source)
XLA Modules:
  0.0 143.5 jit_solution(14136263879084372224)
XLA Ops:
  0.6 2.3 %shard_map.68.sent_hbm = f32[512,128]{1,0:T(8,128)} custom-call(s32[1]{0:T(128)} %bitcast.me_ref, s32[1,512]{1,0:T(1,128)} %bitcast.25, f32[512,128]{1,0:T(8,128)} %obs_hbm.1), custom_call_target="tpu_custom_call" | custom-call | tf_op jit(solution)/shard_map/pallas_call | solution.py:480
  2.9 7.3 %all-to-all-start = ((f32[8,64,128]{2,1,0:T(8,128)}), f32[8,64,128]{2,1,0:T(8,128)S(1)}, u32[]{:S(2)}, u32[]{:S(2)}) async-start(f32[8,64,128]{2,1,0:T(8,128)} %bitcast.5), calls=%async_computation | async-start | bytes 524288 | tf_op jit(solution)/shard_map/all_to_all | solution.py:473
  10.2 5.4 %shard_map.69 = (bf16[512,512]{1,0:T(8,128)(2,1)S(1)}, bf16[3,144,512]{2,1,0:T(8,128)(2,1)S(1)}, f32[8,512]{1,0:T(8,128)S(1)}, f32[512,128]{1,0:T(8,128)S(1)}, f32[12,512,128]{2,1,0:T(8,128)S(1)}) custom-call(s32[1]{0:T(128)} %bitcast.me_ref, s32[1,512]{1,0:T(1,128)} %bitcast.26, s32[1,512]{1,0:T(1,128)} %bitcast.27, f32[1,512]{1,0:T(1,128)} %bitcast.28, ...), custom_call_target="tpu_custom_call" | custom-call | tf_op jit(solution)/shard_map/pallas_call | solution.py:491
  15.7 0.8 copy-done
  16.4 0.8 copy-done.2
  17.2 0.7 copy-done.12
  17.9 1.2 all-to-all-done
  19.1 1.0 copy-done.1
  20.2 0.9 copy-done.13
  21.8 0.7 copy-done.4
  22.5 15.2 %all_to_all.80.gathered_ref = f32[32,16,128]{2,1,0:T(8,128)S(1)} all-to-all(f32[32,16,128]{2,1,0:T(8,128)S(1)} %get-tuple-element.42), channel_id=1, replica_groups=mesh['track'=8,'det'=4] {'track','det'}, dimensions={0} | all-to-all | bytes 524288 | tf_op jit(solution)/shard_map/all_to_all | solution.py:476
  38.4 11.7 %all_to_all.81 = f32[8,64,128]{2,1,0:T(8,128)S(1)} all-to-all(f32[8,64,128]{2,1,0:T(8,128)S(1)} %bitcast.18), channel_id=1, replica_groups=mesh['track'=8,'det'=4] {'track'}, dimensions={0} | all-to-all | bytes 524288 | tf_op jit(solution)/shard_map/all_to_all | solution.py:473
  50.0 0.7 shard_map.72
  50.7 13.4 %all_to_all.82.gathered_ref = f32[32,16,128]{2,1,0:T(8,128)S(1)} all-to-all(f32[32,16,128]{2,1,0:T(8,128)S(1)} %get-tuple-element.45), channel_id=1, replica_groups=mesh['track'=8,'det'=4] {'track','det'}, dimensions={0} | all-to-all | bytes 524288 | tf_op jit(solution)/shard_map/all_to_all | solution.py:476
  64.2 1.0 shard_map.73
  65.1 11.7 %all_to_all.83 = f32[8,64,128]{2,1,0:T(8,128)S(1)} all-to-all(f32[8,64,128]{2,1,0:T(8,128)S(1)} %bitcast.17), channel_id=1, replica_groups=mesh['track'=8,'det'=4] {'track'}, dimensions={0} | all-to-all | bytes 524288 | tf_op jit(solution)/shard_map/all_to_all | solution.py:473
  77.5 13.4 %all_to_all.84.gathered_ref = f32[32,16,128]{2,1,0:T(8,128)S(1)} all-to-all(f32[32,16,128]{2,1,0:T(8,128)S(1)} %get-tuple-element.49), channel_id=1, replica_groups=mesh['track'=8,'det'=4] {'track','det'}, dimensions={0} | all-to-all | bytes 524288 | tf_op jit(solution)/shard_map/all_to_all | solution.py:476
  90.9 1.0 shard_map.75
  91.9 11.7 %all_to_all.85 = f32[8,64,128]{2,1,0:T(8,128)S(1)} all-to-all(f32[8,64,128]{2,1,0:T(8,128)S(1)} %bitcast.16), channel_id=1, replica_groups=mesh['track'=8,'det'=4] {'track'}, dimensions={0} | all-to-all | bytes 524288 | tf_op jit(solution)/shard_map/all_to_all | solution.py:473
  104.3 0.7 copy-done.10
  105.0 13.4 %all_to_all.86.gathered_ref = f32[32,16,128]{2,1,0:T(8,128)S(1)} all-to-all(f32[32,16,128]{2,1,0:T(8,128)S(1)} %get-tuple-element.55), channel_id=1, replica_groups=mesh['track'=8,'det'=4] {'track','det'}, dimensions={0} | all-to-all | bytes 524288 | tf_op jit(solution)/shard_map/all_to_all | solution.py:476
  118.4 1.6 %shard_map.77 = (f32[8,16,128]{2,1,0:T(8,128)}, f32[8,16,128]{2,1,0:T(8,128)S(1)}, f32[8,128]{1,0:T(8,128)S(1)}, f32[16,128]{1,0:T(8,128)S(1)}, f32[8,128]{1,0:T(8,128)S(1)}, /*index=5*/f32[512,128]{1,0:T(8,128)S(1)}) custom-call(s32[1]{0:T(128)} %bitcast.me_ref, f32[32,16,128]{2,1,0:T(8,128)S(1)} %all_to_all.86.gathered_ref, ...), custom_call_target="tpu_custom_call" | custom-call | tf_op jit(solution)/shard_map/pallas_call | solution.py:539
  120.0 11.7 %all_to_all.87 = f32[8,64,128]{2,1,0:T(8,128)S(1)} all-to-all(f32[8,64,128]{2,1,0:T(8,128)S(1)} %bitcast.22), channel_id=1, replica_groups=mesh['track'=8,'det'=4] {'track'}, dimensions={0} | all-to-all | bytes 524288 | tf_op jit(solution)/shard_map/all_to_all | solution.py:473
  131.7 0.8 shard_map.78
  132.5 3.0 %all-to-all-start.9 = ((f32[32,1,128]{2,1,0:T(1,128)}), f32[32,1,128]{2,1,0:T(1,128)S(1)}, u32[]{:S(2)}, u32[]{:S(2)}) async-start(f32[32,1,128]{2,1,0:T(1,128)} %get-tuple-element.61), calls=%async_computation.9 | async-start | bytes 32768 | tf_op jit(solution)/shard_map/all_to_all | solution.py:476
  135.5 1.0 copy-done.3
  136.5 0.9 copy-done.7
  137.5 0.9 copy-done.9
  138.4 0.9 copy-done.11
  139.4 1.2 shard_map.79
  140.6 2.0 %all-to-all-done.9.squares_ref = f32[32,1,128]{2,1,0:T(1,128)S(1)} async-done(((f32[32,1,128]{2,1,0:T(1,128)}), f32[32,1,128]{2,1,0:T(1,128)S(1)}, u32[]{:S(2)}, u32[]{:S(2)}) %all-to-all-start.9) | async-done | bytes 16416 | tf_op jit(solution)/shard_map/all_to_all | solution.py:476
  142.6 0.9 shard_map.80
  (22 shorter events, 2.7 us)
Async XLA Ops:
  2.9 16.2 %all-to-all-start = ((f32[8,64,128]{2,1,0:T(8,128)}), f32[8,64,128]{2,1,0:T(8,128)S(1)}, u32[]{:S(2)}, u32[]{:S(2)}) async-start(f32[8,64,128]{2,1,0:T(8,128)} %bitcast.5), calls=%async_computation | async-start | bytes 524288 | tf_op jit(solution)/shard_map/all_to_all | solution.py:473
  15.6 0.8 copy-start
  16.4 0.8 copy-start.2
  17.2 0.7 copy-start.12
  19.1 1.0 copy-start.1
  20.2 0.9 copy-start.13
  21.8 0.7 copy-start.4
  50.7 26.8 %copy-start.6 = (f32[512,128]{1,0:T(8,128)}, f32[512,128]{1,0:T(8,128)S(1)}, u32[]{:S(2)}) copy-start(f32[512,128]{1,0:T(8,128)S(1)} %get-tuple-element.71.refs_3_) | copy-start | bytes 786436
  77.5 26.8 %copy-start.8 = (f32[512,128]{1,0:T(8,128)}, f32[512,128]{1,0:T(8,128)S(1)}, u32[]{:S(2)}) copy-start(f32[512,128]{1,0:T(8,128)S(1)} %get-tuple-element.72.refs_4_) | copy-start | bytes 786436
  104.3 0.7 copy-start.10
  105.0 30.5 %copy-start.5 = (f32[512,128]{1,0:T(8,128)S(1)}, f32[512,128]{1,0:T(8,128)}, u32[]{:S(2)}) copy-start(f32[512,128]{1,0:T(8,128)} %copy-done.4) | copy-start | bytes 786436
  132.5 10.2 %all-to-all-start.9 = ((f32[32,1,128]{2,1,0:T(1,128)}), f32[32,1,128]{2,1,0:T(1,128)S(1)}, u32[]{:S(2)}, u32[]{:S(2)}) async-start(f32[32,1,128]{2,1,0:T(1,128)} %get-tuple-element.61), calls=%async_computation.9 | async-start | bytes 32768 | tf_op jit(solution)/shard_map/all_to_all | solution.py:476
  135.5 1.0 copy-start.3
  136.5 0.9 copy-start.7
  137.5 0.9 copy-start.9
  138.4 0.9 copy-start.11

commit v8 on v6

--- a/solution.py
+++ b/solution.py
@@ -125,31 +125,14 @@
     return jnp.where(place == cols, 1.0, 0.0).astype(jnp.bfloat16)
 
 
-def order_kernel(q, me_ref, match_hbm, obs_hbm, obs_out, match_ref, obs_ref, sems):
-    copies = [
-        pltpu.make_async_copy(match_hbm, match_ref, sems.at[0]),
-        pltpu.make_async_copy(obs_hbm, obs_ref, sems.at[1]),
-    ]
-    for copy in copies:
-        copy.start()
-    copies[0].wait()
-    perm = crossing_order(me_ref[0], match_ref[...])
-    copies[1].wait()
-
-    def put(_, index, block):
-        obs_out[index * q : (index + 1) * q, :] = block
-
-    to_crossing([obs_ref[...]], perm, q, put)
-
-
-def jac_kernel(
+def setup_kernel(
     q,
     together,
     me_ref,
     match_hbm,
     knot_hbm,
     frac_hbm,
-    sent_hbm,
+    obs_hbm,
     jac_hbm,
     perm_ref,
     weight_ref,
@@ -159,23 +142,24 @@
     match_ref,
     knot_ref,
     frac_ref,
+    obs_ref,
     jac_ref,
     sems,
 ):
     params, tiles, _ = jac_ref.shape
-    pairs = [(match_hbm, match_ref), (knot_hbm, knot_ref), (frac_hbm, frac_ref)]
+    pairs = [(match_hbm, match_ref), (knot_hbm, knot_ref), (frac_hbm, frac_ref), (obs_hbm, obs_ref)]
     pairs += [(jac_hbm.at[p], jac_ref.at[p]) for p in range(params)]
-    pairs += [(sent_hbm, sent_ref)]
     copies = [
         pltpu.make_async_copy(source, target, sems.at[index])
         for index, (source, target) in enumerate(pairs)
     ]
     for copy in copies:
         copy.start()
-    for copy in copies[:3]:
-        copy.wait()
+    copies[0].wait()
     perm = crossing_order(me_ref[0], match_ref[...])
     perm_ref[...] = perm
+    for copy in copies[1:4]:
+        copy.wait()
 
     row = lax.broadcasted_iota(jnp.int32, (SUB, tiles), 0)
     facts = jnp.where(row == 0, knot_ref[...].astype(jnp.float32), frac_ref[...])
@@ -190,15 +174,18 @@
         weight_ref[index, 0:KNOT_DEV, :] = upper
         weight_ref[index, KNOT_DEV : KNOT_DEV + PAD, :] = lower
 
+    def put_obs(_, index, block):
+        sent_ref[index * q : (index + 1) * q, :] = block
+
+    to_crossing([obs_ref[...]], perm, q, put_obs)
     for first in range(0, params, together):
         for p in range(first, first + together):
-            copies[3 + p].wait()
+            copies[4 + p].wait()
 
         def put(index, block_index, block):
             out_ref[first + index, block_index * q : (block_index + 1) * q, :] = block
 
         to_crossing([jac_ref[p] for p in range(first, first + together)], perm, q, put)
-    copies[3 + params].wait()
 
 
 def weight_dot(x, parts, over_tiles):
@@ -379,12 +366,12 @@
     direction_ref,
     norm_ref,
     knot_ref,
-    grad_out,
     direction_out,
     norm_out,
     knot_out,
     length_out,
     sent_ref,
+    grad_out,
     image_ref,
     interp_ref,
 ):
@@ -471,41 +458,30 @@
     def everywhere(values):
         return lax.all_to_all(values, ("track", "det"), split_axis=0, concat_axis=0, tiled=True)
 
-    match_row = from_hbm(match[None])
-    row_scratch = [pltpu.VMEM((1, tiles), jnp.int32)] * 2 + [pltpu.VMEM((1, tiles), jnp.float32)]
-    sent = call(
-        functools.partial(order_kernel, q),
-        f32(tiles, columns),
-        [SMEM, ANY, ANY],
-        [
-            row_scratch[0],
-            pltpu.VMEM((tiles, columns), jnp.float32),
-            pltpu.SemaphoreType.DMA((2,)),
-        ],
-    )(me, match_row, from_hbm(obs))
-    arrived = crossing(sent)
     perm, weights, edge, sent, jac_rows = call(
-        functools.partial(jac_kernel, q, math.gcd(params, 3)),
+        functools.partial(setup_kernel, q, math.gcd(params, 3)),
         (
-            kept((tiles, tiles), jnp.bfloat16),
+            jax.ShapeDtypeStruct((tiles, tiles), jnp.bfloat16),
             kept((3, KNOT_DEV + PAD, tiles), jnp.bfloat16),
             kept((SUB, tiles)),
-            kept((tiles, columns)),
+            f32(tiles, columns),
             kept((params, tiles, columns)),
         ),
         [SMEM] + [ANY] * 5,
-        row_scratch
-        + [
+        [
+            pltpu.VMEM((1, tiles), jnp.int32),
+            pltpu.VMEM((1, tiles), jnp.int32),
+            pltpu.VMEM((1, tiles), jnp.float32),
+            pltpu.VMEM((tiles, columns), jnp.float32),
             pltpu.VMEM((params, tiles, columns), jnp.float32),
             pltpu.SemaphoreType.DMA((4 + params,)),
         ],
     )(
         me,
-        match_row,
-        from_hbm(tile_knot[None]),
-        from_hbm(tile_frac[None]),
-        from_hbm(sent),
-        from_hbm(jnp.transpose(jac, (1, 0, 2))),
+        *map(
+            from_hbm,
+            (match[None], tile_knot[None], tile_frac[None], obs, jnp.transpose(jac, (1, 0, 2))),
+        ),
     )
 
     def adjoint(sent, arrived):
@@ -520,7 +496,7 @@
     field = f32(n_track, PAD, LANES)
     scalar = f32(SUB, LANES)
     interp = pltpu.VMEM((n_track, PAD, LANES), jnp.float32)
-    misfit, gathered = adjoint(sent, arrived)
+    misfit, gathered = adjoint(sent, crossing(sent))
     gradient, slope_norm, sent = call(
         functools.partial(first_kernel, q, n_det),
         (field, scalar, f32(tiles, columns)),
@@ -532,14 +508,18 @@
     lengths, changes = [], []
     for iteration in range(ITERS - 1):
         change, gathered = adjoint(sent, crossing(sent))
-        gradient, direction, slope_norm, knot_field, length, sent = call(
+        last = iteration == ITERS - 2
+        results = call(
             functools.partial(step_kernel, q, n_det),
-            (field, field, scalar, f32(PAD, KNOT_DEV), scalar, f32(tiles, columns)),
+            (field, scalar, f32(PAD, KNOT_DEV), scalar, f32(tiles, columns))
+            + (() if last else (field,)),
             [SMEM] + [VMEM] * 8,
-            [pltpu.VMEM((n_track, PAD, LANES), jnp.float32), interp],
+            [interp] * (3 if last else 2),
         )(
             me, gathered, jac_rows, weights, edge, gradient, direction, slope_norm, knot_field
         )
+        direction, slope_norm, knot_field, length, sent = results[:5]
+        gradient = None if last else results[5]
         lengths.append(length)
         changes.append(change)
     change, squares = call(

time: 144 us -> 142 us (0.986)
  blocking collectives: 102 us -> 117 us
  local copies, waits for them, and re-layouts: 9.51 us -> 0.01 us
  starting transfers between devices: 10.3 us -> 3 us
  waiting for transfers between devices: 3.22 us -> 5.84 us
  Pallas kernels: 17.5 us -> 15 us
    all_to_all x4 -> x5, blocking collectives: 46.8 us -> 62.8 us  [crossing(): lax.all_to_all(values, 'track', split_axis=0, concat_axis=0, tiled=True)]
    unnamed x28 -> x0, local copies, waits for them, and re-layouts: 9.51 us -> none
    all_to_all x1 -> x0, starting transfers between devices: 7.29 us -> none  [crossing(): lax.all_to_all(values, 'track', split_axis=0, concat_axis=0, tiled=True)]
    all_to_all x1, waiting for transfers between devices: 2 us -> 5.84 us  [everywhere(): lax.all_to_all(values, ('track', 'det'), split_axis=0, concat_axis=0, til...]
    pallas_call x5 -> x4, Pallas kernels: 11.2 us -> 8.64 us  [the longest x1 5.75 us: local(): call(functools.partial(setup_kernel, q, math.gcd(params, 3)), (jax.ShapeD...]
  transfers between devices with their start and end apart: 2 -> 1, of which waited for: 2 -> 1; matrix products, arithmetic and copies ran while one was open for 0% -> 0% of each run, Pallas kernels for 5% -> 1%
where the time goes in v8:
time: 142 us
  blocking collectives  117 us (82%)
  Pallas kernels  15 us (11%)
  waiting for transfers between devices  5.84 us (4%)
  starting transfers between devices  3 us (2%)
    all_to_all x5, blocking collectives, crossing(): lax.all_to_all(values, 'track', split_axis=0, concat_axis=0, tiled=True)  62.8 us
    all_to_all x4, blocking collectives, everywhere(): lax.all_to_all(values, ('track', 'det'), split_axis=0, concat_axis=0, til...  54.2 us
    all_to_all x1, waiting for transfers between devices, everywhere(): lax.all_to_all(values, ('track', 'det'), split_axis=0, concat_axis=0, til...  5.84 us
    pallas_call x1, Pallas kernels, local(): call(functools.partial(setup_kernel, q, math.gcd(params, 3)), (jax.ShapeD...  5.75 us
    all_to_all x1, starting transfers between devices, everywhere(): lax.all_to_all(values, ('track', 'det'), split_axis=0, concat_axis=0, til...  3 us
    pallas_call x3, Pallas kernels, local(): call(functools.partial(step_kernel, q, n_det), (field, scalar, f32(PAD, K...  2.88 us
  transfers between devices with their start and end apart: 1, of which 1 were waited for; matrix products, arithmetic and copies ran while one was open for 0% of the time, Pallas kernels for 1%

profile of v8, /device:TPU:0, one launch (start us, length us, event | category | flops | bytes accessed | tf_op | source)
XLA Modules:
  0.0 141.5 jit_solution(3928356995283368988)
XLA Ops:
  0.6 5.8 %shard_map.68 = (bf16[512,512]{1,0:T(8,128)(2,1)S(1)}, bf16[3,144,512]{2,1,0:T(8,128)(2,1)S(1)}, f32[8,512]{1,0:T(8,128)S(1)}, f32[512,128]{1,0:T(8,128)S(1)}, f32[12,512,128]{2,1,0:T(8,128)S(1)}) custom-call(s32[1]{0:T(128)} %bitcast.me_ref, s32[1,512]{1,0:T(1,128)} %bitcast.26, s32[1,512]{1,0:T(1,128)} %bitcast.27, f32[1,512]{1,0:T(1,128)} %bitcast.28, ...), custom_call_target="tpu_custom_call" | custom-call | tf_op jit(solution)/shard_map/pallas_call | solution.py:461
  6.4 16.0 %all_to_all.80 = f32[8,64,128]{2,1,0:T(8,128)S(1)} all-to-all(f32[8,64,128]{2,1,0:T(8,128)S(1)} %bitcast.17), channel_id=1, replica_groups=mesh['track'=8,'det'=4] {'track'}, dimensions={0} | all-to-all | bytes 524288 | tf_op jit(solution)/shard_map/all_to_all | solution.py:456
  22.4 0.7 shard_map.69
  23.1 14.0 %all_to_all.81.gathered_ref = f32[32,16,128]{2,1,0:T(8,128)S(1)} all-to-all(f32[32,16,128]{2,1,0:T(8,128)S(1)} %get-tuple-element.42), channel_id=1, replica_groups=mesh['track'=8,'det'=4] {'track','det'}, dimensions={0} | all-to-all | bytes 524288 | tf_op jit(solution)/shard_map/all_to_all | solution.py:459
  37.1 0.7 shard_map.70
  37.8 11.7 %all_to_all.82 = f32[8,64,128]{2,1,0:T(8,128)S(1)} all-to-all(f32[8,64,128]{2,1,0:T(8,128)S(1)} %bitcast.18), channel_id=1, replica_groups=mesh['track'=8,'det'=4] {'track'}, dimensions={0} | all-to-all | bytes 524288 | tf_op jit(solution)/shard_map/all_to_all | solution.py:456
  49.5 0.7 shard_map.71
  50.1 13.4 %all_to_all.83.gathered_ref = f32[32,16,128]{2,1,0:T(8,128)S(1)} all-to-all(f32[32,16,128]{2,1,0:T(8,128)S(1)} %get-tuple-element.45), channel_id=1, replica_groups=mesh['track'=8,'det'=4] {'track','det'}, dimensions={0} | all-to-all | bytes 524288 | tf_op jit(solution)/shard_map/all_to_all | solution.py:459
  63.5 1.0 shard_map.72
  64.5 11.7 %all_to_all.84 = f32[8,64,128]{2,1,0:T(8,128)S(1)} all-to-all(f32[8,64,128]{2,1,0:T(8,128)S(1)} %bitcast.16), channel_id=1, replica_groups=mesh['track'=8,'det'=4] {'track'}, dimensions={0} | all-to-all | bytes 524288 | tf_op jit(solution)/shard_map/all_to_all | solution.py:456
  76.2 0.7 shard_map.73
  76.9 13.4 %all_to_all.85.gathered_ref = f32[32,16,128]{2,1,0:T(8,128)S(1)} all-to-all(f32[32,16,128]{2,1,0:T(8,128)S(1)} %get-tuple-element.49), channel_id=1, replica_groups=mesh['track'=8,'det'=4] {'track','det'}, dimensions={0} | all-to-all | bytes 524288 | tf_op jit(solution)/shard_map/all_to_all | solution.py:459
  90.3 1.0 shard_map.74
  91.3 11.7 %all_to_all.86 = f32[8,64,128]{2,1,0:T(8,128)S(1)} all-to-all(f32[8,64,128]{2,1,0:T(8,128)S(1)} %bitcast.15), channel_id=1, replica_groups=mesh['track'=8,'det'=4] {'track'}, dimensions={0} | all-to-all | bytes 524288 | tf_op jit(solution)/shard_map/all_to_all | solution.py:456
  103.0 0.7 shard_map.75
  103.6 13.4 %all_to_all.87.gathered_ref = f32[32,16,128]{2,1,0:T(8,128)S(1)} all-to-all(f32[32,16,128]{2,1,0:T(8,128)S(1)} %get-tuple-element.55), channel_id=1, replica_groups=mesh['track'=8,'det'=4] {'track','det'}, dimensions={0} | all-to-all | bytes 524288 | tf_op jit(solution)/shard_map/all_to_all | solution.py:459
  117.1 0.9 shard_map.76
  118.0 11.7 %all_to_all.88 = f32[8,64,128]{2,1,0:T(8,128)S(1)} all-to-all(f32[8,64,128]{2,1,0:T(8,128)S(1)} %bitcast.23), channel_id=1, replica_groups=mesh['track'=8,'det'=4] {'track'}, dimensions={0} | all-to-all | bytes 524288 | tf_op jit(solution)/shard_map/all_to_all | solution.py:456
  129.7 0.8 shard_map.77
  130.5 3.0 %all-to-all-start.9 = ((f32[32,1,128]{2,1,0:T(1,128)}), f32[32,1,128]{2,1,0:T(1,128)S(1)}, u32[]{:S(2)}, u32[]{:S(2)}) async-start(f32[32,1,128]{2,1,0:T(1,128)} %get-tuple-element.61), calls=%async_computation.9 | async-start | bytes 32768 | tf_op jit(solution)/shard_map/all_to_all | solution.py:459
  133.5 1.2 shard_map.78
  134.7 5.8 %all-to-all-done.9.squares_ref = f32[32,1,128]{2,1,0:T(1,128)S(1)} async-done(((f32[32,1,128]{2,1,0:T(1,128)}), f32[32,1,128]{2,1,0:T(1,128)S(1)}, u32[]{:S(2)}, u32[]{:S(2)}) %all-to-all-start.9) | async-done | bytes 16416 | tf_op jit(solution)/shard_map/all_to_all | solution.py:459
  140.6 0.9 shard_map.79
  (1 shorter events, 0.0 us)
Async XLA Ops:
  130.5 10.1 %all-to-all-start.9 = ((f32[32,1,128]{2,1,0:T(1,128)}), f32[32,1,128]{2,1,0:T(1,128)S(1)}, u32[]{:S(2)}, u32[]{:S(2)}) async-start(f32[32,1,128]{2,1,0:T(1,128)} %get-tuple-element.61), calls=%async_computation.9 | async-start | bytes 32768 | tf_op jit(solution)/shard_map/all_to_all | solution.py:459

commit v9 on v8

--- a/solution.py
+++ b/solution.py
@@ -108,7 +108,7 @@
     return sum(bf16_dot(perm, part) for part in reversed(split3(stacked)))
 
 
-def crossing_order(me, match):
+def crossing_order(me, start, n_track, match):
     tiles = match.shape[1]
     slot = lax.broadcasted_iota(jnp.int32, (1, tiles), 1)
     peer = match // tiles
@@ -118,7 +118,8 @@
         jnp.minimum(slot, other) + jnp.where(slot > other, tiles, 0),
         jnp.where(peer > me, slot, other),
     )
-    key = (peer * (2 * tiles) + inner).astype(jnp.float32)
+    place = jnp.where(peer >= start, peer - start, peer - start + n_track)
+    key = (place * (2 * tiles) + inner).astype(jnp.float32)
     key_cols = jnp.broadcast_to(key, (LANES, tiles)).T[:, :1]
     place = jnp.sum(jnp.where(key < key_cols, 1.0, 0.0), axis=1, keepdims=True)
     cols = lax.broadcasted_iota(jnp.int32, (tiles, tiles), 1).astype(jnp.float32)
@@ -156,7 +157,7 @@
     for copy in copies:
         copy.start()
     copies[0].wait()
-    perm = crossing_order(me_ref[0], match_ref[...])
+    perm = crossing_order(me_ref[0], me_ref[2], tiles // q, match_ref[...])
     perm_ref[...] = perm
     for copy in copies[1:4]:
         copy.wait()
@@ -248,7 +249,7 @@
     q, me_ref, sent_ref, arrived_ref, jac_ref, weight_ref, diff_ref, send_ref, values_ref
 ):
     params, tiles, _ = jac_ref.shape
-    difference(me_ref[0], sent_ref, arrived_ref, diff_ref, q)
+    difference(me_ref[1], sent_ref, arrived_ref, diff_ref, q)
     groups = LANES // q
     group = lane_group((PAD, LANES), q)
     for c in range(tiles // LANES):
@@ -272,14 +273,14 @@
         send_ref[d] = block
 
 
-def field_sums(gathered_ref, n_track, n_det, params, store, base=0):
+def field_sums(gathered_ref, n_track, n_det, params, store):
     lane = lax.broadcasted_iota(jnp.int32, (PAD, LANES), 1)
     row = lax.broadcasted_iota(jnp.int32, (PAD, LANES), 0)
     spill = jnp.zeros((PAD, 1), jnp.float32)
     for b in range(n_track):
-        total = gathered_ref[b * n_det, base : base + PAD, :]
+        total = gathered_ref[b]
         for d in range(1, n_det):
-            total = total + gathered_ref[b * n_det + d, base : base + PAD, :]
+            total = total + gathered_ref[d * n_track + b]
         field = jnp.where(row < params, total, 0.0)
         field = field + jnp.where(lane == 0, spill, 0.0)
         store(b, field)
@@ -397,7 +398,7 @@
 
 
 def last_kernel(q, me_ref, sent_ref, arrived_ref, diff_ref, send_ref):
-    difference(me_ref[0], sent_ref, arrived_ref, diff_ref, q)
+    difference(me_ref[1], sent_ref, arrived_ref, diff_ref, q)
     diff = diff_ref[...]
     squares = jnp.sum(diff * diff, axis=0, keepdims=True)
     send_ref[...] = jnp.broadcast_to(squares[None], send_ref.shape)
@@ -444,19 +445,37 @@
     )
 
 
+def rotation(det, n_track, n_det):
+    return det * (n_track // n_det)
+
+
 def local(jac, obs, match, tile_knot, tile_frac):
     tiles, params, columns = jac.shape
     n_track = lax.axis_size("track")
     n_det = lax.axis_size("det")
     n_all = n_track * n_det
     q = tiles // n_track
-    me = lax.axis_index("track").astype(jnp.int32).reshape(1)
+    me = lax.axis_index("track")
+    start = rotation(lax.axis_index("det"), n_track, n_det)
+    me = jnp.stack([me, lax.rem(me - start + n_track, n_track), start]).astype(jnp.int32)
+
+    groups = [
+        [(place + rotation(d, n_track, n_det)) % n_track * n_det + d for place in range(n_track)]
+        for d in range(n_det)
+    ]
 
     def crossing(values):
-        return lax.all_to_all(values, "track", split_axis=0, concat_axis=0, tiled=True)
+        return lax.all_to_all(
+            values,
+            ("track", "det"),
+            split_axis=0,
+            concat_axis=0,
+            axis_index_groups=groups,
+            tiled=True,
+        )
 
     def everywhere(values):
-        return lax.all_to_all(values, ("track", "det"), split_axis=0, concat_axis=0, tiled=True)
+        return lax.all_to_all(values, ("det", "track"), split_axis=0, concat_axis=0, tiled=True)
 
     perm, weights, edge, sent, jac_rows = call(
         functools.partial(setup_kernel, q, math.gcd(params, 3)),

time: 142 us -> 152 us (1.070)
  Pallas kernels: 15 us -> 20.9 us
  blocking collectives: 117 us -> 119 us
    all_to_all x9, blocking collectives: 117 us -> 119 us  [the longest x5 61.3 us: crossing(): lax.all_to_all(values, ('track', 'det'), split_axis=0, concat_axis=0, axi...]
    pallas_call x4, Pallas kernels: 2.68 us -> 4.84 us  [adjoint(): call(functools.partial(adjoint_kernel, q), (f32(tiles, columns), f32(n_al...]
    pallas_call x3, Pallas kernels: 2.88 us -> 4.5 us  [local(): call(functools.partial(step_kernel, q, n_det), (field, scalar, f32(PAD, K...]
where the time goes in v9:
time: 152 us; the launch traced here: 151 us
  blocking collectives  119 us (78%)
  Pallas kernels  20.9 us (14%)
  waiting for transfers between devices  5.81 us (4%)
  starting transfers between devices  4.25 us (3%)
    all_to_all x5, blocking collectives, crossing(): lax.all_to_all(values, ('track', 'det'), split_axis=0, concat_axis=0, axi...  61.3 us
    all_to_all x4, blocking collectives, everywhere(): lax.all_to_all(values, ('det', 'track'), split_axis=0, concat_axis=0, til...  58.1 us
    pallas_call x1, Pallas kernels, local(): call(functools.partial(setup_kernel, q, math.gcd(params, 3)), (jax.ShapeD...  6.29 us
    all_to_all x1, waiting for transfers between devices, everywhere(): lax.all_to_all(values, ('det', 'track'), split_axis=0, concat_axis=0, til...  5.81 us
    pallas_call x4, Pallas kernels, adjoint(): call(functools.partial(adjoint_kernel, q), (f32(tiles, columns), f32(n_al...  4.84 us
    pallas_call x3, Pallas kernels, local(): call(functools.partial(step_kernel, q, n_det), (field, scalar, f32(PAD, K...  4.5 us
    all_to_all x1, starting transfers between devices, everywhere(): lax.all_to_all(values, ('det', 'track'), split_axis=0, concat_axis=0, til...  4.25 us
  transfers between devices with their start and end apart: 1, of which 1 were waited for; matrix products, arithmetic and copies ran while one was open for 0% of the time, Pallas kernels for 1%

profile of v9, /device:TPU:0, one launch (start us, length us, event | category | flops | bytes accessed | tf_op | source)
XLA Modules:
  0.0 151.1 jit_solution(11512037952263471161)
XLA Ops:
  0.6 0.1 pad_add_fusion.me_ref
  0.7 6.3 %shard_map.68 = (bf16[512,512]{1,0:T(8,128)(2,1)S(1)}, bf16[3,144,512]{2,1,0:T(8,128)(2,1)S(1)}, f32[8,512]{1,0:T(8,128)S(1)}, f32[512,128]{1,0:T(8,128)S(1)}, f32[12,512,128]{2,1,0:T(8,128)S(1)}) custom-call(s32[3]{0:T(128)S(1)} %pad_add_fusion.me_ref, s32[1,512]{1,0:T(1,128)} %bitcast.28, s32[1,512]{1,0:T(1,128)} %bitcast.29, f32[1,512]{1,0:T(1,128)} %bitcast.30, ...), custom_call_target="tpu_custom_call" | custom-call | tf_op jit(solution)/shard_map/pallas_call | solution.py:480
  7.0 15.3 %all_to_all.80 = f32[8,64,128]{2,1,0:T(8,128)S(1)} all-to-all(f32[8,64,128]{2,1,0:T(8,128)S(1)} %bitcast.19), channel_id=1, replica_groups={{0,4,8,12,16,20,24,28},{9,13,17,21,25,29,1,5},{18,22,26,30,2,6,10,14},{..., dimensions={0} | all-to-all | bytes 524288 | tf_op jit(solution)/shard_map/all_to_all | solution.py:468
  22.3 1.2 shard_map.69
  23.5 14.0 %all_to_all.81.gathered_ref = f32[32,16,128]{2,1,0:T(8,128)S(1)} all-to-all(f32[32,16,128]{2,1,0:T(8,128)S(1)} %get-tuple-element.42), channel_id=1, replica_groups=mesh['track'=8,'det'=4] {'det','track'}, dimensions={0} | all-to-all | bytes 524288 | tf_op jit(solution)/shard_map/all_to_all | solution.py:478
  37.5 1.2 shard_map.70
  38.7 11.5 %all_to_all.82 = f32[8,64,128]{2,1,0:T(8,128)S(1)} all-to-all(f32[8,64,128]{2,1,0:T(8,128)S(1)} %bitcast.20), channel_id=1, replica_groups={{0,4,8,12,16,20,24,28},{9,13,17,21,25,29,1,5},{18,22,26,30,2,6,10,14},{..., dimensions={0} | all-to-all | bytes 524288 | tf_op jit(solution)/shard_map/all_to_all | solution.py:468
  50.2 1.2 shard_map.71
  51.4 14.7 %all_to_all.83.gathered_ref = f32[32,16,128]{2,1,0:T(8,128)S(1)} all-to-all(f32[32,16,128]{2,1,0:T(8,128)S(1)} %get-tuple-element.45), channel_id=1, replica_groups=mesh['track'=8,'det'=4] {'det','track'}, dimensions={0} | all-to-all | bytes 524288 | tf_op jit(solution)/shard_map/all_to_all | solution.py:478
  66.1 1.5 shard_map.72
  67.7 11.5 %all_to_all.84 = f32[8,64,128]{2,1,0:T(8,128)S(1)} all-to-all(f32[8,64,128]{2,1,0:T(8,128)S(1)} %bitcast.18), channel_id=1, replica_groups={{0,4,8,12,16,20,24,28},{9,13,17,21,25,29,1,5},{18,22,26,30,2,6,10,14},{..., dimensions={0} | all-to-all | bytes 524288 | tf_op jit(solution)/shard_map/all_to_all | solution.py:468
  79.2 1.2 shard_map.73
  80.4 14.7 %all_to_all.85.gathered_ref = f32[32,16,128]{2,1,0:T(8,128)S(1)} all-to-all(f32[32,16,128]{2,1,0:T(8,128)S(1)} %get-tuple-element.49), channel_id=1, replica_groups=mesh['track'=8,'det'=4] {'det','track'}, dimensions={0} | all-to-all | bytes 524288 | tf_op jit(solution)/shard_map/all_to_all | solution.py:478
  95.1 1.5 shard_map.74
  96.6 11.5 %all_to_all.86 = f32[8,64,128]{2,1,0:T(8,128)S(1)} all-to-all(f32[8,64,128]{2,1,0:T(8,128)S(1)} %bitcast.17), channel_id=1, replica_groups={{0,4,8,12,16,20,24,28},{9,13,17,21,25,29,1,5},{18,22,26,30,2,6,10,14},{..., dimensions={0} | all-to-all | bytes 524288 | tf_op jit(solution)/shard_map/all_to_all | solution.py:468
  108.1 1.2 shard_map.75
  109.3 14.7 %all_to_all.87.gathered_ref = f32[32,16,128]{2,1,0:T(8,128)S(1)} all-to-all(f32[32,16,128]{2,1,0:T(8,128)S(1)} %get-tuple-element.55), channel_id=1, replica_groups=mesh['track'=8,'det'=4] {'det','track'}, dimensions={0} | all-to-all | bytes 524288 | tf_op jit(solution)/shard_map/all_to_all | solution.py:478
  124.0 1.5 shard_map.76
  125.5 11.5 %all_to_all.88 = f32[8,64,128]{2,1,0:T(8,128)S(1)} all-to-all(f32[8,64,128]{2,1,0:T(8,128)S(1)} %bitcast.25), channel_id=1, replica_groups={{0,4,8,12,16,20,24,28},{9,13,17,21,25,29,1,5},{18,22,26,30,2,6,10,14},{..., dimensions={0} | all-to-all | bytes 524288 | tf_op jit(solution)/shard_map/all_to_all | solution.py:468
  137.0 1.3 shard_map.77
  138.4 4.2 %all-to-all-start.9 = ((f32[32,1,128]{2,1,0:T(1,128)}), f32[32,1,128]{2,1,0:T(1,128)S(1)}, u32[]{:S(2)}, u32[]{:S(2)}) async-start(f32[32,1,128]{2,1,0:T(1,128)} %get-tuple-element.61), calls=%async_computation.9 | async-start | bytes 32768 | tf_op jit(solution)/shard_map/all_to_all | solution.py:478
  142.6 1.2 shard_map.78
  143.9 5.8 %all-to-all-done.9.squares_ref = f32[32,1,128]{2,1,0:T(1,128)S(1)} async-done(((f32[32,1,128]{2,1,0:T(1,128)}), f32[32,1,128]{2,1,0:T(1,128)S(1)}, u32[]{:S(2)}, u32[]{:S(2)}) %all-to-all-start.9) | async-done | bytes 16416 | tf_op jit(solution)/shard_map/all_to_all | solution.py:478
  149.7 1.5 shard_map.79
  (1 shorter events, 0.0 us)
Async XLA Ops:
  138.4 11.3 %all-to-all-start.9 = ((f32[32,1,128]{2,1,0:T(1,128)}), f32[32,1,128]{2,1,0:T(1,128)S(1)}, u32[]{:S(2)}, u32[]{:S(2)}) async-start(f32[32,1,128]{2,1,0:T(1,128)} %get-tuple-element.61), calls=%async_computation.9 | async-start | bytes 32768 | tf_op jit(solution)/shard_map/all_to_all | solution.py:478

commit v10 on v6

--- a/solution.py
+++ b/solution.py
@@ -142,7 +142,30 @@
     to_crossing([obs_ref[...]], perm, q, put)
 
 
-def jac_kernel(
+def table_rows(params, tiles):
+    return (params + 1) * tiles + 3 * (tiles // LANES) * (KNOT_DEV + PAD)
+
+
+def table_views(table_ref, params, tiles):
+    return [table_ref.at[p * tiles : (p + 1) * tiles] for p in range(params + 1)]
+
+
+def table_weights(table_ref, params, tiles):
+    height = KNOT_DEV + PAD
+    chunks = tiles // LANES
+    parts = []
+    for index in range(3):
+        first = (params + 1) * tiles + index * chunks * height
+        parts.append(
+            jnp.concatenate(
+                [table_ref[first + c * height : first + (c + 1) * height, :] for c in range(chunks)],
+                axis=1,
+            )
+        )
+    return parts
+
+
+def table_kernel(
     q,
     together,
     me_ref,
@@ -151,11 +174,7 @@
     frac_hbm,
     sent_hbm,
     jac_hbm,
-    perm_ref,
-    weight_ref,
-    edge_ref,
-    sent_ref,
-    out_ref,
+    table_ref,
     match_ref,
     knot_ref,
     frac_ref,
@@ -163,9 +182,10 @@
     sems,
 ):
     params, tiles, _ = jac_ref.shape
+    views = table_views(table_ref, params, tiles)
     pairs = [(match_hbm, match_ref), (knot_hbm, knot_ref), (frac_hbm, frac_ref)]
     pairs += [(jac_hbm.at[p], jac_ref.at[p]) for p in range(params)]
-    pairs += [(sent_hbm, sent_ref)]
+    pairs += [(sent_hbm, views[params])]
     copies = [
         pltpu.make_async_copy(source, target, sems.at[index])
         for index, (source, target) in enumerate(pairs)
@@ -175,8 +195,6 @@
     for copy in copies[:3]:
         copy.wait()
     perm = crossing_order(me_ref[0], match_ref[...])
-    perm_ref[...] = perm
-
     row = lax.broadcasted_iota(jnp.int32, (SUB, tiles), 0)
     facts = jnp.where(row == 0, knot_ref[...].astype(jnp.float32), frac_ref[...])
     moved = sum(bf16_dot(part, perm) for part in reversed(split3(facts)))
@@ -185,17 +203,21 @@
     main = jnp.where(knots == knot, 1.0 - frac, 0.0) + jnp.where(knots == knot + 1.0, frac, 0.0)
     first_row = lax.broadcasted_iota(jnp.int32, (PAD, tiles), 0) == 0
     edge = jnp.where(first_row, jnp.where(knot == KNOT_DEV - 1.0, frac, 0.0), 0.0)
-    edge_ref[...] = edge[0:SUB]
-    for index, (upper, lower) in enumerate(zip(split3(main), split3(edge))):
-        weight_ref[index, 0:KNOT_DEV, :] = upper
-        weight_ref[index, KNOT_DEV : KNOT_DEV + PAD, :] = lower
+    place = (params + 1) * tiles
+    for upper, lower in zip(split3(main), split3(edge)):
+        for c in range(tiles // LANES):
+            lanes = slice(c * LANES, (c + 1) * LANES)
+            table_ref[place : place + KNOT_DEV, :] = upper[:, lanes].astype(jnp.float32)
+            place += KNOT_DEV
+            table_ref[place : place + PAD, :] = lower[:, lanes].astype(jnp.float32)
+            place += PAD
 
     for first in range(0, params, together):
         for p in range(first, first + together):
             copies[3 + p].wait()
 
         def put(index, block_index, block):
-            out_ref[first + index, block_index * q : (block_index + 1) * q, :] = block
+            views[first + index][block_index * q : (block_index + 1) * q, :] = block
 
         to_crossing([jac_ref[p] for p in range(first, first + together)], perm, q, put)
     copies[3 + params].wait()
@@ -257,11 +279,27 @@
     out_ref[...] = sent_ref[...] - out_ref[...]
 
 
+def first_adjoint_kernel(
+    q, params, me_ref, arrived_ref, table_ref, diff_ref, send_ref, values_ref
+):
+    tiles = arrived_ref.shape[0]
+    views = table_views(table_ref, params, tiles)
+    parts = [part.astype(jnp.bfloat16) for part in table_weights(table_ref, params, tiles)]
+    difference(me_ref[0], views[params], arrived_ref, diff_ref, q)
+    adjoint_rows(q, params, diff_ref, views, parts, send_ref, values_ref)
+
+
 def adjoint_kernel(
-    q, me_ref, sent_ref, arrived_ref, jac_ref, weight_ref, diff_ref, send_ref, values_ref
+    q, params, me_ref, sent_ref, arrived_ref, table_ref, weight_ref, diff_ref, send_ref, values_ref
 ):
-    params, tiles, _ = jac_ref.shape
+    views = table_views(table_ref, params, sent_ref.shape[0])
     difference(me_ref[0], sent_ref, arrived_ref, diff_ref, q)
+    parts = [weight_ref[index] for index in range(3)]
+    adjoint_rows(q, params, diff_ref, views, parts, send_ref, values_ref)
+
+
+def adjoint_rows(q, params, diff_ref, views, parts, send_ref, values_ref):
+    tiles = diff_ref.shape[0]
     groups = LANES // q
     group = lane_group((PAD, LANES), q)
     for c in range(tiles // LANES):
@@ -270,11 +308,11 @@
             rows = slice((c * groups + i) * q, (c * groups + i + 1) * q)
             diff = diff_ref[rows, :]
             sums = fold_lanes(
-                row_sums([fold_rows(jac_ref[p, rows, :] * diff) for p in range(params)]), q
+                row_sums([fold_rows(views[p][rows, :] * diff) for p in range(params)]), q
             )
             values = sums if values is None else jnp.where(group == i, sums, values)
         values_ref[:, c * LANES : (c + 1) * LANES] = values
-    spread = weight_dot(values_ref[...], [weight_ref[index] for index in range(3)], True)
+    spread = weight_dot(values_ref[...], parts, True)
     lane = lax.broadcasted_iota(jnp.int32, (PAD, LANES), 1)
     row = lax.broadcasted_iota(jnp.int32, (PAD, LANES), 0)
     spill = jnp.sum(
@@ -314,13 +352,13 @@
     return jnp.sum(total, keepdims=True)
 
 
-def predict(me, q, direction_ref, jac_ref, weight_ref, edge_ref, interp_ref, sent_ref):
-    params, tiles, _ = jac_ref.shape
+def predict(me, q, direction_ref, views, parts, edge, interp_ref, sent_ref):
+    params = len(views) - 1
+    tiles = sent_ref.shape[0]
     n_track = direction_ref.shape[0]
     following = direction_ref[jnp.minimum(me + 1, n_track - 1)][:, 0:1]
     following = jnp.where(me + 1 < n_track, following, 0.0)
-    parts = [weight_ref[index, 0:KNOT_DEV, :] for index in range(3)]
-    interp = weight_dot(direction_ref[me], parts, False) + following * edge_ref[0:1, :]
+    interp = weight_dot(direction_ref[me], parts, False) + following * edge
     groups = LANES // q
     group = lane_group((PAD, LANES), q)
     for c in range(tiles // LANES):
@@ -335,9 +373,9 @@
     def block_values(b, carry):
         rows = pl.ds(pl.multiple_of(b * q, SUB), q)
         interp = interp_ref[b]
-        total = jac_ref[0, rows, :] * interp[0:1]
+        total = views[0][rows, :] * interp[0:1]
         for p in range(1, params):
-            total = total + jac_ref[p, rows, :] * interp[p : p + 1]
+            total = total + views[p][rows, :] * interp[p : p + 1]
         sent_ref[rows, :] = total
         return carry
 
@@ -347,44 +385,55 @@
 def first_kernel(
     q,
     n_det,
+    params,
     me_ref,
     gathered_ref,
-    jac_ref,
-    weight_ref,
-    edge_ref,
+    table_ref,
     grad_ref,
     norm_ref,
     sent_ref,
+    weight_ref,
+    edge_ref,
     interp_ref,
 ):
     n_track = grad_ref.shape[0]
+    tiles = sent_ref.shape[0]
 
     def put(b, field):
         grad_ref[b] = field
 
-    field_sums(gathered_ref, n_track, n_det, jac_ref.shape[0], put)
+    field_sums(gathered_ref, n_track, n_det, params, put)
     norm_ref[...] = jnp.broadcast_to(full_dot(grad_ref, grad_ref), norm_ref.shape)
-    predict(me_ref[0], q, grad_ref, jac_ref, weight_ref, edge_ref, interp_ref, sent_ref)
+    wide = table_weights(table_ref, params, tiles)
+    edge = sum(part[KNOT_DEV : KNOT_DEV + SUB] for part in reversed(wide))
+    edge_ref[...] = edge
+    parts = [part.astype(jnp.bfloat16) for part in wide]
+    for index, part in enumerate(parts):
+        weight_ref[index] = part
+    upper = [part[0:KNOT_DEV] for part in parts]
+    views = table_views(table_ref, params, tiles)
+    predict(me_ref[0], q, grad_ref, views, upper, edge[0:1], interp_ref, sent_ref)
 
 
 def step_kernel(
     q,
     n_det,
+    params,
     me_ref,
     gathered_ref,
-    jac_ref,
+    table_ref,
     weight_ref,
     edge_ref,
     grad_ref,
     direction_ref,
     norm_ref,
     knot_ref,
-    grad_out,
     direction_out,
     norm_out,
     knot_out,
     length_out,
     sent_ref,
+    grad_out,
     image_ref,
     interp_ref,
 ):
@@ -394,7 +443,7 @@
     def put(b, field):
         image_ref[b] = field + damping * direction_ref[b]
 
-    field_sums(gathered_ref, n_track, n_det, jac_ref.shape[0], put)
+    field_sums(gathered_ref, n_track, n_det, params, put)
     norm = norm_ref[0:1, 0:1]
     length = norm / full_dot(direction_ref, image_ref)
     length_out[...] = jnp.broadcast_to(length, length_out.shape)
@@ -406,7 +455,9 @@
     ratio = new_norm / norm
     for b in range(n_track):
         direction_out[b] = grad_out[b] + ratio * direction_ref[b]
-    predict(me, q, direction_out, jac_ref, weight_ref, edge_ref, interp_ref, sent_ref)
+    views = table_views(table_ref, params, sent_ref.shape[0])
+    parts = [weight_ref[index, 0:KNOT_DEV, :] for index in range(3)]
+    predict(me, q, direction_out, views, parts, edge_ref[0:1, :], interp_ref, sent_ref)
 
 
 def last_kernel(q, me_ref, sent_ref, arrived_ref, diff_ref, send_ref):
@@ -416,17 +467,21 @@
     send_ref[...] = jnp.broadcast_to(squares[None], send_ref.shape)
 
 
-def restore_kernel(q, perm_ref, misfit_ref, diff_ref, *refs):
-    steps = (len(refs) - 3) // 2
-    residual_out, diff_out, residual_ref = refs[2 * steps :]
+def restore_kernel(q, me_ref, match_hbm, misfit_ref, diff_ref, *refs):
+    steps = (len(refs) - 5) // 2
+    residual_out, diff_out, residual_ref, match_ref, sem = refs[2 * steps :]
     tiles = misfit_ref.shape[0]
+    copy = pltpu.make_async_copy(match_hbm, match_ref, sem)
+    copy.start()
+    copy.wait()
+    perm = crossing_order(me_ref[0], match_ref[...])
     residual = misfit_ref[...]
     for length_ref, change_ref in zip(refs[:steps], refs[steps : 2 * steps]):
         residual = residual - length_ref[0:1, 0:1] * change_ref[...]
     residual_ref[...] = residual
     for source, target in ((residual_ref, residual_out), (diff_ref, diff_out)):
         target[...] = from_crossing(
-            lambda index: source[index * q : (index + 1) * q, :], perm_ref[...], q, tiles
+            lambda index: source[index * q : (index + 1) * q, :], perm, q, tiles
         )
 
 
@@ -472,74 +527,71 @@
         return lax.all_to_all(values, ("track", "det"), split_axis=0, concat_axis=0, tiled=True)
 
     match_row = from_hbm(match[None])
-    row_scratch = [pltpu.VMEM((1, tiles), jnp.int32)] * 2 + [pltpu.VMEM((1, tiles), jnp.float32)]
+    int_row = pltpu.VMEM((1, tiles), jnp.int32)
     sent = call(
         functools.partial(order_kernel, q),
         f32(tiles, columns),
         [SMEM, ANY, ANY],
-        [
-            row_scratch[0],
-            pltpu.VMEM((tiles, columns), jnp.float32),
-            pltpu.SemaphoreType.DMA((2,)),
-        ],
+        [int_row, pltpu.VMEM((tiles, columns), jnp.float32), pltpu.SemaphoreType.DMA((2,))],
     )(me, match_row, from_hbm(obs))
     arrived = crossing(sent)
-    perm, weights, edge, sent, jac_rows = call(
-        functools.partial(jac_kernel, q, math.gcd(params, 3)),
-        (
-            kept((tiles, tiles), jnp.bfloat16),
-            kept((3, KNOT_DEV + PAD, tiles), jnp.bfloat16),
-            kept((SUB, tiles)),
-            kept((tiles, columns)),
-            kept((params, tiles, columns)),
-        ),
+    table = call(
+        functools.partial(table_kernel, q, math.gcd(params, 3)),
+        kept((table_rows(params, tiles), columns)),
         [SMEM] + [ANY] * 5,
-        row_scratch
-        + [
+        [
+            int_row,
+            int_row,
+            pltpu.VMEM((1, tiles), jnp.float32),
             pltpu.VMEM((params, tiles, columns), jnp.float32),
             pltpu.SemaphoreType.DMA((4 + params,)),
         ],
     )(
         me,
         match_row,
-        from_hbm(tile_knot[None]),
-        from_hbm(tile_frac[None]),
-        from_hbm(sent),
-        from_hbm(jnp.transpose(jac, (1, 0, 2))),
+        *map(from_hbm, (tile_knot[None], tile_frac[None], sent, jnp.transpose(jac, (1, 0, 2)))),
     )
-
-    def adjoint(sent, arrived):
-        diff, payload = call(
-            functools.partial(adjoint_kernel, q),
-            (f32(tiles, columns), f32(n_all, PAD, LANES)),
-            [SMEM] + [VMEM] * 4,
-            [pltpu.VMEM((PAD, tiles), jnp.float32)],
-        )(me, sent, arrived, jac_rows, weights)
-        return diff, everywhere(payload)
 
     field = f32(n_track, PAD, LANES)
     scalar = f32(SUB, LANES)
     interp = pltpu.VMEM((n_track, PAD, LANES), jnp.float32)
-    misfit, gathered = adjoint(sent, arrived)
-    gradient, slope_norm, sent = call(
-        functools.partial(first_kernel, q, n_det),
-        (field, scalar, f32(tiles, columns)),
-        [SMEM] + [VMEM] * 4,
+    adjoint_out = (f32(tiles, columns), f32(n_all, PAD, LANES))
+    values = [pltpu.VMEM((PAD, tiles), jnp.float32)]
+    misfit, payload = call(
+        functools.partial(first_adjoint_kernel, q, params), adjoint_out, [SMEM] + [VMEM] * 2, values
+    )(me, arrived, table)
+    gradient, slope_norm, sent, weights, edge = call(
+        functools.partial(first_kernel, q, n_det, params),
+        (
+            field,
+            scalar,
+            f32(tiles, columns),
+            jax.ShapeDtypeStruct((3, KNOT_DEV + PAD, tiles), jnp.bfloat16),
+            f32(SUB, tiles),
+        ),
+        [SMEM] + [VMEM] * 2,
         [interp],
-    )(me, gathered, jac_rows, weights, edge)
+    )(me, everywhere(payload), table)
     direction = gradient
     knot_field = jnp.zeros((PAD, KNOT_DEV), jnp.float32)
     lengths, changes = [], []
     for iteration in range(ITERS - 1):
-        change, gathered = adjoint(sent, crossing(sent))
-        gradient, direction, slope_norm, knot_field, length, sent = call(
-            functools.partial(step_kernel, q, n_det),
-            (field, field, scalar, f32(PAD, KNOT_DEV), scalar, f32(tiles, columns)),
+        change, payload = call(
+            functools.partial(adjoint_kernel, q, params), adjoint_out, [SMEM] + [VMEM] * 4, values
+        )(me, sent, crossing(sent), table, weights)
+        gathered = everywhere(payload)
+        last = iteration == ITERS - 2
+        results = call(
+            functools.partial(step_kernel, q, n_det, params),
+            (field, scalar, f32(PAD, KNOT_DEV), scalar, f32(tiles, columns))
+            + (() if last else (field,)),
             [SMEM] + [VMEM] * 8,
-            [pltpu.VMEM((n_track, PAD, LANES), jnp.float32), interp],
+            [interp] * (3 if last else 2),
         )(
-            me, gathered, jac_rows, weights, edge, gradient, direction, slope_norm, knot_field
+            me, gathered, table, weights, edge, gradient, direction, slope_norm, knot_field
         )
+        direction, slope_norm, knot_field, length, sent = results[:5]
+        gradient = None if last else results[5]
         lengths.append(length)
         changes.append(change)
     change, squares = call(
@@ -551,9 +603,9 @@
     residual, change = call(
         functools.partial(restore_kernel, q),
         (f32(tiles, columns), f32(tiles, columns)),
-        [VMEM] * (3 + 2 * len(changes)),
-        [pltpu.VMEM((tiles, columns), jnp.float32)],
-    )(perm, misfit, change, *lengths, *changes)
+        [SMEM, ANY] + [VMEM] * (2 + 2 * len(changes)),
+        [pltpu.VMEM((tiles, columns), jnp.float32), int_row, pltpu.SemaphoreType.DMA],
+    )(me, match_row, misfit, change, *lengths, *changes)
     return call(
         finish_kernel,
         (f32(params, KNOT_DEV), f32(tiles, columns)),

time: 144 us -> 142 us (0.986)
  local copies, waits for them, and re-layouts: 9.51 us -> 4.18 us
  waiting for transfers between devices: 3.22 us -> 5.7 us
    unnamed x28 -> x4, local copies, waits for them, and re-layouts: 9.51 us -> 4.18 us
    all_to_all x1, waiting for transfers between devices: 2 us -> 4.15 us  [everywhere(): lax.all_to_all(values, ('track', 'det'), split_axis=0, concat_axis=0, til...]
    pallas_call x1, Pallas kernels: 1.24 us -> 2.92 us  [local(): call(functools.partial(restore_kernel, q), (f32(tiles, columns), f32(tile...]
  transfers between devices with their start and end apart: 2 -> 2, of which waited for: 2 -> 2; matrix products, arithmetic and copies ran while one was open for 0% -> 0% of each run, Pallas kernels for 5% -> 6%
where the time goes in v10:
time: 142 us; the launch traced here: 141 us
  blocking collectives  102 us (72%)
  Pallas kernels  18.5 us (13%)
  starting transfers between devices  10.3 us (7%)
  waiting for transfers between devices  5.7 us (4%)
  local copies, waits for them, and re-layouts  4.18 us (3%)
    all_to_all x4, blocking collectives, everywhere(): lax.all_to_all(values, ('track', 'det'), split_axis=0, concat_axis=0, til...  55.1 us
    all_to_all x4, blocking collectives, crossing(): lax.all_to_all(values, 'track', split_axis=0, concat_axis=0, tiled=True)  46.8 us
    all_to_all x1, starting transfers between devices, crossing(): lax.all_to_all(values, 'track', split_axis=0, concat_axis=0, tiled=True)  7.29 us
    pallas_call x1, Pallas kernels, local(): call(functools.partial(table_kernel, q, math.gcd(params, 3)), kept((table...  5.39 us
    unnamed x4, local copies, waits for them, and re-layouts  4.18 us
    all_to_all x1, waiting for transfers between devices, everywhere(): lax.all_to_all(values, ('track', 'det'), split_axis=0, concat_axis=0, til...  4.15 us
    all_to_all x1, starting transfers between devices, everywhere(): lax.all_to_all(values, ('track', 'det'), split_axis=0, concat_axis=0, til...  3 us
    pallas_call x1, Pallas kernels, local(): call(functools.partial(restore_kernel, q), (f32(tiles, columns), f32(tile...  2.92 us
  transfers between devices with their start and end apart: 2, of which 2 were waited for; matrix products, arithmetic and copies ran while one was open for 0% of the time, Pallas kernels for 6%

profile of v10, /device:TPU:0, one launch (start us, length us, event | category | flops | bytes accessed | tf_op | source)
XLA Modules:
  0.0 141.3 jit_solution(2806729108915209220)
XLA Ops:
  0.6 2.3 %shard_map.68.sent_hbm = f32[512,128]{1,0:T(8,128)} custom-call(s32[1]{0:T(128)} %bitcast.me_ref, s32[1,512]{1,0:T(1,128)} %bitcast.25, f32[512,128]{1,0:T(8,128)} %obs_hbm.1), custom_call_target="tpu_custom_call" | custom-call | tf_op jit(solution)/shard_map/pallas_call | solution.py:531
  2.9 7.3 %all-to-all-start = ((f32[8,64,128]{2,1,0:T(8,128)}), f32[8,64,128]{2,1,0:T(8,128)S(1)}, u32[]{:S(2)}, u32[]{:S(2)}) async-start(f32[8,64,128]{2,1,0:T(8,128)} %bitcast.2), calls=%async_computation | async-start | bytes 524288 | tf_op jit(solution)/shard_map/all_to_all | solution.py:524
  10.2 5.4 %shard_map.69.table_ref = f32[8384,128]{1,0:T(8,128)S(1)} custom-call(s32[1]{0:T(128)} %bitcast.me_ref, s32[1,512]{1,0:T(1,128)} %bitcast.26, s32[1,512]{1,0:T(1,128)} %bitcast.28, f32[1,512]{1,0:T(1,128)} %bitcast.29, f32[512,128]{1,0:T(8,128)} %shard_map.68.sent_hbm, f32[12,512,128]{2,1,0:T(8,128)} %bitcast.24), custom_call_target="tpu_custom_call" | custom-call | tf_op jit(solution)/shard_map/pallas_call | solution.py:538
  15.6 0.0 copy-start
  15.6 2.0 %copy-done = f32[8384,128]{1,0:T(8,128)} copy-done((f32[8384,128]{1,0:T(8,128)}, f32[8384,128]{1,0:T(8,128)S(1)}, u32[]{:S(2)}) %copy-start) | copy-done | bytes 4292632
  17.6 1.6 %all-to-all-done = f32[8,64,128]{2,1,0:T(8,128)S(1)} async-done(((f32[8,64,128]{2,1,0:T(8,128)}), f32[8,64,128]{2,1,0:T(8,128)S(1)}, u32[]{:S(2)}, u32[]{:S(2)}) %all-to-all-start) | async-done | bytes 262176 | tf_op jit(solution)/shard_map/all_to_all | solution.py:524
  19.1 0.0 copy-start.1
  19.1 2.2 %copy-done.1 = f32[8384,128]{1,0:T(8,128)S(1)} copy-done((f32[8384,128]{1,0:T(8,128)S(1)}, f32[8384,128]{1,0:T(8,128)}, u32[]{:S(2)}) %copy-start.1) | copy-done | bytes 4292632
  21.4 0.7 shard_map.70
  22.0 14.9 %all_to_all.80.gathered_ref = f32[32,16,128]{2,1,0:T(8,128)S(1)} all-to-all(f32[32,16,128]{2,1,0:T(8,128)S(1)} %get-tuple-element.36), channel_id=1, replica_groups=mesh['track'=8,'det'=4] {'track','det'}, dimensions={0} | all-to-all | bytes 524288 | tf_op jit(solution)/shard_map/all_to_all | solution.py:527
  36.9 0.7 shard_map.71
  37.6 11.7 %all_to_all.81 = f32[8,64,128]{2,1,0:T(8,128)S(1)} all-to-all(f32[8,64,128]{2,1,0:T(8,128)S(1)} %bitcast.20), channel_id=1, replica_groups=mesh['track'=8,'det'=4] {'track'}, dimensions={0} | all-to-all | bytes 524288 | tf_op jit(solution)/shard_map/all_to_all | solution.py:524
  49.2 0.7 shard_map.72
  49.9 13.4 %all_to_all.82.gathered_ref = f32[32,16,128]{2,1,0:T(8,128)S(1)} all-to-all(f32[32,16,128]{2,1,0:T(8,128)S(1)} %get-tuple-element.39), channel_id=1, replica_groups=mesh['track'=8,'det'=4] {'track','det'}, dimensions={0} | all-to-all | bytes 524288 | tf_op jit(solution)/shard_map/all_to_all | solution.py:527
  63.3 1.0 shard_map.73
  64.3 11.7 %all_to_all.83 = f32[8,64,128]{2,1,0:T(8,128)S(1)} all-to-all(f32[8,64,128]{2,1,0:T(8,128)S(1)} %bitcast.19), channel_id=1, replica_groups=mesh['track'=8,'det'=4] {'track'}, dimensions={0} | all-to-all | bytes 524288 | tf_op jit(solution)/shard_map/all_to_all | solution.py:524
  76.0 0.7 shard_map.74
  76.7 13.4 %all_to_all.84.gathered_ref = f32[32,16,128]{2,1,0:T(8,128)S(1)} all-to-all(f32[32,16,128]{2,1,0:T(8,128)S(1)} %get-tuple-element.44), channel_id=1, replica_groups=mesh['track'=8,'det'=4] {'track','det'}, dimensions={0} | all-to-all | bytes 524288 | tf_op jit(solution)/shard_map/all_to_all | solution.py:527
  90.1 1.0 shard_map.75
  91.1 11.7 %all_to_all.85 = f32[8,64,128]{2,1,0:T(8,128)S(1)} all-to-all(f32[8,64,128]{2,1,0:T(8,128)S(1)} %bitcast.18), channel_id=1, replica_groups=mesh['track'=8,'det'=4] {'track'}, dimensions={0} | all-to-all | bytes 524288 | tf_op jit(solution)/shard_map/all_to_all | solution.py:524
  102.8 0.7 shard_map.76
  103.4 13.4 %all_to_all.86.gathered_ref = f32[32,16,128]{2,1,0:T(8,128)S(1)} all-to-all(f32[32,16,128]{2,1,0:T(8,128)S(1)} %get-tuple-element.50), channel_id=1, replica_groups=mesh['track'=8,'det'=4] {'track','det'}, dimensions={0} | all-to-all | bytes 524288 | tf_op jit(solution)/shard_map/all_to_all | solution.py:527
  116.8 0.9 shard_map.77
  117.8 11.7 %all_to_all.87 = f32[8,64,128]{2,1,0:T(8,128)S(1)} all-to-all(f32[8,64,128]{2,1,0:T(8,128)S(1)} %bitcast.16), channel_id=1, replica_groups=mesh['track'=8,'det'=4] {'track'}, dimensions={0} | all-to-all | bytes 524288 | tf_op jit(solution)/shard_map/all_to_all | solution.py:524
  129.5 0.8 shard_map.78
  130.3 3.0 %all-to-all-start.9 = ((f32[32,1,128]{2,1,0:T(1,128)}), f32[32,1,128]{2,1,0:T(1,128)S(1)}, u32[]{:S(2)}, u32[]{:S(2)}) async-start(f32[32,1,128]{2,1,0:T(1,128)} %get-tuple-element.56), calls=%async_computation.9 | async-start | bytes 32768 | tf_op jit(solution)/shard_map/all_to_all | solution.py:527
  133.3 2.9 %shard_map.79 = (f32[512,128]{1,0:T(8,128)S(1)}, f32[512,128]{1,0:T(8,128)S(1)}) custom-call(s32[1]{0:T(128)} %bitcast.me_ref, s32[1,512]{1,0:T(1,128)} %bitcast.27, f32[512,128]{1,0:T(8,128)S(1)} %get-tuple-element.60.misfit_ref, f32[512,128]{1,0:T(8,128)S(1)} %get-tuple-element.61.diff_ref, f32[8,128]{1,0:T(8,128)S(1)} %get-tuple-element.62.refs_0_, ...), custom_call_target="tpu_custom_call" | custom-call | tf_op jit(solution)/shard_map/pallas_call | solution.py:603
  136.2 4.1 %all-to-all-done.9.squares_ref = f32[32,1,128]{2,1,0:T(1,128)S(1)} async-done(((f32[32,1,128]{2,1,0:T(1,128)}), f32[32,1,128]{2,1,0:T(1,128)S(1)}, u32[]{:S(2)}, u32[]{:S(2)}) %all-to-all-start.9) | async-done | bytes 16416 | tf_op jit(solution)/shard_map/all_to_all | solution.py:527
  140.4 0.9 shard_map.80
  (1 shorter events, 0.0 us)
Async XLA Ops:
  2.9 16.2 %all-to-all-start = ((f32[8,64,128]{2,1,0:T(8,128)}), f32[8,64,128]{2,1,0:T(8,128)S(1)}, u32[]{:S(2)}, u32[]{:S(2)}) async-start(f32[8,64,128]{2,1,0:T(8,128)} %bitcast.2), calls=%async_computation | async-start | bytes 524288 | tf_op jit(solution)/shard_map/all_to_all | solution.py:524
  15.6 2.0 %copy-start = (f32[8384,128]{1,0:T(8,128)}, f32[8384,128]{1,0:T(8,128)S(1)}, u32[]{:S(2)}) copy-start(f32[8384,128]{1,0:T(8,128)S(1)} %shard_map.69.table_ref) | copy-start | bytes 12877828
  19.1 2.2 %copy-start.1 = (f32[8384,128]{1,0:T(8,128)S(1)}, f32[8384,128]{1,0:T(8,128)}, u32[]{:S(2)}) copy-start(f32[8384,128]{1,0:T(8,128)} %copy-done) | copy-start | bytes 12877828
  130.3 10.1 %all-to-all-start.9 = ((f32[32,1,128]{2,1,0:T(1,128)}), f32[32,1,128]{2,1,0:T(1,128)S(1)}, u32[]{:S(2)}, u32[]{:S(2)}) async-start(f32[32,1,128]{2,1,0:T(1,128)} %get-tuple-element.56), calls=%async_computation.9 | async-start | bytes 32768 | tf_op jit(solution)/shard_map/all_to_all | solution.py:527

commit v11 on v10

--- a/solution.py
+++ b/solution.py
@@ -13,7 +13,7 @@
 LANES = 128
 SUB = 8
 PAD = 16
-VMEM_BYTES = 14 * 2**20
+VMEM_BYTES = 6 * 2**20
 
 
 damping = 1.0
@@ -178,13 +178,12 @@
     match_ref,
     knot_ref,
     frac_ref,
-    jac_ref,
     sems,
 ):
-    params, tiles, _ = jac_ref.shape
+    params, tiles, _ = jac_hbm.shape
     views = table_views(table_ref, params, tiles)
     pairs = [(match_hbm, match_ref), (knot_hbm, knot_ref), (frac_hbm, frac_ref)]
-    pairs += [(jac_hbm.at[p], jac_ref.at[p]) for p in range(params)]
+    pairs += [(jac_hbm.at[p], views[p]) for p in range(params)]
     pairs += [(sent_hbm, views[params])]
     copies = [
         pltpu.make_async_copy(source, target, sems.at[index])
@@ -219,7 +218,7 @@
         def put(index, block_index, block):
             views[first + index][block_index * q : (block_index + 1) * q, :] = block
 
-        to_crossing([jac_ref[p] for p in range(first, first + together)], perm, q, put)
+        to_crossing([views[p][...] for p in range(first, first + together)], perm, q, put)
     copies[3 + params].wait()
 
 
@@ -543,7 +542,6 @@
             int_row,
             int_row,
             pltpu.VMEM((1, tiles), jnp.float32),
-            pltpu.VMEM((params, tiles, columns), jnp.float32),
             pltpu.SemaphoreType.DMA((4 + params,)),
         ],
     )(

time: 142 us -> 142 us (level)
    unnamed x4 -> x8, local copies, waits for them, and re-layouts: 4.18 us -> 4.19 us
where the time goes in v11:
time: 142 us; the launch traced here: 141 us
  blocking collectives  102 us (72%)
  Pallas kernels  18.6 us (13%)
  starting transfers between devices  10.3 us (7%)
  waiting for transfers between devices  5.67 us (4%)
  local copies, waits for them, and re-layouts  4.19 us (3%)
    all_to_all x4, blocking collectives, everywhere(): lax.all_to_all(values, ('track', 'det'), split_axis=0, concat_axis=0, til...  55.1 us
    all_to_all x4, blocking collectives, crossing(): lax.all_to_all(values, 'track', split_axis=0, concat_axis=0, tiled=True)  46.8 us
    all_to_all x1, starting transfers between devices, crossing(): lax.all_to_all(values, 'track', split_axis=0, concat_axis=0, tiled=True)  7.29 us
    pallas_call x1, Pallas kernels, local(): call(functools.partial(table_kernel, q, math.gcd(params, 3)), kept((table...  5.42 us
    unnamed x8, local copies, waits for them, and re-layouts  4.19 us
    all_to_all x1, waiting for transfers between devices, everywhere(): lax.all_to_all(values, ('track', 'det'), split_axis=0, concat_axis=0, til...  4.15 us
    all_to_all x1, starting transfers between devices, everywhere(): lax.all_to_all(values, ('track', 'det'), split_axis=0, concat_axis=0, til...  3 us
    pallas_call x1, Pallas kernels, local(): call(functools.partial(restore_kernel, q), (f32(tiles, columns), f32(tile...  2.92 us
  transfers between devices with their start and end apart: 2, of which 2 were waited for; matrix products, arithmetic and copies ran while one was open for 0% of the time, Pallas kernels for 6%

profile of v11, /device:TPU:0, one launch (start us, length us, event | category | flops | bytes accessed | tf_op | source)
XLA Modules:
  0.0 141.4 jit_solution(617021279917091303)
XLA Ops:
  0.6 2.3 %shard_map.68.sent_hbm = f32[512,128]{1,0:T(8,128)} custom-call(s32[1]{0:T(128)} %bitcast.me_ref, s32[1,512]{1,0:T(1,128)} %bitcast.27, f32[512,128]{1,0:T(8,128)} %obs_hbm.1), custom_call_target="tpu_custom_call" | custom-call | tf_op jit(solution)/shard_map/pallas_call | solution.py:530
  2.9 7.3 %all-to-all-start = ((f32[8,64,128]{2,1,0:T(8,128)}), f32[8,64,128]{2,1,0:T(8,128)S(1)}, u32[]{:S(2)}, u32[]{:S(2)}) async-start(f32[8,64,128]{2,1,0:T(8,128)} %bitcast.2), calls=%async_computation | async-start | bytes 524288 | tf_op jit(solution)/shard_map/all_to_all | solution.py:523
  10.2 5.4 %shard_map.69.table_ref = f32[8384,128]{1,0:T(8,128)S(1)} custom-call(s32[1]{0:T(128)} %bitcast.me_ref, s32[1,512]{1,0:T(1,128)} %bitcast.28, s32[1,512]{1,0:T(1,128)} %bitcast.30, f32[1,512]{1,0:T(1,128)} %bitcast.31, f32[512,128]{1,0:T(8,128)} %shard_map.68.sent_hbm, f32[12,512,128]{2,1,0:T(8,128)} %bitcast.26), custom_call_target="tpu_custom_call" | custom-call | tf_op jit(solution)/shard_map/pallas_call | solution.py:537
  15.6 0.0 copy-start
  15.7 2.0 %copy-done = f32[8384,128]{1,0:T(8,128)} copy-done((f32[8384,128]{1,0:T(8,128)}, f32[8384,128]{1,0:T(8,128)S(1)}, u32[]{:S(2)}) %copy-start) | copy-done | bytes 4292632
  17.6 1.5 %all-to-all-done = f32[8,64,128]{2,1,0:T(8,128)S(1)} async-done(((f32[8,64,128]{2,1,0:T(8,128)}), f32[8,64,128]{2,1,0:T(8,128)S(1)}, u32[]{:S(2)}, u32[]{:S(2)}) %all-to-all-start) | async-done | bytes 262176 | tf_op jit(solution)/shard_map/all_to_all | solution.py:523
  19.1 0.0 copy-start.1
  19.1 2.2 %copy-done.1 = f32[8384,128]{1,0:T(8,128)S(1)} copy-done((f32[8384,128]{1,0:T(8,128)S(1)}, f32[8384,128]{1,0:T(8,128)}, u32[]{:S(2)}) %copy-start.1) | copy-done | bytes 4292632
  21.4 0.0 slice-start
  21.4 0.7 shard_map.70
  22.0 14.9 %all_to_all.80.gathered_ref = f32[32,16,128]{2,1,0:T(8,128)S(1)} all-to-all(f32[32,16,128]{2,1,0:T(8,128)S(1)} %get-tuple-element.36), channel_id=1, replica_groups=mesh['track'=8,'det'=4] {'track','det'}, dimensions={0} | all-to-all | bytes 524288 | tf_op jit(solution)/shard_map/all_to_all | solution.py:526
  36.9 0.7 shard_map.71
  37.6 11.7 %all_to_all.81 = f32[8,64,128]{2,1,0:T(8,128)S(1)} all-to-all(f32[8,64,128]{2,1,0:T(8,128)S(1)} %bitcast.22), channel_id=1, replica_groups=mesh['track'=8,'det'=4] {'track'}, dimensions={0} | all-to-all | bytes 524288 | tf_op jit(solution)/shard_map/all_to_all | solution.py:523
  49.3 0.7 shard_map.72
  50.0 13.4 %all_to_all.82.gathered_ref = f32[32,16,128]{2,1,0:T(8,128)S(1)} all-to-all(f32[32,16,128]{2,1,0:T(8,128)S(1)} %get-tuple-element.39), channel_id=1, replica_groups=mesh['track'=8,'det'=4] {'track','det'}, dimensions={0} | all-to-all | bytes 524288 | tf_op jit(solution)/shard_map/all_to_all | solution.py:526
  63.4 0.0 slice-done
  63.4 0.0 slice-done.1
  63.4 1.0 shard_map.73
  64.4 11.7 %all_to_all.83 = f32[8,64,128]{2,1,0:T(8,128)S(1)} all-to-all(f32[8,64,128]{2,1,0:T(8,128)S(1)} %bitcast.21), channel_id=1, replica_groups=mesh['track'=8,'det'=4] {'track'}, dimensions={0} | all-to-all | bytes 524288 | tf_op jit(solution)/shard_map/all_to_all | solution.py:523
  76.1 0.7 shard_map.74
  76.7 13.4 %all_to_all.84.gathered_ref = f32[32,16,128]{2,1,0:T(8,128)S(1)} all-to-all(f32[32,16,128]{2,1,0:T(8,128)S(1)} %get-tuple-element.44), channel_id=1, replica_groups=mesh['track'=8,'det'=4] {'track','det'}, dimensions={0} | all-to-all | bytes 524288 | tf_op jit(solution)/shard_map/all_to_all | solution.py:526
  90.2 1.0 shard_map.75
  91.1 11.7 %all_to_all.85 = f32[8,64,128]{2,1,0:T(8,128)S(1)} all-to-all(f32[8,64,128]{2,1,0:T(8,128)S(1)} %bitcast.20), channel_id=1, replica_groups=mesh['track'=8,'det'=4] {'track'}, dimensions={0} | all-to-all | bytes 524288 | tf_op jit(solution)/shard_map/all_to_all | solution.py:523
  102.8 0.7 shard_map.76
  103.5 13.4 %all_to_all.86.gathered_ref = f32[32,16,128]{2,1,0:T(8,128)S(1)} all-to-all(f32[32,16,128]{2,1,0:T(8,128)S(1)} %get-tuple-element.50), channel_id=1, replica_groups=mesh['track'=8,'det'=4] {'track','det'}, dimensions={0} | all-to-all | bytes 524288 | tf_op jit(solution)/shard_map/all_to_all | solution.py:526
  116.9 0.9 shard_map.77
  117.9 11.7 %all_to_all.87 = f32[8,64,128]{2,1,0:T(8,128)S(1)} all-to-all(f32[8,64,128]{2,1,0:T(8,128)S(1)} %bitcast.18), channel_id=1, replica_groups=mesh['track'=8,'det'=4] {'track'}, dimensions={0} | all-to-all | bytes 524288 | tf_op jit(solution)/shard_map/all_to_all | solution.py:523
  129.6 0.8 shard_map.78
  130.4 3.0 %all-to-all-start.9 = ((f32[32,1,128]{2,1,0:T(1,128)}), f32[32,1,128]{2,1,0:T(1,128)S(1)}, u32[]{:S(2)}, u32[]{:S(2)}) async-start(f32[32,1,128]{2,1,0:T(1,128)} %get-tuple-element.56), calls=%async_computation.9 | async-start | bytes 32768 | tf_op jit(solution)/shard_map/all_to_all | solution.py:526
  133.4 2.9 %shard_map.79 = (f32[512,128]{1,0:T(8,128)S(1)}, f32[512,128]{1,0:T(8,128)S(1)}) custom-call(s32[1]{0:T(128)} %bitcast.me_ref, s32[1,512]{1,0:T(1,128)} %bitcast.29, f32[512,128]{1,0:T(8,128)S(1)} %get-tuple-element.60.misfit_ref, f32[512,128]{1,0:T(8,128)S(1)} %get-tuple-element.61.diff_ref, f32[8,128]{1,0:T(8,128)S(1)} %get-tuple-element.62.refs_0_, ...), custom_call_target="tpu_custom_call" | custom-call | tf_op jit(solution)/shard_map/pallas_call | solution.py:601
  136.3 4.1 %all-to-all-done.9.squares_ref = f32[32,1,128]{2,1,0:T(1,128)S(1)} async-done(((f32[32,1,128]{2,1,0:T(1,128)}), f32[32,1,128]{2,1,0:T(1,128)S(1)}, u32[]{:S(2)}, u32[]{:S(2)}) %all-to-all-start.9) | async-done | bytes 16416 | tf_op jit(solution)/shard_map/all_to_all | solution.py:526
  140.4 0.9 shard_map.80
  (3 shorter events, 0.0 us)
Async XLA Ops:
  2.9 16.2 %all-to-all-start = ((f32[8,64,128]{2,1,0:T(8,128)}), f32[8,64,128]{2,1,0:T(8,128)S(1)}, u32[]{:S(2)}, u32[]{:S(2)}) async-start(f32[8,64,128]{2,1,0:T(8,128)} %bitcast.2), calls=%async_computation | async-start | bytes 524288 | tf_op jit(solution)/shard_map/all_to_all | solution.py:523
  15.6 2.0 %copy-start = (f32[8384,128]{1,0:T(8,128)}, f32[8384,128]{1,0:T(8,128)S(1)}, u32[]{:S(2)}) copy-start(f32[8384,128]{1,0:T(8,128)S(1)} %shard_map.69.table_ref) | copy-start | bytes 12877828
  19.1 2.2 %copy-start.1 = (f32[8384,128]{1,0:T(8,128)S(1)}, f32[8384,128]{1,0:T(8,128)}, u32[]{:S(2)}) copy-start(f32[8384,128]{1,0:T(8,128)} %copy-done) | copy-start | bytes 12877828
  21.4 42.0 %slice-start = ((s8[4292608]{0:T(1024)(128)(4,1)}), s8[4194304]{0:T(1024)(128)(4,1)S(1)}, s32[]{:S(2)}) async-start(s8[4292608]{0:T(1024)(128)(4,1)} %bitcast.15), calls=%async_computation.10 | async-start | bytes 8388608
  36.9 26.4 %slice-start.1 = ((s8[4292608]{0:T(1024)(128)(4,1)}), s8[98304]{0:T(1024)(128)(4,1)S(1)}, s32[]{:S(2)}) async-start(s8[4292608]{0:T(1024)(128)(4,1)} %bitcast.15), calls=%async_computation.11 | async-start | bytes 196608
  130.4 10.1 %all-to-all-start.9 = ((f32[32,1,128]{2,1,0:T(1,128)}), f32[32,1,128]{2,1,0:T(1,128)S(1)}, u32[]{:S(2)}, u32[]{:S(2)}) async-start(f32[32,1,128]{2,1,0:T(1,128)} %get-tuple-element.56), calls=%async_computation.9 | async-start | bytes 32768 | tf_op jit(solution)/shard_map/all_to_all | solution.py:526

commit v12 on v11

--- a/solution.py
+++ b/solution.py
@@ -142,49 +142,25 @@
     to_crossing([obs_ref[...]], perm, q, put)
 
 
-def table_rows(params, tiles):
-    return (params + 1) * tiles + 3 * (tiles // LANES) * (KNOT_DEV + PAD)
-
-
-def table_views(table_ref, params, tiles):
-    return [table_ref.at[p * tiles : (p + 1) * tiles] for p in range(params + 1)]
-
-
-def table_weights(table_ref, params, tiles):
-    height = KNOT_DEV + PAD
-    chunks = tiles // LANES
-    parts = []
-    for index in range(3):
-        first = (params + 1) * tiles + index * chunks * height
-        parts.append(
-            jnp.concatenate(
-                [table_ref[first + c * height : first + (c + 1) * height, :] for c in range(chunks)],
-                axis=1,
-            )
-        )
-    return parts
-
-
-def table_kernel(
+def rows_kernel(
     q,
     together,
     me_ref,
     match_hbm,
     knot_hbm,
     frac_hbm,
-    sent_hbm,
+    _,
     jac_hbm,
-    table_ref,
+    rows_ref,
+    weight_ref,
     match_ref,
     knot_ref,
     frac_ref,
     sems,
 ):
-    params, tiles, _ = jac_hbm.shape
-    views = table_views(table_ref, params, tiles)
+    params, tiles = jac_hbm.shape[:2]
     pairs = [(match_hbm, match_ref), (knot_hbm, knot_ref), (frac_hbm, frac_ref)]
-    pairs += [(jac_hbm.at[p], views[p]) for p in range(params)]
-    pairs += [(sent_hbm, views[params])]
+    pairs += [(jac_hbm.at[p], rows_ref.at[p]) for p in range(params)]
     copies = [
         pltpu.make_async_copy(source, target, sems.at[index])
         for index, (source, target) in enumerate(pairs)
@@ -202,24 +178,18 @@
     main = jnp.where(knots == knot, 1.0 - frac, 0.0) + jnp.where(knots == knot + 1.0, frac, 0.0)
     first_row = lax.broadcasted_iota(jnp.int32, (PAD, tiles), 0) == 0
     edge = jnp.where(first_row, jnp.where(knot == KNOT_DEV - 1.0, frac, 0.0), 0.0)
-    place = (params + 1) * tiles
-    for upper, lower in zip(split3(main), split3(edge)):
-        for c in range(tiles // LANES):
-            lanes = slice(c * LANES, (c + 1) * LANES)
-            table_ref[place : place + KNOT_DEV, :] = upper[:, lanes].astype(jnp.float32)
-            place += KNOT_DEV
-            table_ref[place : place + PAD, :] = lower[:, lanes].astype(jnp.float32)
-            place += PAD
+    for index, (upper, lower) in enumerate(zip(split3(main), split3(edge))):
+        weight_ref[index, 0:KNOT_DEV, :] = upper
+        weight_ref[index, KNOT_DEV : KNOT_DEV + PAD, :] = lower
 
     for first in range(0, params, together):
         for p in range(first, first + together):
             copies[3 + p].wait()
 
         def put(index, block_index, block):
-            views[first + index][block_index * q : (block_index + 1) * q, :] = block
-
-        to_crossing([views[p][...] for p in range(first, first + together)], perm, q, put)
-    copies[3 + params].wait()
+            rows_ref[first + index, block_index * q : (block_index + 1) * q, :] = block
+
+        to_crossing([rows_ref[p] for p in range(first, first + together)], perm, q, put)
 
 
 def weight_dot(x, parts, over_tiles):
@@ -279,26 +249,42 @@
 
 
 def first_adjoint_kernel(
-    q, params, me_ref, arrived_ref, table_ref, diff_ref, send_ref, values_ref
+    q,
+    me_ref,
+    arrived_ref,
+    rows_ref,
+    sent_hbm,
+    weight_hbm,
+    diff_ref,
+    send_ref,
+    weight_ref,
+    values_ref,
+    sent_ref,
+    sems,
 ):
-    tiles = arrived_ref.shape[0]
-    views = table_views(table_ref, params, tiles)
-    parts = [part.astype(jnp.bfloat16) for part in table_weights(table_ref, params, tiles)]
-    difference(me_ref[0], views[params], arrived_ref, diff_ref, q)
-    adjoint_rows(q, params, diff_ref, views, parts, send_ref, values_ref)
+    copies = [
+        pltpu.make_async_copy(sent_hbm, sent_ref, sems.at[0]),
+        pltpu.make_async_copy(weight_hbm, weight_ref, sems.at[1]),
+    ]
+    for copy in copies:
+        copy.start()
+    copies[0].wait()
+    difference(me_ref[0], sent_ref, arrived_ref, diff_ref, q)
+    adjoint_values(q, diff_ref, rows_ref, values_ref)
+    copies[1].wait()
+    adjoint_rows(rows_ref.shape[0], values_ref, weight_ref, send_ref)
 
 
 def adjoint_kernel(
-    q, params, me_ref, sent_ref, arrived_ref, table_ref, weight_ref, diff_ref, send_ref, values_ref
+    q, me_ref, sent_ref, arrived_ref, rows_ref, weight_ref, diff_ref, send_ref, values_ref
 ):
-    views = table_views(table_ref, params, sent_ref.shape[0])
     difference(me_ref[0], sent_ref, arrived_ref, diff_ref, q)
-    parts = [weight_ref[index] for index in range(3)]
-    adjoint_rows(q, params, diff_ref, views, parts, send_ref, values_ref)
-
-
-def adjoint_rows(q, params, diff_ref, views, parts, send_ref, values_ref):
-    tiles = diff_ref.shape[0]
+    adjoint_values(q, diff_ref, rows_ref, values_ref)
+    adjoint_rows(rows_ref.shape[0], values_ref, weight_ref, send_ref)
+
+
+def adjoint_values(q, diff_ref, jac_ref, values_ref):
+    params, tiles, _ = jac_ref.shape
     groups = LANES // q
     group = lane_group((PAD, LANES), q)
     for c in range(tiles // LANES):
@@ -307,11 +293,14 @@
             rows = slice((c * groups + i) * q, (c * groups + i + 1) * q)
             diff = diff_ref[rows, :]
             sums = fold_lanes(
-                row_sums([fold_rows(views[p][rows, :] * diff) for p in range(params)]), q
+                row_sums([fold_rows(jac_ref[p, rows, :] * diff) for p in range(params)]), q
             )
             values = sums if values is None else jnp.where(group == i, sums, values)
         values_ref[:, c * LANES : (c + 1) * LANES] = values
-    spread = weight_dot(values_ref[...], parts, True)
+
+
+def adjoint_rows(params, values_ref, weight_ref, send_ref):
+    spread = weight_dot(values_ref[...], [weight_ref[index] for index in range(3)], True)
     lane = lax.broadcasted_iota(jnp.int32, (PAD, LANES), 1)
     row = lax.broadcasted_iota(jnp.int32, (PAD, LANES), 0)
     spill = jnp.sum(
@@ -351,9 +340,8 @@
     return jnp.sum(total, keepdims=True)
 
 
-def predict(me, q, direction_ref, views, parts, edge, interp_ref, sent_ref):
-    params = len(views) - 1
-    tiles = sent_ref.shape[0]
+def predict(me, q, direction_ref, jac_ref, parts, edge, interp_ref, sent_ref):
+    params, tiles, _ = jac_ref.shape
     n_track = direction_ref.shape[0]
     following = direction_ref[jnp.minimum(me + 1, n_track - 1)][:, 0:1]
     following = jnp.where(me + 1 < n_track, following, 0.0)
@@ -372,9 +360,9 @@
     def block_values(b, carry):
         rows = pl.ds(pl.multiple_of(b * q, SUB), q)
         interp = interp_ref[b]
-        total = views[0][rows, :] * interp[0:1]
+        total = jac_ref[0, rows, :] * interp[0:1]
         for p in range(1, params):
-            total = total + views[p][rows, :] * interp[p : p + 1]
+            total = total + jac_ref[p, rows, :] * interp[p : p + 1]
         sent_ref[rows, :] = total
         return carry
 
@@ -384,43 +372,37 @@
 def first_kernel(
     q,
     n_det,
-    params,
     me_ref,
     gathered_ref,
-    table_ref,
+    rows_ref,
+    weight_ref,
     grad_ref,
     norm_ref,
     sent_ref,
-    weight_ref,
     edge_ref,
     interp_ref,
 ):
     n_track = grad_ref.shape[0]
-    tiles = sent_ref.shape[0]
 
     def put(b, field):
         grad_ref[b] = field
 
-    field_sums(gathered_ref, n_track, n_det, params, put)
+    field_sums(gathered_ref, n_track, n_det, rows_ref.shape[0], put)
     norm_ref[...] = jnp.broadcast_to(full_dot(grad_ref, grad_ref), norm_ref.shape)
-    wide = table_weights(table_ref, params, tiles)
-    edge = sum(part[KNOT_DEV : KNOT_DEV + SUB] for part in reversed(wide))
+    edge = sum(
+        weight_ref[index, KNOT_DEV : KNOT_DEV + PAD, :].astype(jnp.float32) for index in (2, 1, 0)
+    )[0:SUB]
     edge_ref[...] = edge
-    parts = [part.astype(jnp.bfloat16) for part in wide]
-    for index, part in enumerate(parts):
-        weight_ref[index] = part
-    upper = [part[0:KNOT_DEV] for part in parts]
-    views = table_views(table_ref, params, tiles)
-    predict(me_ref[0], q, grad_ref, views, upper, edge[0:1], interp_ref, sent_ref)
+    parts = [weight_ref[index, 0:KNOT_DEV, :] for index in range(3)]
+    predict(me_ref[0], q, grad_ref, rows_ref, parts, edge[0:1], interp_ref, sent_ref)
 
 
 def step_kernel(
     q,
     n_det,
-    params,
     me_ref,
     gathered_ref,
-    table_ref,
+    rows_ref,
     weight_ref,
     edge_ref,
     grad_ref,
@@ -442,7 +424,7 @@
     def put(b, field):
         image_ref[b] = field + damping * direction_ref[b]
 
-    field_sums(gathered_ref, n_track, n_det, params, put)
+    field_sums(gathered_ref, n_track, n_det, rows_ref.shape[0], put)
     norm = norm_ref[0:1, 0:1]
     length = norm / full_dot(direction_ref, image_ref)
     length_out[...] = jnp.broadcast_to(length, length_out.shape)
@@ -454,9 +436,8 @@
     ratio = new_norm / norm
     for b in range(n_track):
         direction_out[b] = grad_out[b] + ratio * direction_ref[b]
-    views = table_views(table_ref, params, sent_ref.shape[0])
     parts = [weight_ref[index, 0:KNOT_DEV, :] for index in range(3)]
-    predict(me, q, direction_out, views, parts, edge_ref[0:1, :], interp_ref, sent_ref)
+    predict(me, q, direction_out, rows_ref, parts, edge_ref[0:1, :], interp_ref, sent_ref)
 
 
 def last_kernel(q, me_ref, sent_ref, arrived_ref, diff_ref, send_ref):
@@ -534,15 +515,16 @@
         [int_row, pltpu.VMEM((tiles, columns), jnp.float32), pltpu.SemaphoreType.DMA((2,))],
     )(me, match_row, from_hbm(obs))
     arrived = crossing(sent)
-    table = call(
-        functools.partial(table_kernel, q, math.gcd(params, 3)),
-        kept((table_rows(params, tiles), columns)),
+    weight_shape = (3, KNOT_DEV + PAD, tiles)
+    rows, weights = call(
+        functools.partial(rows_kernel, q, math.gcd(params, 3)),
+        (kept((params, tiles, columns)), pltpu.HBM(weight_shape, jnp.bfloat16)),
         [SMEM] + [ANY] * 5,
         [
             int_row,
             int_row,
             pltpu.VMEM((1, tiles), jnp.float32),
-            pltpu.SemaphoreType.DMA((4 + params,)),
+            pltpu.SemaphoreType.DMA((3 + params,)),
         ],
     )(
         me,
@@ -554,39 +536,36 @@
     scalar = f32(SUB, LANES)
     interp = pltpu.VMEM((n_track, PAD, LANES), jnp.float32)
     adjoint_out = (f32(tiles, columns), f32(n_all, PAD, LANES))
-    values = [pltpu.VMEM((PAD, tiles), jnp.float32)]
-    misfit, payload = call(
-        functools.partial(first_adjoint_kernel, q, params), adjoint_out, [SMEM] + [VMEM] * 2, values
-    )(me, arrived, table)
-    gradient, slope_norm, sent, weights, edge = call(
-        functools.partial(first_kernel, q, n_det, params),
-        (
-            field,
-            scalar,
-            f32(tiles, columns),
-            jax.ShapeDtypeStruct((3, KNOT_DEV + PAD, tiles), jnp.bfloat16),
-            f32(SUB, tiles),
-        ),
-        [SMEM] + [VMEM] * 2,
+    values = pltpu.VMEM((PAD, tiles), jnp.float32)
+    misfit, payload, weights = call(
+        functools.partial(first_adjoint_kernel, q),
+        adjoint_out + (jax.ShapeDtypeStruct(weight_shape, jnp.bfloat16),),
+        [SMEM, VMEM, VMEM, ANY, ANY],
+        [values, pltpu.VMEM((tiles, columns), jnp.float32), pltpu.SemaphoreType.DMA((2,))],
+    )(me, arrived, rows, from_hbm(sent), from_hbm(weights))
+    gradient, slope_norm, sent, edge = call(
+        functools.partial(first_kernel, q, n_det),
+        (field, scalar, f32(tiles, columns), f32(SUB, tiles)),
+        [SMEM] + [VMEM] * 3,
         [interp],
-    )(me, everywhere(payload), table)
+    )(me, everywhere(payload), rows, weights)
     direction = gradient
     knot_field = jnp.zeros((PAD, KNOT_DEV), jnp.float32)
     lengths, changes = [], []
     for iteration in range(ITERS - 1):
         change, payload = call(
-            functools.partial(adjoint_kernel, q, params), adjoint_out, [SMEM] + [VMEM] * 4, values
-        )(me, sent, crossing(sent), table, weights)
+            functools.partial(adjoint_kernel, q), adjoint_out, [SMEM] + [VMEM] * 4, [values]
+        )(me, sent, crossing(sent), rows, weights)
         gathered = everywhere(payload)
         last = iteration == ITERS - 2
         results = call(
-            functools.partial(step_kernel, q, n_det, params),
+            functools.partial(step_kernel, q, n_det),
             (field, scalar, f32(PAD, KNOT_DEV), scalar, f32(tiles, columns))
             + (() if last else (field,)),
             [SMEM] + [VMEM] * 8,
             [interp] * (3 if last else 2),
         )(
-            me, gathered, table, weights, edge, gradient, direction, slope_norm, knot_field
+            me, gathered, rows, weights, edge, gradient, direction, slope_norm, knot_field
         )
         direction, slope_norm, knot_field, length, sent = results[:5]
         gradient = None if last else results[5]

time: 142 us -> 141 us (level)
    all_to_all x1, waiting for transfers between devices: 4.15 us -> 1.37 us  [everywhere(): lax.all_to_all(values, ('track', 'det'), split_axis=0, concat_axis=0, til...]
    all_to_all x1, waiting for transfers between devices: 1.52 us -> 3.52 us  [crossing(): lax.all_to_all(values, 'track', split_axis=0, concat_axis=0, tiled=True)]
    unnamed x8 -> x16, local copies, waits for them, and re-layouts: 4.19 us -> 4.24 us
where the time goes in v12:
time: 141 us
  blocking collectives  101 us (72%)
  Pallas kernels  19.6 us (14%)
  starting transfers between devices  10.3 us (7%)
  waiting for transfers between devices  4.89 us (3%)
  local copies, waits for them, and re-layouts  4.25 us (3%)
    all_to_all x4, blocking collectives, everywhere(): lax.all_to_all(values, ('track', 'det'), split_axis=0, concat_axis=0, til...  54.2 us
    all_to_all x4, blocking collectives, crossing(): lax.all_to_all(values, 'track', split_axis=0, concat_axis=0, tiled=True)  46.8 us
    all_to_all x1, starting transfers between devices, crossing(): lax.all_to_all(values, 'track', split_axis=0, concat_axis=0, tiled=True)  7.29 us
    pallas_call x1, Pallas kernels, local(): call(functools.partial(rows_kernel, q, math.gcd(params, 3)), (kept((param...  5.39 us
    unnamed x16, local copies, waits for them, and re-layouts  4.24 us
    all_to_all x1, waiting for transfers between devices, crossing(): lax.all_to_all(values, 'track', split_axis=0, concat_axis=0, tiled=True)  3.52 us
    all_to_all x1, starting transfers between devices, everywhere(): lax.all_to_all(values, ('track', 'det'), split_axis=0, concat_axis=0, til...  3 us
    pallas_call x1, Pallas kernels, local(): call(functools.partial(restore_kernel, q), (f32(tiles, columns), f32(tile...  2.91 us
  transfers between devices with their start and end apart: 2, of which 2 were waited for; matrix products, arithmetic and copies ran while one was open for 0% of the time, Pallas kernels for 6%

profile of v12, /device:TPU:0, one launch (start us, length us, event | category | flops | bytes accessed | tf_op | source)
XLA Modules:
  0.0 140.8 jit_solution(8124015211927664856)
XLA Ops:
  0.6 2.3 %shard_map.68._.sent_hbm = f32[512,128]{1,0:T(8,128)} custom-call(s32[1]{0:T(128)} %bitcast.me_ref, s32[1,512]{1,0:T(1,128)} %bitcast.25, f32[512,128]{1,0:T(8,128)} %obs_hbm.1), custom_call_target="tpu_custom_call" | custom-call | tf_op jit(solution)/shard_map/pallas_call | solution.py:511
  2.9 7.3 %all-to-all-start = ((f32[8,64,128]{2,1,0:T(8,128)}), f32[8,64,128]{2,1,0:T(8,128)S(1)}, u32[]{:S(2)}, u32[]{:S(2)}) async-start(f32[8,64,128]{2,1,0:T(8,128)} %bitcast.2), calls=%async_computation | async-start | bytes 524288 | tf_op jit(solution)/shard_map/all_to_all | solution.py:504
  10.2 5.4 %shard_map.69 = (f32[12,512,128]{2,1,0:T(8,128)S(1)}, bf16[3,144,512]{2,1,0:T(8,128)(2,1)}) custom-call(s32[1]{0:T(128)} %bitcast.me_ref, s32[1,512]{1,0:T(1,128)} %bitcast.26, s32[1,512]{1,0:T(1,128)} %bitcast.28, f32[1,512]{1,0:T(1,128)} %bitcast.29, f32[512,128]{1,0:T(8,128)} %shard_map.68._.sent_hbm, f32[12,512,128]{2,1,0:T(8,128)} %bitcast.24), custom_call_target="tpu_custom_call" | custom-call | tf_op jit(solution)/shard_map/pallas_call | solution.py:519
  15.6 3.5 %all-to-all-done = f32[8,64,128]{2,1,0:T(8,128)S(1)} async-done(((f32[8,64,128]{2,1,0:T(8,128)}), f32[8,64,128]{2,1,0:T(8,128)S(1)}, u32[]{:S(2)}, u32[]{:S(2)}) %all-to-all-start) | async-done | bytes 262176 | tf_op jit(solution)/shard_map/all_to_all | solution.py:504
  19.1 1.7 %shard_map.70 = (f32[512,128]{1,0:T(8,128)S(1)}, f32[32,16,128]{2,1,0:T(8,128)S(1)}, bf16[3,144,512]{2,1,0:T(8,128)(2,1)S(1)}) custom-call(s32[1]{0:T(128)} %bitcast.me_ref, f32[512,128]{1,0:T(8,128)S(1)} %bitcast.15, f32[12,512,128]{2,1,0:T(8,128)S(1)} %get-tuple-element.38.rows_ref, f32[512,128]{1,0:T(8,128)} %shard_map.68._.sent_hbm, ...), custom_call_target="tpu_custom_call" | custom-call | tf_op jit(solution)/shard_map/pallas_call | solution.py:540
  20.9 0.0 copy-start
  20.9 0.7 copy-done
  21.6 14.0 %all_to_all.80.gathered_ref = f32[32,16,128]{2,1,0:T(8,128)S(1)} all-to-all(f32[32,16,128]{2,1,0:T(8,128)S(1)} %get-tuple-element.40), channel_id=1, replica_groups=mesh['track'=8,'det'=4] {'track','det'}, dimensions={0} | all-to-all | bytes 524288 | tf_op jit(solution)/shard_map/all_to_all | solution.py:507
  35.6 0.7 shard_map.71
  36.2 11.7 %all_to_all.81 = f32[8,64,128]{2,1,0:T(8,128)S(1)} all-to-all(f32[8,64,128]{2,1,0:T(8,128)S(1)} %bitcast.18), channel_id=1, replica_groups=mesh['track'=8,'det'=4] {'track'}, dimensions={0} | all-to-all | bytes 524288 | tf_op jit(solution)/shard_map/all_to_all | solution.py:504
  47.9 0.7 shard_map.72
  48.6 0.7 copy-done.2
  49.3 13.4 %all_to_all.82.gathered_ref = f32[32,16,128]{2,1,0:T(8,128)S(1)} all-to-all(f32[32,16,128]{2,1,0:T(8,128)S(1)} %get-tuple-element.43), channel_id=1, replica_groups=mesh['track'=8,'det'=4] {'track','det'}, dimensions={0} | all-to-all | bytes 524288 | tf_op jit(solution)/shard_map/all_to_all | solution.py:507
  62.7 1.0 shard_map.73
  63.7 11.7 %all_to_all.83 = f32[8,64,128]{2,1,0:T(8,128)S(1)} all-to-all(f32[8,64,128]{2,1,0:T(8,128)S(1)} %bitcast.17), channel_id=1, replica_groups=mesh['track'=8,'det'=4] {'track'}, dimensions={0} | all-to-all | bytes 524288 | tf_op jit(solution)/shard_map/all_to_all | solution.py:504
  75.4 0.7 shard_map.74
  76.1 13.4 %all_to_all.84.gathered_ref = f32[32,16,128]{2,1,0:T(8,128)S(1)} all-to-all(f32[32,16,128]{2,1,0:T(8,128)S(1)} %get-tuple-element.48), channel_id=1, replica_groups=mesh['track'=8,'det'=4] {'track','det'}, dimensions={0} | all-to-all | bytes 524288 | tf_op jit(solution)/shard_map/all_to_all | solution.py:507
  89.5 1.0 shard_map.75
  90.4 11.7 %all_to_all.85 = f32[8,64,128]{2,1,0:T(8,128)S(1)} all-to-all(f32[8,64,128]{2,1,0:T(8,128)S(1)} %bitcast.16), channel_id=1, replica_groups=mesh['track'=8,'det'=4] {'track'}, dimensions={0} | all-to-all | bytes 524288 | tf_op jit(solution)/shard_map/all_to_all | solution.py:504
  102.1 0.7 shard_map.76
  102.8 0.0 copy-start.1
  102.8 13.4 %all_to_all.86.gathered_ref = f32[32,16,128]{2,1,0:T(8,128)S(1)} all-to-all(f32[32,16,128]{2,1,0:T(8,128)S(1)} %get-tuple-element.54), channel_id=1, replica_groups=mesh['track'=8,'det'=4] {'track','det'}, dimensions={0} | all-to-all | bytes 524288 | tf_op jit(solution)/shard_map/all_to_all | solution.py:507
  116.3 0.9 shard_map.77
  117.2 11.7 %all_to_all.87 = f32[8,64,128]{2,1,0:T(8,128)S(1)} all-to-all(f32[8,64,128]{2,1,0:T(8,128)S(1)} %bitcast.22), channel_id=1, replica_groups=mesh['track'=8,'det'=4] {'track'}, dimensions={0} | all-to-all | bytes 524288 | tf_op jit(solution)/shard_map/all_to_all | solution.py:504
  128.9 0.8 shard_map.78
  129.7 3.0 %all-to-all-start.9 = ((f32[32,1,128]{2,1,0:T(1,128)}), f32[32,1,128]{2,1,0:T(1,128)S(1)}, u32[]{:S(2)}, u32[]{:S(2)}) async-start(f32[32,1,128]{2,1,0:T(1,128)} %get-tuple-element.60), calls=%async_computation.9 | async-start | bytes 32768 | tf_op jit(solution)/shard_map/all_to_all | solution.py:507
  132.7 0.9 copy-done.3
  133.7 0.9 copy-done.5
  134.6 0.9 copy-done.7
  135.6 2.9 %shard_map.79 = (f32[512,128]{1,0:T(8,128)S(1)}, f32[512,128]{1,0:T(8,128)S(1)}) custom-call(s32[1]{0:T(128)} %bitcast.me_ref, s32[1,512]{1,0:T(1,128)} %bitcast.27, f32[512,128]{1,0:T(8,128)S(1)} %copy-done.1, f32[512,128]{1,0:T(8,128)S(1)} %get-tuple-element.65.diff_ref, f32[8,128]{1,0:T(8,128)S(1)} %get-tuple-element.66.refs_0_, ...), custom_call_target="tpu_custom_call" | custom-call | tf_op jit(solution)/shard_map/pallas_call | solution.py:580
  138.5 1.4 all-to-all-done.9.squares_ref
  139.9 0.9 shard_map.80
  (10 shorter events, 0.0 us)
Async XLA Ops:
  2.9 16.2 %all-to-all-start = ((f32[8,64,128]{2,1,0:T(8,128)}), f32[8,64,128]{2,1,0:T(8,128)S(1)}, u32[]{:S(2)}, u32[]{:S(2)}) async-start(f32[8,64,128]{2,1,0:T(8,128)} %bitcast.2), calls=%async_computation | async-start | bytes 524288 | tf_op jit(solution)/shard_map/all_to_all | solution.py:504
  20.9 0.7 copy-start
  48.6 0.7 copy-start.2
  76.1 26.8 %copy-start.4 = (f32[512,128]{1,0:T(8,128)}, f32[512,128]{1,0:T(8,128)S(1)}, u32[]{:S(2)}) copy-start(f32[512,128]{1,0:T(8,128)S(1)} %get-tuple-element.70.refs_4_) | copy-start | bytes 786436
  102.8 14.4 %copy-start.6 = (f32[512,128]{1,0:T(8,128)}, f32[512,128]{1,0:T(8,128)S(1)}, u32[]{:S(2)}) copy-start(f32[512,128]{1,0:T(8,128)S(1)} %get-tuple-element.71.refs_5_) | copy-start | bytes 786436
  102.8 29.9 %copy-start.1 = (f32[512,128]{1,0:T(8,128)S(1)}, f32[512,128]{1,0:T(8,128)}, u32[]{:S(2)}) copy-start(f32[512,128]{1,0:T(8,128)} %copy-done) | copy-start | bytes 786436
  129.7 10.2 %all-to-all-start.9 = ((f32[32,1,128]{2,1,0:T(1,128)}), f32[32,1,128]{2,1,0:T(1,128)S(1)}, u32[]{:S(2)}, u32[]{:S(2)}) async-start(f32[32,1,128]{2,1,0:T(1,128)} %get-tuple-element.60), calls=%async_computation.9 | async-start | bytes 32768 | tf_op jit(solution)/shard_map/all_to_all | solution.py:507
  132.7 1.0 copy-start.3
  133.7 0.9 copy-start.5
  134.6 0.9 copy-start.7

commit v13 on v12

--- a/solution.py
+++ b/solution.py
@@ -255,10 +255,11 @@
     rows_ref,
     sent_hbm,
     weight_hbm,
-    diff_ref,
+    diff_hbm,
     send_ref,
     weight_ref,
     values_ref,
+    diff_ref,
     sent_ref,
     sems,
 ):
@@ -270,17 +271,33 @@
         copy.start()
     copies[0].wait()
     difference(me_ref[0], sent_ref, arrived_ref, diff_ref, q)
+    out = pltpu.make_async_copy(diff_ref, diff_hbm, sems.at[2])
+    out.start()
     adjoint_values(q, diff_ref, rows_ref, values_ref)
     copies[1].wait()
     adjoint_rows(rows_ref.shape[0], values_ref, weight_ref, send_ref)
+    out.wait()
 
 
 def adjoint_kernel(
-    q, me_ref, sent_ref, arrived_ref, rows_ref, weight_ref, diff_ref, send_ref, values_ref
+    q,
+    me_ref,
+    sent_ref,
+    arrived_ref,
+    rows_ref,
+    weight_ref,
+    diff_hbm,
+    send_ref,
+    values_ref,
+    diff_ref,
+    sem,
 ):
     difference(me_ref[0], sent_ref, arrived_ref, diff_ref, q)
+    out = pltpu.make_async_copy(diff_ref, diff_hbm, sem)
+    out.start()
     adjoint_values(q, diff_ref, rows_ref, values_ref)
     adjoint_rows(rows_ref.shape[0], values_ref, weight_ref, send_ref)
+    out.wait()
 
 
 def adjoint_values(q, diff_ref, jac_ref, values_ref):
@@ -447,22 +464,29 @@
     send_ref[...] = jnp.broadcast_to(squares[None], send_ref.shape)
 
 
-def restore_kernel(q, me_ref, match_hbm, misfit_ref, diff_ref, *refs):
-    steps = (len(refs) - 5) // 2
-    residual_out, diff_out, residual_ref, match_ref, sem = refs[2 * steps :]
-    tiles = misfit_ref.shape[0]
-    copy = pltpu.make_async_copy(match_hbm, match_ref, sem)
-    copy.start()
-    copy.wait()
+def restore_kernel(q, me_ref, match_hbm, diff_ref, *refs):
+    steps = (len(refs) - 7) // 2
+    residual_out, diff_out, residual_ref, match_ref, held_ref, sems = refs[2 * steps + 1 :]
+    tiles = diff_ref.shape[0]
+    copies = [pltpu.make_async_copy(match_hbm, match_ref, sems.at[steps + 1])]
+    for index, source in enumerate(refs[steps : 2 * steps + 1]):
+        copies.append(pltpu.make_async_copy(source, held_ref.at[index], sems.at[index]))
+    for copy in copies:
+        copy.start()
+    copies[0].wait()
     perm = crossing_order(me_ref[0], match_ref[...])
-    residual = misfit_ref[...]
-    for length_ref, change_ref in zip(refs[:steps], refs[steps : 2 * steps]):
-        residual = residual - length_ref[0:1, 0:1] * change_ref[...]
+    diff_out[...] = from_crossing(
+        lambda index: diff_ref[index * q : (index + 1) * q, :], perm, q, tiles
+    )
+    for copy in copies[1:]:
+        copy.wait()
+    residual = held_ref[0]
+    for index, length_ref in enumerate(refs[:steps]):
+        residual = residual - length_ref[0:1, 0:1] * held_ref[index + 1]
     residual_ref[...] = residual
-    for source, target in ((residual_ref, residual_out), (diff_ref, diff_out)):
-        target[...] = from_crossing(
-            lambda index: source[index * q : (index + 1) * q, :], perm, q, tiles
-        )
+    residual_out[...] = from_crossing(
+        lambda index: residual_ref[index * q : (index + 1) * q, :], perm, q, tiles
+    )
 
 
 def finish_kernel(
@@ -481,12 +505,12 @@
     residual_out[...] = residual_ref[...] - length * diff_ref[...]
 
 
-def call(kernel, outs, ins, scratch=()):
+def call(kernel, outs, ins, scratch=(), places=None):
     return pl.pallas_call(
         kernel,
         out_shape=outs,
         in_specs=ins,
-        out_specs=jax.tree.map(lambda _: VMEM, outs),
+        out_specs=places or jax.tree.map(lambda _: VMEM, outs),
         scratch_shapes=list(scratch),
         compiler_params=PARAMS,
     )
@@ -535,13 +559,15 @@
     field = f32(n_track, PAD, LANES)
     scalar = f32(SUB, LANES)
     interp = pltpu.VMEM((n_track, PAD, LANES), jnp.float32)
-    adjoint_out = (f32(tiles, columns), f32(n_all, PAD, LANES))
+    adjoint_out = (pltpu.HBM((tiles, columns), jnp.float32), f32(n_all, PAD, LANES))
     values = pltpu.VMEM((PAD, tiles), jnp.float32)
+    plane = pltpu.VMEM((tiles, columns), jnp.float32)
     misfit, payload, weights = call(
         functools.partial(first_adjoint_kernel, q),
         adjoint_out + (jax.ShapeDtypeStruct(weight_shape, jnp.bfloat16),),
         [SMEM, VMEM, VMEM, ANY, ANY],
-        [values, pltpu.VMEM((tiles, columns), jnp.float32), pltpu.SemaphoreType.DMA((2,))],
+        [values, plane, plane, pltpu.SemaphoreType.DMA((3,))],
+        (ANY, VMEM, VMEM),
     )(me, arrived, rows, from_hbm(sent), from_hbm(weights))
     gradient, slope_norm, sent, edge = call(
         functools.partial(first_kernel, q, n_det),
@@ -554,7 +580,11 @@
     lengths, changes = [], []
     for iteration in range(ITERS - 1):
         change, payload = call(
-            functools.partial(adjoint_kernel, q), adjoint_out, [SMEM] + [VMEM] * 4, [values]
+            functools.partial(adjoint_kernel, q),
+            adjoint_out,
+            [SMEM] + [VMEM] * 4,
+            [values, plane, pltpu.SemaphoreType.DMA],
+            (ANY, VMEM),
         )(me, sent, crossing(sent), rows, weights)
         gathered = everywhere(payload)
         last = iteration == ITERS - 2
@@ -580,9 +610,14 @@
     residual, change = call(
         functools.partial(restore_kernel, q),
         (f32(tiles, columns), f32(tiles, columns)),
-        [SMEM, ANY] + [VMEM] * (2 + 2 * len(changes)),
-        [pltpu.VMEM((tiles, columns), jnp.float32), int_row, pltpu.SemaphoreType.DMA],
-    )(me, match_row, misfit, change, *lengths, *changes)
+        [SMEM, ANY, VMEM] + [VMEM] * len(lengths) + [ANY] * (1 + len(changes)),
+        [
+            plane,
+            int_row,
+            pltpu.VMEM((1 + len(changes), tiles, columns), jnp.float32),
+            pltpu.SemaphoreType.DMA((2 + len(changes),)),
+        ],
+    )(me, match_row, change, *lengths, *map(from_hbm, [misfit] + changes))
     return call(
         finish_kernel,
         (f32(params, KNOT_DEV), f32(tiles, columns)),

time: 141 us -> 141 us (level)
  local copies, waits for them, and re-layouts: 4.25 us -> 0.01 us
  Pallas kernels: 19.6 us -> 22.3 us
  waiting for transfers between devices: 4.89 us -> 6.41 us
    unnamed x16 -> x0, local copies, waits for them, and re-layouts: 4.24 us -> none
    all_to_all x1, waiting for transfers between devices: 1.37 us -> 2.89 us  [everywhere(): lax.all_to_all(values, ('track', 'det'), split_axis=0, concat_axis=0, til...]
  transfers between devices with their start and end apart: 2 -> 2, of which waited for: 2 -> 2; matrix products, arithmetic and copies ran while one was open for 0% -> 0% of each run, Pallas kernels for 6% -> 7%
where the time goes in v13:
time: 141 us
  blocking collectives  101 us (72%)
  Pallas kernels  22.3 us (16%)
  starting transfers between devices  10.3 us (7%)
  waiting for transfers between devices  6.41 us (5%)
    all_to_all x4, blocking collectives, everywhere(): lax.all_to_all(values, ('track', 'det'), split_axis=0, concat_axis=0, til...  54.2 us
    all_to_all x4, blocking collectives, crossing(): lax.all_to_all(values, 'track', split_axis=0, concat_axis=0, tiled=True)  46.8 us
    all_to_all x1, starting transfers between devices, crossing(): lax.all_to_all(values, 'track', split_axis=0, concat_axis=0, tiled=True)  7.29 us
    pallas_call x1, Pallas kernels, local(): call(functools.partial(rows_kernel, q, math.gcd(params, 3)), (kept((param...  5.39 us
    pallas_call x1, Pallas kernels, local(): call(functools.partial(restore_kernel, q), (f32(tiles, columns), f32(tile...  4.25 us
    all_to_all x1, waiting for transfers between devices, crossing(): lax.all_to_all(values, 'track', split_axis=0, concat_axis=0, tiled=True)  3.52 us
    pallas_call x3, Pallas kernels, local(): call(functools.partial(adjoint_kernel, q), adjoint_out, [SMEM] + [VMEM] *...  3.08 us
    all_to_all x1, starting transfers between devices, everywhere(): lax.all_to_all(values, ('track', 'det'), split_axis=0, concat_axis=0, til...  3 us
  transfers between devices with their start and end apart: 2, of which 2 were waited for; matrix products, arithmetic and copies ran while one was open for 0% of the time, Pallas kernels for 7%

profile of v13, /device:TPU:0, one launch (start us, length us, event | category | flops | bytes accessed | tf_op | source)
XLA Modules:
  0.0 140.7 jit_solution(15919436371803516587)
XLA Ops:
  0.6 2.3 %shard_map.68._.sent_hbm = f32[512,128]{1,0:T(8,128)} custom-call(s32[1]{0:T(128)} %bitcast.me_ref, s32[1,512]{1,0:T(1,128)} %bitcast.25, f32[512,128]{1,0:T(8,128)} %obs_hbm.1), custom_call_target="tpu_custom_call" | custom-call | tf_op jit(solution)/shard_map/pallas_call | solution.py:535
  2.9 7.3 %all-to-all-start = ((f32[8,64,128]{2,1,0:T(8,128)}), f32[8,64,128]{2,1,0:T(8,128)S(1)}, u32[]{:S(2)}, u32[]{:S(2)}) async-start(f32[8,64,128]{2,1,0:T(8,128)} %bitcast.2), calls=%async_computation | async-start | bytes 524288 | tf_op jit(solution)/shard_map/all_to_all | solution.py:528
  10.2 5.4 %shard_map.69 = (f32[12,512,128]{2,1,0:T(8,128)S(1)}, bf16[3,144,512]{2,1,0:T(8,128)(2,1)}) custom-call(s32[1]{0:T(128)} %bitcast.me_ref, s32[1,512]{1,0:T(1,128)} %bitcast.26, s32[1,512]{1,0:T(1,128)} %bitcast.28, f32[1,512]{1,0:T(1,128)} %bitcast.29, f32[512,128]{1,0:T(8,128)} %shard_map.68._.sent_hbm, f32[12,512,128]{2,1,0:T(8,128)} %bitcast.24), custom_call_target="tpu_custom_call" | custom-call | tf_op jit(solution)/shard_map/pallas_call | solution.py:543
  15.6 3.5 %all-to-all-done = f32[8,64,128]{2,1,0:T(8,128)S(1)} async-done(((f32[8,64,128]{2,1,0:T(8,128)}), f32[8,64,128]{2,1,0:T(8,128)S(1)}, u32[]{:S(2)}, u32[]{:S(2)}) %all-to-all-start) | async-done | bytes 262176 | tf_op jit(solution)/shard_map/all_to_all | solution.py:528
  19.1 2.0 %shard_map.70 = (f32[512,128]{1,0:T(8,128)}, f32[32,16,128]{2,1,0:T(8,128)S(1)}, bf16[3,144,512]{2,1,0:T(8,128)(2,1)S(1)}) custom-call(s32[1]{0:T(128)} %bitcast.me_ref, f32[512,128]{1,0:T(8,128)S(1)} %bitcast.15, f32[12,512,128]{2,1,0:T(8,128)S(1)} %get-tuple-element.38.rows_ref, f32[512,128]{1,0:T(8,128)} %shard_map.68._.sent_hbm, ...), custom_call_target="tpu_custom_call" | custom-call | tf_op jit(solution)/shard_map/pallas_call | solution.py:565
  21.1 14.0 %all_to_all.80.gathered_ref = f32[32,16,128]{2,1,0:T(8,128)S(1)} all-to-all(f32[32,16,128]{2,1,0:T(8,128)S(1)} %get-tuple-element.40), channel_id=1, replica_groups=mesh['track'=8,'det'=4] {'track','det'}, dimensions={0} | all-to-all | bytes 524288 | tf_op jit(solution)/shard_map/all_to_all | solution.py:531
  35.2 0.7 shard_map.71
  35.8 11.7 %all_to_all.81 = f32[8,64,128]{2,1,0:T(8,128)S(1)} all-to-all(f32[8,64,128]{2,1,0:T(8,128)S(1)} %bitcast.18), channel_id=1, replica_groups=mesh['track'=8,'det'=4] {'track'}, dimensions={0} | all-to-all | bytes 524288 | tf_op jit(solution)/shard_map/all_to_all | solution.py:528
  47.5 1.0 shard_map.72
  48.6 13.4 %all_to_all.82.gathered_ref = f32[32,16,128]{2,1,0:T(8,128)S(1)} all-to-all(f32[32,16,128]{2,1,0:T(8,128)S(1)} %get-tuple-element.43), channel_id=1, replica_groups=mesh['track'=8,'det'=4] {'track','det'}, dimensions={0} | all-to-all | bytes 524288 | tf_op jit(solution)/shard_map/all_to_all | solution.py:531
  62.0 1.0 shard_map.73
  62.9 11.7 %all_to_all.83 = f32[8,64,128]{2,1,0:T(8,128)S(1)} all-to-all(f32[8,64,128]{2,1,0:T(8,128)S(1)} %bitcast.17), channel_id=1, replica_groups=mesh['track'=8,'det'=4] {'track'}, dimensions={0} | all-to-all | bytes 524288 | tf_op jit(solution)/shard_map/all_to_all | solution.py:528
  74.6 1.0 shard_map.74
  75.7 13.4 %all_to_all.84.gathered_ref = f32[32,16,128]{2,1,0:T(8,128)S(1)} all-to-all(f32[32,16,128]{2,1,0:T(8,128)S(1)} %get-tuple-element.48), channel_id=1, replica_groups=mesh['track'=8,'det'=4] {'track','det'}, dimensions={0} | all-to-all | bytes 524288 | tf_op jit(solution)/shard_map/all_to_all | solution.py:531
  89.1 1.0 shard_map.75
  90.1 11.7 %all_to_all.85 = f32[8,64,128]{2,1,0:T(8,128)S(1)} all-to-all(f32[8,64,128]{2,1,0:T(8,128)S(1)} %bitcast.16), channel_id=1, replica_groups=mesh['track'=8,'det'=4] {'track'}, dimensions={0} | all-to-all | bytes 524288 | tf_op jit(solution)/shard_map/all_to_all | solution.py:528
  101.8 1.0 shard_map.76
  102.8 13.4 %all_to_all.86.gathered_ref = f32[32,16,128]{2,1,0:T(8,128)S(1)} all-to-all(f32[32,16,128]{2,1,0:T(8,128)S(1)} %get-tuple-element.54), channel_id=1, replica_groups=mesh['track'=8,'det'=4] {'track','det'}, dimensions={0} | all-to-all | bytes 524288 | tf_op jit(solution)/shard_map/all_to_all | solution.py:531
  116.2 0.9 shard_map.77
  117.1 11.7 %all_to_all.87 = f32[8,64,128]{2,1,0:T(8,128)S(1)} all-to-all(f32[8,64,128]{2,1,0:T(8,128)S(1)} %bitcast.22), channel_id=1, replica_groups=mesh['track'=8,'det'=4] {'track'}, dimensions={0} | all-to-all | bytes 524288 | tf_op jit(solution)/shard_map/all_to_all | solution.py:528
  128.8 0.8 shard_map.78
  129.6 3.0 %all-to-all-start.9 = ((f32[32,1,128]{2,1,0:T(1,128)}), f32[32,1,128]{2,1,0:T(1,128)S(1)}, u32[]{:S(2)}, u32[]{:S(2)}) async-start(f32[32,1,128]{2,1,0:T(1,128)} %get-tuple-element.60), calls=%async_computation.9 | async-start | bytes 32768 | tf_op jit(solution)/shard_map/all_to_all | solution.py:531
  132.6 4.3 %shard_map.79 = (f32[512,128]{1,0:T(8,128)S(1)}, f32[512,128]{1,0:T(8,128)S(1)}) custom-call(s32[1]{0:T(128)} %bitcast.me_ref, s32[1,512]{1,0:T(1,128)} %bitcast.27, f32[512,128]{1,0:T(8,128)S(1)} %get-tuple-element.64.diff_ref, f32[8,128]{1,0:T(8,128)S(1)} %get-tuple-element.65.refs_0_, f32[8,128]{1,0:T(8,128)S(1)} %get-tuple-element.66.refs_1_, ...), custom_call_target="tpu_custom_call" | custom-call | tf_op jit(solution)/shard_map/pallas_call | solution.py:610
  136.9 2.9 %all-to-all-done.9.squares_ref = f32[32,1,128]{2,1,0:T(1,128)S(1)} async-done(((f32[32,1,128]{2,1,0:T(1,128)}), f32[32,1,128]{2,1,0:T(1,128)S(1)}, u32[]{:S(2)}, u32[]{:S(2)}) %all-to-all-start.9) | async-done | bytes 16416 | tf_op jit(solution)/shard_map/all_to_all | solution.py:531
  139.8 0.9 shard_map.80
  (1 shorter events, 0.0 us)
Async XLA Ops:
  2.9 16.2 %all-to-all-start = ((f32[8,64,128]{2,1,0:T(8,128)}), f32[8,64,128]{2,1,0:T(8,128)S(1)}, u32[]{:S(2)}, u32[]{:S(2)}) async-start(f32[8,64,128]{2,1,0:T(8,128)} %bitcast.2), calls=%async_computation | async-start | bytes 524288 | tf_op jit(solution)/shard_map/all_to_all | solution.py:528
  129.6 10.2 %all-to-all-start.9 = ((f32[32,1,128]{2,1,0:T(1,128)}), f32[32,1,128]{2,1,0:T(1,128)S(1)}, u32[]{:S(2)}, u32[]{:S(2)}) async-start(f32[32,1,128]{2,1,0:T(1,128)} %get-tuple-element.60), calls=%async_computation.9 | async-start | bytes 32768 | tf_op jit(solution)/shard_map/all_to_all | solution.py:531

commit v14 on v12

--- a/solution.py
+++ b/solution.py
@@ -409,10 +409,12 @@
     direction_ref,
     norm_ref,
     knot_ref,
+    residual_ref,
+    diff_ref,
     direction_out,
     norm_out,
     knot_out,
-    length_out,
+    residual_out,
     sent_ref,
     grad_out,
     image_ref,
@@ -427,7 +429,7 @@
     field_sums(gathered_ref, n_track, n_det, rows_ref.shape[0], put)
     norm = norm_ref[0:1, 0:1]
     length = norm / full_dot(direction_ref, image_ref)
-    length_out[...] = jnp.broadcast_to(length, length_out.shape)
+    residual_out[...] = residual_ref[...] - length * diff_ref[...]
     knot_out[...] = knot_ref[...] + length * direction_ref[me]
     for b in range(n_track):
         grad_out[b] = grad_ref[b] - length * image_ref[b]
@@ -447,18 +449,14 @@
     send_ref[...] = jnp.broadcast_to(squares[None], send_ref.shape)
 
 
-def restore_kernel(q, me_ref, match_hbm, misfit_ref, diff_ref, *refs):
-    steps = (len(refs) - 5) // 2
-    residual_out, diff_out, residual_ref, match_ref, sem = refs[2 * steps :]
-    tiles = misfit_ref.shape[0]
+def restore_kernel(
+    q, me_ref, match_hbm, residual_ref, diff_ref, residual_out, diff_out, match_ref, sem
+):
+    tiles = residual_ref.shape[0]
     copy = pltpu.make_async_copy(match_hbm, match_ref, sem)
     copy.start()
     copy.wait()
     perm = crossing_order(me_ref[0], match_ref[...])
-    residual = misfit_ref[...]
-    for length_ref, change_ref in zip(refs[:steps], refs[steps : 2 * steps]):
-        residual = residual - length_ref[0:1, 0:1] * change_ref[...]
-    residual_ref[...] = residual
     for source, target in ((residual_ref, residual_out), (diff_ref, diff_out)):
         target[...] = from_crossing(
             lambda index: source[index * q : (index + 1) * q, :], perm, q, tiles
@@ -537,7 +535,7 @@
     interp = pltpu.VMEM((n_track, PAD, LANES), jnp.float32)
     adjoint_out = (f32(tiles, columns), f32(n_all, PAD, LANES))
     values = pltpu.VMEM((PAD, tiles), jnp.float32)
-    misfit, payload, weights = call(
+    residual, payload, weights = call(
         functools.partial(first_adjoint_kernel, q),
         adjoint_out + (jax.ShapeDtypeStruct(weight_shape, jnp.bfloat16),),
         [SMEM, VMEM, VMEM, ANY, ANY],
@@ -551,7 +549,6 @@
     )(me, everywhere(payload), rows, weights)
     direction = gradient
     knot_field = jnp.zeros((PAD, KNOT_DEV), jnp.float32)
-    lengths, changes = [], []
     for iteration in range(ITERS - 1):
         change, payload = call(
             functools.partial(adjoint_kernel, q), adjoint_out, [SMEM] + [VMEM] * 4, [values]
@@ -560,17 +557,25 @@
         last = iteration == ITERS - 2
         results = call(
             functools.partial(step_kernel, q, n_det),
-            (field, scalar, f32(PAD, KNOT_DEV), scalar, f32(tiles, columns))
+            (field, scalar, f32(PAD, KNOT_DEV), f32(tiles, columns), f32(tiles, columns))
             + (() if last else (field,)),
-            [SMEM] + [VMEM] * 8,
+            [SMEM] + [VMEM] * 10,
             [interp] * (3 if last else 2),
         )(
-            me, gathered, rows, weights, edge, gradient, direction, slope_norm, knot_field
+            me,
+            gathered,
+            rows,
+            weights,
+            edge,
+            gradient,
+            direction,
+            slope_norm,
+            knot_field,
+            residual,
+            change,
         )
-        direction, slope_norm, knot_field, length, sent = results[:5]
+        direction, slope_norm, knot_field, residual, sent = results[:5]
         gradient = None if last else results[5]
-        lengths.append(length)
-        changes.append(change)
     change, squares = call(
         functools.partial(last_kernel, q),
         (f32(tiles, columns), f32(n_all, 1, LANES)),
@@ -580,9 +585,9 @@
     residual, change = call(
         functools.partial(restore_kernel, q),
         (f32(tiles, columns), f32(tiles, columns)),
-        [SMEM, ANY] + [VMEM] * (2 + 2 * len(changes)),
-        [pltpu.VMEM((tiles, columns), jnp.float32), int_row, pltpu.SemaphoreType.DMA],
-    )(me, match_row, misfit, change, *lengths, *changes)
+        [SMEM, ANY, VMEM, VMEM],
+        [int_row, pltpu.SemaphoreType.DMA],
+    )(me, match_row, residual, change)
     return call(
         finish_kernel,
         (f32(params, KNOT_DEV), f32(tiles, columns)),

time: 141 us -> 140 us (level)
  local copies, waits for them, and re-layouts: 4.25 us -> 0.01 us
  waiting for transfers between devices: 4.89 us -> 7.71 us
    unnamed x16 -> x0, local copies, waits for them, and re-layouts: 4.24 us -> none
    all_to_all x1, waiting for transfers between devices: 1.37 us -> 4.19 us  [everywhere(): lax.all_to_all(values, ('track', 'det'), split_axis=0, concat_axis=0, til...]
where the time goes in v14:
time: 140 us; the launch traced here: 139 us
  blocking collectives  101 us (72%)
  Pallas kernels  19.7 us (14%)
  starting transfers between devices  10.3 us (7%)
  waiting for transfers between devices  7.71 us (6%)
    all_to_all x4, blocking collectives, everywhere(): lax.all_to_all(values, ('track', 'det'), split_axis=0, concat_axis=0, til...  54.2 us
    all_to_all x4, blocking collectives, crossing(): lax.all_to_all(values, 'track', split_axis=0, concat_axis=0, tiled=True)  46.8 us
    all_to_all x1, starting transfers between devices, crossing(): lax.all_to_all(values, 'track', split_axis=0, concat_axis=0, tiled=True)  7.29 us
    pallas_call x1, Pallas kernels, local(): call(functools.partial(rows_kernel, q, math.gcd(params, 3)), (kept((param...  5.39 us
    all_to_all x1, waiting for transfers between devices, everywhere(): lax.all_to_all(values, ('track', 'det'), split_axis=0, concat_axis=0, til...  4.19 us
    all_to_all x1, waiting for transfers between devices, crossing(): lax.all_to_all(values, 'track', split_axis=0, concat_axis=0, tiled=True)  3.52 us
    all_to_all x1, starting transfers between devices, everywhere(): lax.all_to_all(values, ('track', 'det'), split_axis=0, concat_axis=0, til...  3 us
    pallas_call x3, Pallas kernels, local(): call(functools.partial(step_kernel, q, n_det), (field, scalar, f32(PAD, K...  3 us
  transfers between devices with their start and end apart: 2, of which 2 were waited for; matrix products, arithmetic and copies ran while one was open for 0% of the time, Pallas kernels for 6%

profile of v14, /device:TPU:0, one launch (start us, length us, event | category | flops | bytes accessed | tf_op | source)
XLA Modules:
  0.0 139.4 jit_solution(9289931813009744659)
XLA Ops:
  0.6 2.3 %shard_map.68._.sent_hbm = f32[512,128]{1,0:T(8,128)} custom-call(s32[1]{0:T(128)} %bitcast.me_ref, s32[1,512]{1,0:T(1,128)} %bitcast.25, f32[512,128]{1,0:T(8,128)} %obs_hbm.1), custom_call_target="tpu_custom_call" | custom-call | tf_op jit(solution)/shard_map/pallas_call | solution.py:509
  2.9 7.3 %all-to-all-start = ((f32[8,64,128]{2,1,0:T(8,128)}), f32[8,64,128]{2,1,0:T(8,128)S(1)}, u32[]{:S(2)}, u32[]{:S(2)}) async-start(f32[8,64,128]{2,1,0:T(8,128)} %bitcast.2), calls=%async_computation | async-start | bytes 524288 | tf_op jit(solution)/shard_map/all_to_all | solution.py:502
  10.2 5.4 %shard_map.69 = (f32[12,512,128]{2,1,0:T(8,128)S(1)}, bf16[3,144,512]{2,1,0:T(8,128)(2,1)}) custom-call(s32[1]{0:T(128)} %bitcast.me_ref, s32[1,512]{1,0:T(1,128)} %bitcast.26, s32[1,512]{1,0:T(1,128)} %bitcast.28, f32[1,512]{1,0:T(1,128)} %bitcast.29, f32[512,128]{1,0:T(8,128)} %shard_map.68._.sent_hbm, f32[12,512,128]{2,1,0:T(8,128)} %bitcast.24), custom_call_target="tpu_custom_call" | custom-call | tf_op jit(solution)/shard_map/pallas_call | solution.py:517
  15.6 3.5 %all-to-all-done = f32[8,64,128]{2,1,0:T(8,128)S(1)} async-done(((f32[8,64,128]{2,1,0:T(8,128)}), f32[8,64,128]{2,1,0:T(8,128)S(1)}, u32[]{:S(2)}, u32[]{:S(2)}) %all-to-all-start) | async-done | bytes 262176 | tf_op jit(solution)/shard_map/all_to_all | solution.py:502
  19.1 1.7 %shard_map.70 = (f32[512,128]{1,0:T(8,128)S(1)}, f32[32,16,128]{2,1,0:T(8,128)S(1)}, bf16[3,144,512]{2,1,0:T(8,128)(2,1)S(1)}) custom-call(s32[1]{0:T(128)} %bitcast.me_ref, f32[512,128]{1,0:T(8,128)S(1)} %bitcast.15, f32[12,512,128]{2,1,0:T(8,128)S(1)} %get-tuple-element.38.rows_ref, f32[512,128]{1,0:T(8,128)} %shard_map.68._.sent_hbm, ...), custom_call_target="tpu_custom_call" | custom-call | tf_op jit(solution)/shard_map/pallas_call | solution.py:538
  20.9 14.0 %all_to_all.80.gathered_ref = f32[32,16,128]{2,1,0:T(8,128)S(1)} all-to-all(f32[32,16,128]{2,1,0:T(8,128)S(1)} %get-tuple-element.40), channel_id=1, replica_groups=mesh['track'=8,'det'=4] {'track','det'}, dimensions={0} | all-to-all | bytes 524288 | tf_op jit(solution)/shard_map/all_to_all | solution.py:505
  34.9 0.7 shard_map.71
  35.5 11.7 %all_to_all.81 = f32[8,64,128]{2,1,0:T(8,128)S(1)} all-to-all(f32[8,64,128]{2,1,0:T(8,128)S(1)} %bitcast.18), channel_id=1, replica_groups=mesh['track'=8,'det'=4] {'track'}, dimensions={0} | all-to-all | bytes 524288 | tf_op jit(solution)/shard_map/all_to_all | solution.py:502
  47.2 0.7 shard_map.72
  47.9 13.4 %all_to_all.82.gathered_ref = f32[32,16,128]{2,1,0:T(8,128)S(1)} all-to-all(f32[32,16,128]{2,1,0:T(8,128)S(1)} %get-tuple-element.43), channel_id=1, replica_groups=mesh['track'=8,'det'=4] {'track','det'}, dimensions={0} | all-to-all | bytes 524288 | tf_op jit(solution)/shard_map/all_to_all | solution.py:505
  61.3 1.0 shard_map.73
  62.3 11.7 %all_to_all.83 = f32[8,64,128]{2,1,0:T(8,128)S(1)} all-to-all(f32[8,64,128]{2,1,0:T(8,128)S(1)} %bitcast.17), channel_id=1, replica_groups=mesh['track'=8,'det'=4] {'track'}, dimensions={0} | all-to-all | bytes 524288 | tf_op jit(solution)/shard_map/all_to_all | solution.py:502
  74.0 0.7 shard_map.74
  74.7 13.4 %all_to_all.84.gathered_ref = f32[32,16,128]{2,1,0:T(8,128)S(1)} all-to-all(f32[32,16,128]{2,1,0:T(8,128)S(1)} %get-tuple-element.50), channel_id=1, replica_groups=mesh['track'=8,'det'=4] {'track','det'}, dimensions={0} | all-to-all | bytes 524288 | tf_op jit(solution)/shard_map/all_to_all | solution.py:505
  88.1 1.0 shard_map.75
  89.1 11.7 %all_to_all.85 = f32[8,64,128]{2,1,0:T(8,128)S(1)} all-to-all(f32[8,64,128]{2,1,0:T(8,128)S(1)} %bitcast.16), channel_id=1, replica_groups=mesh['track'=8,'det'=4] {'track'}, dimensions={0} | all-to-all | bytes 524288 | tf_op jit(solution)/shard_map/all_to_all | solution.py:502
  100.8 0.7 shard_map.76
  101.5 13.4 %all_to_all.86.gathered_ref = f32[32,16,128]{2,1,0:T(8,128)S(1)} all-to-all(f32[32,16,128]{2,1,0:T(8,128)S(1)} %get-tuple-element.58), channel_id=1, replica_groups=mesh['track'=8,'det'=4] {'track','det'}, dimensions={0} | all-to-all | bytes 524288 | tf_op jit(solution)/shard_map/all_to_all | solution.py:505
  114.9 1.0 shard_map.77
  115.9 11.7 %all_to_all.87 = f32[8,64,128]{2,1,0:T(8,128)S(1)} all-to-all(f32[8,64,128]{2,1,0:T(8,128)S(1)} %bitcast.22), channel_id=1, replica_groups=mesh['track'=8,'det'=4] {'track'}, dimensions={0} | all-to-all | bytes 524288 | tf_op jit(solution)/shard_map/all_to_all | solution.py:502
  127.6 0.8 shard_map.78
  128.4 3.0 %all-to-all-start.9 = ((f32[32,1,128]{2,1,0:T(1,128)}), f32[32,1,128]{2,1,0:T(1,128)S(1)}, u32[]{:S(2)}, u32[]{:S(2)}) async-start(f32[32,1,128]{2,1,0:T(1,128)} %get-tuple-element.66), calls=%async_computation.9 | async-start | bytes 32768 | tf_op jit(solution)/shard_map/all_to_all | solution.py:505
  131.4 2.9 %shard_map.79 = (f32[512,128]{1,0:T(8,128)S(1)}, f32[512,128]{1,0:T(8,128)S(1)}) custom-call(s32[1]{0:T(128)} %bitcast.me_ref, s32[1,512]{1,0:T(1,128)} %bitcast.27, f32[512,128]{1,0:T(8,128)S(1)} %get-tuple-element.70.residual_ref, f32[512,128]{1,0:T(8,128)S(1)} %get-tuple-element.71.diff_ref), custom_call_target="tpu_custom_call" | custom-call | tf_op jit(solution)/shard_map/pallas_call | solution.py:585
  134.3 4.2 %all-to-all-done.9.squares_ref = f32[32,1,128]{2,1,0:T(1,128)S(1)} async-done(((f32[32,1,128]{2,1,0:T(1,128)}), f32[32,1,128]{2,1,0:T(1,128)S(1)}, u32[]{:S(2)}, u32[]{:S(2)}) %all-to-all-start.9) | async-done | bytes 16416 | tf_op jit(solution)/shard_map/all_to_all | solution.py:505
  138.5 0.9 shard_map.80
  (1 shorter events, 0.0 us)
Async XLA Ops:
  2.9 16.2 %all-to-all-start = ((f32[8,64,128]{2,1,0:T(8,128)}), f32[8,64,128]{2,1,0:T(8,128)S(1)}, u32[]{:S(2)}, u32[]{:S(2)}) async-start(f32[8,64,128]{2,1,0:T(8,128)} %bitcast.2), calls=%async_computation | async-start | bytes 524288 | tf_op jit(solution)/shard_map/all_to_all | solution.py:502
  128.4 10.1 %all-to-all-start.9 = ((f32[32,1,128]{2,1,0:T(1,128)}), f32[32,1,128]{2,1,0:T(1,128)S(1)}, u32[]{:S(2)}, u32[]{:S(2)}) async-start(f32[32,1,128]{2,1,0:T(1,128)} %get-tuple-element.66), calls=%async_computation.9 | async-start | bytes 32768 | tf_op jit(solution)/shard_map/all_to_all | solution.py:505

commit v15 on v14

--- a/solution.py
+++ b/solution.py
@@ -149,18 +149,21 @@
     match_hbm,
     knot_hbm,
     frac_hbm,
-    _,
+    sent_hbm,
     jac_hbm,
     rows_ref,
     weight_ref,
+    values_ref,
     match_ref,
     knot_ref,
     frac_ref,
+    sent_ref,
     sems,
 ):
     params, tiles = jac_hbm.shape[:2]
     pairs = [(match_hbm, match_ref), (knot_hbm, knot_ref), (frac_hbm, frac_ref)]
     pairs += [(jac_hbm.at[p], rows_ref.at[p]) for p in range(params)]
+    pairs += [(sent_hbm, sent_ref)]
     copies = [
         pltpu.make_async_copy(source, target, sems.at[index])
         for index, (source, target) in enumerate(pairs)
@@ -190,6 +193,8 @@
             rows_ref[first + index, block_index * q : (block_index + 1) * q, :] = block
 
         to_crossing([rows_ref[p] for p in range(first, first + together)], perm, q, put)
+    copies[3 + params].wait()
+    adjoint_values(q, sent_ref, rows_ref, values_ref)
 
 
 def weight_dot(x, parts, over_tiles):
@@ -253,26 +258,32 @@
     me_ref,
     arrived_ref,
     rows_ref,
+    own_hbm,
     sent_hbm,
     weight_hbm,
     diff_ref,
     send_ref,
     weight_ref,
     values_ref,
+    own_ref,
     sent_ref,
     sems,
 ):
     copies = [
-        pltpu.make_async_copy(sent_hbm, sent_ref, sems.at[0]),
+        pltpu.make_async_copy(own_hbm, own_ref, sems.at[0]),
         pltpu.make_async_copy(weight_hbm, weight_ref, sems.at[1]),
+        pltpu.make_async_copy(sent_hbm, sent_ref, sems.at[2]),
     ]
     for copy in copies:
         copy.start()
+    crossing_values(me_ref[0], arrived_ref, diff_ref, q)
+    adjoint_values(q, diff_ref, rows_ref, values_ref)
     copies[0].wait()
-    difference(me_ref[0], sent_ref, arrived_ref, diff_ref, q)
-    adjoint_values(q, diff_ref, rows_ref, values_ref)
+    values_ref[...] = own_ref[...] - values_ref[...]
     copies[1].wait()
     adjoint_rows(rows_ref.shape[0], values_ref, weight_ref, send_ref)
+    copies[2].wait()
+    diff_ref[...] = sent_ref[...] - diff_ref[...]
 
 
 def adjoint_kernel(
@@ -514,15 +525,20 @@
     )(me, match_row, from_hbm(obs))
     arrived = crossing(sent)
     weight_shape = (3, KNOT_DEV + PAD, tiles)
-    rows, weights = call(
+    rows, weights, own = call(
         functools.partial(rows_kernel, q, math.gcd(params, 3)),
-        (kept((params, tiles, columns)), pltpu.HBM(weight_shape, jnp.bfloat16)),
+        (
+            kept((params, tiles, columns)),
+            pltpu.HBM(weight_shape, jnp.bfloat16),
+            pltpu.HBM((PAD, tiles), jnp.float32),
+        ),
         [SMEM] + [ANY] * 5,
         [
             int_row,
             int_row,
             pltpu.VMEM((1, tiles), jnp.float32),
-            pltpu.SemaphoreType.DMA((3 + params,)),
+            pltpu.VMEM((tiles, columns), jnp.float32),
+            pltpu.SemaphoreType.DMA((4 + params,)),
         ],
     )(
         me,
@@ -538,9 +554,9 @@
     residual, payload, weights = call(
         functools.partial(first_adjoint_kernel, q),
         adjoint_out + (jax.ShapeDtypeStruct(weight_shape, jnp.bfloat16),),
-        [SMEM, VMEM, VMEM, ANY, ANY],
-        [values, pltpu.VMEM((tiles, columns), jnp.float32), pltpu.SemaphoreType.DMA((2,))],
-    )(me, arrived, rows, from_hbm(sent), from_hbm(weights))
+        [SMEM, VMEM, VMEM, ANY, ANY, ANY],
+        [values, values, pltpu.VMEM((tiles, columns), jnp.float32), pltpu.SemaphoreType.DMA((3,))],
+    )(me, arrived, rows, *map(from_hbm, (own, sent, weights)))
     gradient, slope_norm, sent, edge = call(
         functools.partial(first_kernel, q, n_det),
         (field, scalar, f32(tiles, columns), f32(SUB, tiles)),

time: 140 us -> 140 us (level)
  transfers between devices with their start and end apart: 2 -> 2, of which waited for: 2 -> 2; matrix products, arithmetic and copies ran while one was open for 0% -> 0% of each run, Pallas kernels for 6% -> 7%
where the time goes in v15:
time: 140 us; the launch traced here: 139 us
  blocking collectives  101 us (72%)
  Pallas kernels  20.7 us (15%)
  starting transfers between devices  10.3 us (7%)
  waiting for transfers between devices  6.7 us (5%)
    all_to_all x4, blocking collectives, everywhere(): lax.all_to_all(values, ('track', 'det'), split_axis=0, concat_axis=0, til...  54.2 us
    all_to_all x4, blocking collectives, crossing(): lax.all_to_all(values, 'track', split_axis=0, concat_axis=0, tiled=True)  46.8 us
    all_to_all x1, starting transfers between devices, crossing(): lax.all_to_all(values, 'track', split_axis=0, concat_axis=0, tiled=True)  7.29 us
    pallas_call x1, Pallas kernels, local(): call(functools.partial(rows_kernel, q, math.gcd(params, 3)), (kept((param...  6.4 us
    all_to_all x1, waiting for transfers between devices, everywhere(): lax.all_to_all(values, ('track', 'det'), split_axis=0, concat_axis=0, til...  4.19 us
    all_to_all x1, starting transfers between devices, everywhere(): lax.all_to_all(values, ('track', 'det'), split_axis=0, concat_axis=0, til...  3 us
    pallas_call x3, Pallas kernels, local(): call(functools.partial(step_kernel, q, n_det), (field, scalar, f32(PAD, K...  3 us
    pallas_call x1, Pallas kernels, local(): call(functools.partial(restore_kernel, q), (f32(tiles, columns), f32(tile...  2.88 us
  transfers between devices with their start and end apart: 2, of which 2 were waited for; matrix products, arithmetic and copies ran while one was open for 0% of the time, Pallas kernels for 7%

profile of v15, /device:TPU:0, one launch (start us, length us, event | category | flops | bytes accessed | tf_op | source)
XLA Modules:
  0.0 139.5 jit_solution(14463974949950631649)
XLA Ops:
  0.6 2.3 %shard_map.68.sent_hbm = f32[512,128]{1,0:T(8,128)} custom-call(s32[1]{0:T(128)} %bitcast.me_ref, s32[1,512]{1,0:T(1,128)} %bitcast.25, f32[512,128]{1,0:T(8,128)} %obs_hbm.1), custom_call_target="tpu_custom_call" | custom-call | tf_op jit(solution)/shard_map/pallas_call | solution.py:520
  2.9 7.3 %all-to-all-start = ((f32[8,64,128]{2,1,0:T(8,128)}), f32[8,64,128]{2,1,0:T(8,128)S(1)}, u32[]{:S(2)}, u32[]{:S(2)}) async-start(f32[8,64,128]{2,1,0:T(8,128)} %bitcast.2), calls=%async_computation | async-start | bytes 524288 | tf_op jit(solution)/shard_map/all_to_all | solution.py:513
  10.2 6.4 %shard_map.69 = (f32[12,512,128]{2,1,0:T(8,128)S(1)}, bf16[3,144,512]{2,1,0:T(8,128)(2,1)}, f32[16,512]{1,0:T(8,128)}) custom-call(s32[1]{0:T(128)} %bitcast.me_ref, s32[1,512]{1,0:T(1,128)} %bitcast.26, s32[1,512]{1,0:T(1,128)} %bitcast.28, f32[1,512]{1,0:T(1,128)} %bitcast.29, f32[512,128]{1,0:T(8,128)} %shard_map.68.sent_hbm, f32[12,512,128]{2,1,0:T(8,128)} %bitcast.24), custom_call_target="tpu_custom_call" | custom-call | tf_op jit(solution)/shard_map/pallas_call | solution.py:528
  16.6 2.5 %all-to-all-done = f32[8,64,128]{2,1,0:T(8,128)S(1)} async-done(((f32[8,64,128]{2,1,0:T(8,128)}), f32[8,64,128]{2,1,0:T(8,128)S(1)}, u32[]{:S(2)}, u32[]{:S(2)}) %all-to-all-start) | async-done | bytes 262176 | tf_op jit(solution)/shard_map/all_to_all | solution.py:513
  19.1 1.7 %shard_map.70 = (f32[512,128]{1,0:T(8,128)S(1)}, f32[32,16,128]{2,1,0:T(8,128)S(1)}, bf16[3,144,512]{2,1,0:T(8,128)(2,1)S(1)}) custom-call(s32[1]{0:T(128)} %bitcast.me_ref, f32[512,128]{1,0:T(8,128)S(1)} %bitcast.15, f32[12,512,128]{2,1,0:T(8,128)S(1)} %get-tuple-element.39.rows_ref, f32[16,512]{1,0:T(8,128)} %get-tuple-element.40.own_hbm, ...), custom_call_target="tpu_custom_call" | custom-call | tf_op jit(solution)/shard_map/pallas_call | solution.py:554
  20.9 14.0 %all_to_all.80.gathered_ref = f32[32,16,128]{2,1,0:T(8,128)S(1)} all-to-all(f32[32,16,128]{2,1,0:T(8,128)S(1)} %get-tuple-element.42), channel_id=1, replica_groups=mesh['track'=8,'det'=4] {'track','det'}, dimensions={0} | all-to-all | bytes 524288 | tf_op jit(solution)/shard_map/all_to_all | solution.py:516
  34.9 0.7 shard_map.71
  35.6 11.7 %all_to_all.81 = f32[8,64,128]{2,1,0:T(8,128)S(1)} all-to-all(f32[8,64,128]{2,1,0:T(8,128)S(1)} %bitcast.18), channel_id=1, replica_groups=mesh['track'=8,'det'=4] {'track'}, dimensions={0} | all-to-all | bytes 524288 | tf_op jit(solution)/shard_map/all_to_all | solution.py:513
  47.3 0.7 shard_map.72
  47.9 13.4 %all_to_all.82.gathered_ref = f32[32,16,128]{2,1,0:T(8,128)S(1)} all-to-all(f32[32,16,128]{2,1,0:T(8,128)S(1)} %get-tuple-element.45), channel_id=1, replica_groups=mesh['track'=8,'det'=4] {'track','det'}, dimensions={0} | all-to-all | bytes 524288 | tf_op jit(solution)/shard_map/all_to_all | solution.py:516
  61.4 1.0 shard_map.73
  62.4 11.7 %all_to_all.83 = f32[8,64,128]{2,1,0:T(8,128)S(1)} all-to-all(f32[8,64,128]{2,1,0:T(8,128)S(1)} %bitcast.17), channel_id=1, replica_groups=mesh['track'=8,'det'=4] {'track'}, dimensions={0} | all-to-all | bytes 524288 | tf_op jit(solution)/shard_map/all_to_all | solution.py:513
  74.1 0.7 shard_map.74
  74.7 13.4 %all_to_all.84.gathered_ref = f32[32,16,128]{2,1,0:T(8,128)S(1)} all-to-all(f32[32,16,128]{2,1,0:T(8,128)S(1)} %get-tuple-element.52), channel_id=1, replica_groups=mesh['track'=8,'det'=4] {'track','det'}, dimensions={0} | all-to-all | bytes 524288 | tf_op jit(solution)/shard_map/all_to_all | solution.py:516
  88.2 1.0 shard_map.75
  89.2 11.7 %all_to_all.85 = f32[8,64,128]{2,1,0:T(8,128)S(1)} all-to-all(f32[8,64,128]{2,1,0:T(8,128)S(1)} %bitcast.16), channel_id=1, replica_groups=mesh['track'=8,'det'=4] {'track'}, dimensions={0} | all-to-all | bytes 524288 | tf_op jit(solution)/shard_map/all_to_all | solution.py:513
  100.9 0.7 shard_map.76
  101.5 13.4 %all_to_all.86.gathered_ref = f32[32,16,128]{2,1,0:T(8,128)S(1)} all-to-all(f32[32,16,128]{2,1,0:T(8,128)S(1)} %get-tuple-element.60), channel_id=1, replica_groups=mesh['track'=8,'det'=4] {'track','det'}, dimensions={0} | all-to-all | bytes 524288 | tf_op jit(solution)/shard_map/all_to_all | solution.py:516
  114.9 1.0 shard_map.77
  116.0 11.7 %all_to_all.87 = f32[8,64,128]{2,1,0:T(8,128)S(1)} all-to-all(f32[8,64,128]{2,1,0:T(8,128)S(1)} %bitcast.22), channel_id=1, replica_groups=mesh['track'=8,'det'=4] {'track'}, dimensions={0} | all-to-all | bytes 524288 | tf_op jit(solution)/shard_map/all_to_all | solution.py:513
  127.6 0.8 shard_map.78
  128.4 3.0 %all-to-all-start.9 = ((f32[32,1,128]{2,1,0:T(1,128)}), f32[32,1,128]{2,1,0:T(1,128)S(1)}, u32[]{:S(2)}, u32[]{:S(2)}) async-start(f32[32,1,128]{2,1,0:T(1,128)} %get-tuple-element.68), calls=%async_computation.9 | async-start | bytes 32768 | tf_op jit(solution)/shard_map/all_to_all | solution.py:516
  131.5 2.9 %shard_map.79 = (f32[512,128]{1,0:T(8,128)S(1)}, f32[512,128]{1,0:T(8,128)S(1)}) custom-call(s32[1]{0:T(128)} %bitcast.me_ref, s32[1,512]{1,0:T(1,128)} %bitcast.27, f32[512,128]{1,0:T(8,128)S(1)} %get-tuple-element.72.residual_ref, f32[512,128]{1,0:T(8,128)S(1)} %get-tuple-element.73.diff_ref), custom_call_target="tpu_custom_call" | custom-call | tf_op jit(solution)/shard_map/pallas_call | solution.py:601
  134.3 4.2 %all-to-all-done.9.squares_ref = f32[32,1,128]{2,1,0:T(1,128)S(1)} async-done(((f32[32,1,128]{2,1,0:T(1,128)}), f32[32,1,128]{2,1,0:T(1,128)S(1)}, u32[]{:S(2)}, u32[]{:S(2)}) %all-to-all-start.9) | async-done | bytes 16416 | tf_op jit(solution)/shard_map/all_to_all | solution.py:516
  138.5 0.9 shard_map.80
  (1 shorter events, 0.0 us)
Async XLA Ops:
  2.9 16.2 %all-to-all-start = ((f32[8,64,128]{2,1,0:T(8,128)}), f32[8,64,128]{2,1,0:T(8,128)S(1)}, u32[]{:S(2)}, u32[]{:S(2)}) async-start(f32[8,64,128]{2,1,0:T(8,128)} %bitcast.2), calls=%async_computation | async-start | bytes 524288 | tf_op jit(solution)/shard_map/all_to_all | solution.py:513
  128.4 10.1 %all-to-all-start.9 = ((f32[32,1,128]{2,1,0:T(1,128)}), f32[32,1,128]{2,1,0:T(1,128)S(1)}, u32[]{:S(2)}, u32[]{:S(2)}) async-start(f32[32,1,128]{2,1,0:T(1,128)} %get-tuple-element.68), calls=%async_computation.9 | async-start | bytes 32768 | tf_op jit(solution)/shard_map/all_to_all | solution.py:516
